TPU v7x, 512 devices: a whole 4x8x8 slice. The times are simulated.
512 devices in a mesh: seq: 32 (over z, x_hi, core), ctx: 16 (over x_lo, y).
Axes of the slice: x: 4 (x_hi: 2, x_lo: 2; x = x_hi * 2 + x_lo), y: 8, z: 8, core: 2. Of those that a mesh axis runs over, the one named last changes fastest.
Arguments:
- queries: bfloat16 [32, 2048, 8192], P('seq', 'ctx'), may hold values from -6 to 6
- keys: bfloat16 [32, 2048, 1024], P('seq', 'ctx'), may hold values from -6 to 6
- doc_ids: int32 [32, 2048], P('seq'), may hold values from 0 to 2, never falling along the last dimension, each value on 1 to 1792 neighbouring positions
- gate_query_weight: bfloat16 [8192, 1024], P('ctx'), may hold values from -1 to 1
- gate_key_weight: bfloat16 [1024, 1024], P('ctx'), may hold values from -1 to 1
Outputs:
- grad_query_weight: bfloat16 [8192, 1024], P('ctx')
- grad_key_weight: bfloat16 [1024, 1024], P('ctx')
Inputs may be any that keep to these rules, and one draw needn't show every extreme that they name: `doc_ids`: document ids of a sequence never fall, there are 3 documents, each of at most 1792 tokens, one exactly that long.
All inputs are finite; a program needn't handle non-finite values.
Results may differ from a plain program's by a relative error of at most 0.012.
The roundings to bfloat16 on the way count: a program that leaves them out, or rounds other values in their place, can miss the bound.
Values may be sent and summed in bfloat16 or wider, within the bound.
No kernel may reach another device: no remote copies, remote signals or barrier semaphores. Data moves between devices by JAX's collectives and lax.ppermute only.
A program may use at most 64 MiB of HBM per device.

v0:
```python
import jax
import jax.numpy as jnp
from jax import lax
from jax.sharding import PartitionSpec as P

HEADS = 64
KV_HEADS = 8
HEAD_DIM = 128
GATE_DIM = 128
BLOCK = 64


NEG_FILL = -1e30


def cycle_targets(local_q, local_k, doc_all, my_rank, tok_rows, num_blocks):
    group_size = HEADS // KV_HEADS
    attn_scale = 1.0 / HEAD_DIM**0.5
    query_heads = local_q.reshape(tok_rows, KV_HEADS, group_size, HEAD_DIM)
    row_start = my_rank * tok_rows
    query_pos = row_start + jnp.arange(tok_rows, dtype=jnp.int32)
    query_doc = lax.dynamic_slice_in_dim(doc_all, row_start, tok_rows)
    init = (
        jnp.full((KV_HEADS, group_size, tok_rows), NEG_FILL, jnp.float32),
        jnp.zeros((KV_HEADS, group_size, tok_rows), jnp.float32),
        jnp.full((KV_HEADS, group_size, tok_rows, num_blocks), NEG_FILL, jnp.float32),
    )
    running = init
    panel = lax.all_gather(local_k, "ctx", axis=0, tiled=True)
    tile_len = min(tok_rows, panel.shape[0])

    def one_tile(which, running):
        key_start = which * tile_len

        def refresh(running):
            run_max, run_sum, block_max = running
            key_tile = lax.dynamic_slice_in_dim(panel, which * tile_len, tile_len, 0).reshape(
                tile_len, KV_HEADS, HEAD_DIM
            )
            scores = (
                jnp.einsum(
                    "rhgd,chd->hgrc", query_heads, key_tile, preferred_element_type=jnp.float32
                )
                * attn_scale
            )
            key_pos = key_start + jnp.arange(tile_len, dtype=jnp.int32)
            key_doc = lax.dynamic_slice_in_dim(doc_all, key_start, tile_len)
            visible = (key_pos[None, :] <= query_pos[:, None]) & (
                key_doc[None, :] == query_doc[:, None]
            )
            scores = jnp.where(visible, scores, NEG_FILL)
            peak = jnp.maximum(run_max, jnp.max(scores, axis=-1))
            fresh = jnp.sum(jnp.where(visible, jnp.exp(scores - peak[..., None]), 0.0), axis=-1)
            new_sum = run_sum * jnp.exp(run_max - peak) + fresh
            blockwise = scores.reshape(
                KV_HEADS, group_size, tok_rows, tile_len // BLOCK, BLOCK
            ).max(axis=-1)
            new_block = lax.dynamic_update_slice_in_dim(block_max, blockwise, key_start // BLOCK, 3)
            return (peak, new_sum, new_block)

        return lax.cond(key_start <= row_start + tok_rows - 1, refresh, lambda kept: kept, running)

    run_max, run_sum, block_max = lax.fori_loop(0, panel.shape[0] // tile_len, one_tile, running)
    lse = run_max + jnp.log(run_sum)
    probs = jnp.exp(block_max - lse[..., None])
    head_probs = probs.reshape(KV_HEADS, group_size, tok_rows // BLOCK, BLOCK, num_blocks).max(
        axis=3
    )
    return head_probs.sum(axis=1)


def shards(queries, keys, doc_ids, gate_query_weight, gate_key_weight):
    tok_rows = queries.shape[1]
    cycle_size = lax.axis_size("ctx")
    my_rank = lax.axis_index("ctx")
    blocks_dev = tok_rows // BLOCK
    num_blocks = blocks_dev * cycle_size
    gate_scale = 1.0 / GATE_DIM**0.5
    local_q = queries[0]
    local_k = keys[0]
    doc_all = doc_ids[0]
    raw_target = cycle_targets(local_q, local_k, doc_all, my_rank, tok_rows, num_blocks)
    target = raw_target / jnp.sum(raw_target, axis=-1, keepdims=True)
    pool_q = (
        jnp.sum(local_q.reshape(blocks_dev, BLOCK, -1), axis=1, dtype=jnp.float32) / BLOCK
    ).astype(jnp.bfloat16)
    pool_k = jnp.max(local_k.reshape(blocks_dev, BLOCK, -1), axis=1)
    pooled_q, pooled_k = (
        lax.all_to_all(pool_q, "ctx", split_axis=1, concat_axis=0, tiled=True),
        lax.all_to_all(pool_k, "ctx", split_axis=1, concat_axis=0, tiled=True),
    )
    part_q = jnp.dot(pooled_q, gate_query_weight, preferred_element_type=jnp.float32)
    part_k = jnp.dot(pooled_k, gate_key_weight, preferred_element_type=jnp.float32)
    projected = lax.psum_scatter(
        jnp.concatenate([part_q, part_k], axis=1), "ctx", scatter_dimension=0, tiled=True
    )
    gate_width = gate_query_weight.shape[1]
    gate_q = projected[:, :gate_width].astype(jnp.bfloat16)
    gate_k_mine = projected[:, gate_width:].astype(jnp.bfloat16)
    gate_k_all = lax.all_gather(gate_k_mine, "ctx", axis=0, tiled=True)
    gq_heads = gate_q.reshape(blocks_dev, KV_HEADS, GATE_DIM)
    gk_heads = gate_k_all.reshape(num_blocks, KV_HEADS, GATE_DIM)
    logits = (
        jnp.einsum("ahe,bhe->hab", gq_heads, gk_heads, preferred_element_type=jnp.float32)
        * gate_scale
    )
    query_block = my_rank * blocks_dev + jnp.arange(blocks_dev, dtype=jnp.int32)
    key_block = jnp.arange(num_blocks, dtype=jnp.int32)
    causal = key_block[None, :] <= query_block[:, None]
    masked = jnp.where(causal, logits, NEG_FILL)
    peak = jnp.max(masked, axis=-1, keepdims=True)
    weights = jnp.where(causal, jnp.exp(masked - peak), 0.0)
    gate_prob = weights / jnp.sum(weights, axis=-1, keepdims=True)
    score_grad = jnp.where(causal, gate_prob - target, 0.0)
    grad_gate_q = (
        jnp.einsum(
            "hab,bhe->ahe",
            score_grad,
            gk_heads.astype(jnp.float32),
            precision=lax.Precision.HIGHEST,
        )
        * gate_scale
    ).astype(jnp.bfloat16)
    key_part = (
        jnp.einsum(
            "hab,ahe->bhe",
            score_grad,
            gq_heads.astype(jnp.float32),
            precision=lax.Precision.HIGHEST,
        )
        * gate_scale
    )
    grad_gate_k = lax.psum(key_part, "ctx").astype(jnp.bfloat16).reshape(num_blocks, gate_width)
    grad_gate_q_all = lax.all_gather(
        grad_gate_q.reshape(blocks_dev, gate_width), "ctx", axis=0, tiled=True
    )
    grad_q = jnp.dot(pooled_q.T, grad_gate_q_all, preferred_element_type=jnp.float32)
    grad_k = jnp.dot(pooled_k.T, grad_gate_k, preferred_element_type=jnp.float32)
    summed_q, summed_k = lax.psum((grad_q, grad_k), "seq")
    return (summed_q.astype(jnp.bfloat16), summed_k.astype(jnp.bfloat16))


def solution(mesh):
    in_specs = (
        P("seq", "ctx", None),
        P("seq", "ctx", None),
        P("seq", None),
        P("ctx", None),
        P("ctx", None),
    )
    out_specs = (P("ctx", None), P("ctx", None))
    return jax.shard_map(shards, mesh=mesh, in_specs=in_specs, out_specs=out_specs, check_vma=False)
```

profile of v0, /device:TPU:1, one launch (start us, length us, event | category | flops | bytes accessed | tf_op | source)
XLA Modules:
  0.0 518.4 jit_solution(14918549334567777085)
XLA Ops:
  7.2 0.0 copy-start
  7.2 0.0 copy-start.1
  7.2 0.0 all-gather.5.cloned.1.call-start
  7.2 1.9 copy.55
  9.2 0.0 all-gather.5.cloned.1.call-update
  9.2 1.0 reduce_max.45
  10.2 0.1 all_to_all.29
  10.3 0.6 copy.53
  10.9 8.7 %all-to-all-start.1 = ((bf16[2,16,64]{2,0,1:T(2,128)(2,1)}), bf16[2,16,64]{2,0,1:T(2,128)(2,1)S(1)}, u32[]{:S(2)}, u32[]{:S(2)}) async-start(bf16[2,16,64]{2,0,1:T(2,128)(2,1)} %copy.53), calls=%async_computation.1 | async-start | bytes 16384 | tf_op jit(solution)/shard_map/all_to_all | solution.py:90
  19.6 2.0 convert_reduce_fusion
  21.6 0.1 iota_compare_fusion
  21.7 0.6 multiply_convert_fusion
  22.4 0.7 dynamic-slice_bitcast_fusion
  23.0 2.4 copy.56
  25.5 3.0 copy.57
  28.5 1.3 dynamic-slice.1
  30.4 7.6 %all-to-all-start = ((bf16[2,16,512]{2,0,1:T(2,128)(2,1)}), bf16[2,16,512]{2,0,1:T(2,128)(2,1)S(1)}, u32[]{:S(2)}, u32[]{:S(2)}) async-start(bf16[2,16,512]{2,0,1:T(2,128)(2,1)} %bitcast.5), calls=%async_computation | async-start | bytes 65536 | tf_op jit(solution)/shard_map/all_to_all | solution.py:89
  38.0 0.1 fusion.24
  38.1 7.3 %all-to-all-done = bf16[2,16,512]{2,0,1:T(2,128)(2,1)S(1)} async-done(((bf16[2,16,512]{2,0,1:T(2,128)(2,1)}), bf16[2,16,512]{2,0,1:T(2,128)(2,1)S(1)}, u32[]{:S(2)}, u32[]{:S(2)}) %all-to-all-start) | async-done | bytes 32800 | tf_op jit(solution)/shard_map/all_to_all | solution.py:89
  45.5 0.0 copy-start.2
  45.5 0.6 copy-done.2
  46.1 0.3 fusion.23
  46.4 53.3 %all-reduce.5 = bf16[32,2048]{1,0:T(8,128)(2,1)S(1)} all-reduce(f32[32,2048]{1,0:T(8,128)S(1)} %pad_maximum_fusion), channel_id=3, replica_groups=mesh['seq'=32,'ctx'=16] {'ctx'}, use_global_device_ids=true, to_apply=%region_2.3.clone | all-reduce | flops 65536 | bytes 393216
  99.8 24.9 %all-gather.1 = bf16[16,2,1024]{2,1,0:T(2,128)(2,1)S(1)} all-gather(bf16[1,2,1024]{2,1,0:T(2,128)(2,1)S(1)} %slice_bitcast_fusion.1), channel_id=1, replica_groups=mesh['seq'=32,'ctx'=16] {'ctx'}, dimensions={0}, use_global_device_ids=true | all-gather | bytes 69632 | tf_op jit(solution)/shard_map/all_gather | solution.py:100
  124.7 0.3 fusion.20
  125.0 0.0 all-gather.5.cloned.1.call-done
  125.1 1.1 broadcast_in_dim.51
  126.2 7.8 %while.20 = (s32[]{:T(128)}, f32[8,8,128]{2,1,0:T(8,128)S(1)}, f32[8,8,128]{2,1,0:T(8,128)S(1)}, f32[8,8,128,32]{2,3,1,0:T(8,128)}, s32[]{:T(128)}, /*index=5*/s...) while((s32[]{:T(128)}, f32[8,8,128]{2,1,0:T(8,128)S(1)}, ...), condition=%wide.region_11.12_spmd.clone, body=%wide.region_5.11_spmd.clone.sunk | while | flops 280019200 | bytes 16160314 | solution.py:63
  126.2 7.0 %conditional.3 = ((f32[8,8,128]{2,1,0:T(8,128)S(1)}, f32[8,8,128]{2,1,0:T(8,128)S(1)}, f32[8,8,128,32]{2,3,1,0:T(8,128)})) conditional(s32[]{:T(128)} %convert_element_type.62, (f32[8,8,128]{2,1,0:T(8,128)S(1)}, f32[8,8,128]{2,1,0:T(8,128)S(1)}, f32[8,8,128,32]{2,3,1,0:T(8,128)}) %tuple.63, (s32[]{:T(128)}, s32[]{:T(128)}, s32[2048]{0:T(1024)}, ...), branch_computations={%region_6.6_spmd, %region_7.10_spmd} | conditional | flops 280019200 | bytes 16159539 | solution.py:61
  126.2 0.8 dynamic_slice.2
  126.9 0.1 compare_and_fusion
  127.1 1.0 constant_dynamic-slice_fusion
  128.0 0.8 fusion.2
  128.9 1.2 select_reduce_fusion
  130.2 1.1 bitcast_reduce_fusion
  131.3 1.8 dynamic_update_slice.2
  134.0 2.4 subtract_exponential_fusion
  136.4 2.5 reshape.56
  138.9 3.2 reduce_max.47
  142.1 1.4 fusion.19
  143.5 0.1 copy.58
  143.6 0.3 fusion.10
  143.8 0.4 fusion.4
  144.2 126.9 %all-gather.2 = bf16[16,2,1024]{2,1,0:T(2,128)(2,1)S(1)} all-gather(bf16[1,2,1024]{2,1,0:T(2,128)(2,1)S(1)} %fusion.10), channel_id=1, replica_groups=mesh['seq'=32,'ctx'=16] {'ctx'}, dimensions={0}, use_global_device_ids=true | all-gather | bytes 69632 | tf_op jit(solution)/shard_map/all_gather | solution.py:134
  271.2 0.5 fusion.25
  271.6 46.7 %all-reduce.6 = bf16[32,8,128]{2,0,1:T(8,128)(2,1)S(1)} all-reduce(f32[32,8,128]{2,0,1:T(8,128)S(1)} %fusion.4), channel_id=1, replica_groups=mesh['seq'=32,'ctx'=16] {'ctx'}, use_global_device_ids=true, to_apply=%region_16.17 | all-reduce | flops 32768 | bytes 196608 | tf_op jit(solution)/shard_map/psum | solution.py:133
  318.3 0.2 fusion.11
  318.5 193.0 %all-reduce.7 = (bf16[512,1024]{1,0:T(8,128)(2,1)}, bf16[64,1024]{1,0:T(8,128)(2,1)}) all-reduce(f32[512,1024]{1,0:T(8,128)S(1)} %fusion.25, f32[64,1024]{1,0:T(8,128)S(1)} %fusion.11), channel_id=1, replica_groups=mesh['seq'=32,'ctx'=16] {'seq'}, use_global_device_ids=true, to_apply=%region_15.16 | all-reduce | flops 589824 | bytes 3538944 | tf_op jit(solution)/shard_map/psum | solution.py:139
  (52 shorter events, 0.5 us)
Async XLA Ops:
  7.2 38.9 %copy-start = (bf16[512,1024]{1,0:T(8,128)(2,1)S(1)}, bf16[512,1024]{1,0:T(8,128)(2,1)}, u32[]{:S(2)}) copy-start(bf16[512,1024]{1,0:T(8,128)(2,1)} %param.12) | copy-start | bytes 3145732
  7.2 15.8 %copy-start.1 = (bf16[1,128,8192]{2,1,0:T(8,128)(2,1)S(1)}, bf16[1,128,8192]{2,1,0:T(8,128)(2,1)}, u32[]{:S(2)}) copy-start(bf16[1,128,8192]{2,1,0:T(8,128)(2,1)} %param.9) | copy-start | bytes 6291460
  7.2 117.9 %all-gather.5.cloned.1.call-start = ((), (), s32[]{:S(2)}) async-start(), calls=%async_computation.2 | async-start | bytes 4456448 | tf_op jit(solution)/shard_map/all_gather | solution.py:29
  10.9 19.5 %all-to-all-start.1 = ((bf16[2,16,64]{2,0,1:T(2,128)(2,1)}), bf16[2,16,64]{2,0,1:T(2,128)(2,1)S(1)}, u32[]{:S(2)}, u32[]{:S(2)}) async-start(bf16[2,16,64]{2,0,1:T(2,128)(2,1)} %copy.53), calls=%async_computation.1 | async-start | bytes 16384 | tf_op jit(solution)/shard_map/all_to_all | solution.py:90
  23.0 15.0 %copy-start.4 = (bf16[64,1024]{1,0:T(8,128)(2,1)S(1)}, bf16[64,1024]{1,0:T(8,128)(2,1)}, u32[]{:S(2)}) copy-start(bf16[64,1024]{1,0:T(8,128)(2,1)} %param.13) | copy-start | bytes 393220
  30.4 15.0 %all-to-all-start = ((bf16[2,16,512]{2,0,1:T(2,128)(2,1)}), bf16[2,16,512]{2,0,1:T(2,128)(2,1)S(1)}, u32[]{:S(2)}, u32[]{:S(2)}) async-start(bf16[2,16,512]{2,0,1:T(2,128)(2,1)} %bitcast.5), calls=%async_computation | async-start | bytes 65536 | tf_op jit(solution)/shard_map/all_to_all | solution.py:89
  45.5 0.6 copy-start.2
  136.4 134.8 %copy-start.3 = (bf16[32,512]{1,0:T(8,128)(2,1)S(1)}, bf16[32,512]{1,0:T(8,128)(2,1)}, u32[]{:S(2)}) copy-start(bf16[32,512]{1,0:T(8,128)(2,1)} %copy-done.2) | copy-start | bytes 98308
Sparse Core Ops, SparseCore 0:
  10.6 91.4 all-gather.4
where the time goes:
time: 523 us; the launch traced here: 518 us
  blocking collectives  445 us (85%)
  local copies, waits for them, and re-layouts  18.1 us (3%)
  starting transfers between devices  16.3 us (3%)
  between operations  14.9 us (3%)
  other arithmetic  13.2 us (3%)
  waiting for transfers between devices  7.35 us (1%)
    psum x1, blocking collectives, shards(): summed_q, summed_k = lax.psum((grad_q, grad_k), 'seq')  193 us
    all_gather x1, blocking collectives, shards(): lax.all_gather(grad_gate_q.reshape(blocks_dev, gate_width), 'ctx', axis=0...  127 us
    unnamed x1, blocking collectives  53.3 us
    psum x1, blocking collectives, shards(): lax.psum(key_part, 'ctx').astype(jnp.bfloat16)  46.7 us
    all_gather x1, blocking collectives, shards(): gate_k_all = lax.all_gather(gate_k_mine, 'ctx', axis=0, tiled=True)  24.9 us
  transfers between devices with their start and end apart: 3, of which 1 were waited for; matrix products, arithmetic and copies ran while one was open for 2% of the time, Pallas kernels for 0%

commit v1 on v0

v1 whole, which is shorter than its diff:
```python
import functools
import math

import jax
import jax.numpy as jnp
from jax import lax
from jax.experimental import pallas as pl
from jax.experimental.pallas import tpu as pltpu
from jax.sharding import Mesh, PartitionSpec as P

HEADS = 64
KV_HEADS = 8
GROUP = 8
HEAD_DIM = 128
GATE_DIM = 128
BLOCK = 64
SHARD = 128
TILE = 256
LOCAL_KV = 4
NUM_BLOCKS = 32
SEQ_AXES = ("z", "xh", "co")
CTX_AXES = ("xl", "y")
SWAP = [(0, 1), (1, 0)]
NEG_FILL = -1e30
EXP2_SCALE = math.log2(math.e) / math.sqrt(HEAD_DIM)


def attention_kernel(sc, q_own, q_recv, k_ref, out_ref, bias_s, m_s, l_s, bm_s, acc_s):
    h = pl.program_id(0)
    n0, n1, xl, y = sc[0], sc[1], sc[2], sc[3]
    lane = lax.broadcasted_iota(jnp.int32, (NUM_BLOCKS, 128), 1)

    @pl.when(h == 0)
    def _():
        acc_s[...] = jnp.zeros_like(acc_s)

    for rs, q_ref in enumerate((q_own, q_recv)):
        half = xl if rs == 0 else 1 - xl
        rank = half * 8 + y
        row0 = rank * SHARD
        first = jnp.where(row0 >= n1, n1, jnp.where(row0 >= n0, n0, 0))
        t_lo = first // TILE
        t_hi = rank // 2 + 1

        @pl.when(h == 0)
        def _():
            rowpos = row0 + lax.broadcasted_iota(jnp.int32, (TILE, SHARD), 1)
            rowstart = jnp.where(rowpos >= n1, n1, jnp.where(rowpos >= n0, n0, 0))

            def fill(t, _):
                kpos = t * TILE + lax.broadcasted_iota(jnp.int32, (TILE, SHARD), 0)
                seen = (kpos <= rowpos) & (kpos >= rowstart)
                bias_s[rs, t] = jnp.where(seen, 0.0, NEG_FILL)
                return 0

            lax.fori_loop(t_lo, t_hi, fill, 0)

        m_s[...] = jnp.full_like(m_s, NEG_FILL)
        l_s[...] = jnp.zeros_like(l_s)
        bm_s[...] = jnp.full_like(bm_s, NEG_FILL)

        def step(t, _):
            parts = []
            for o in range(2):
                j = 2 * t + o
                pos = (j % 8) * 2 + jnp.where(j // 8 != xl, 1, 0)
                parts.append(k_ref[pl.ds(pl.multiple_of(pos * SHARD, SHARD), SHARD), :])
            kt = jnp.concatenate(parts, axis=0)
            bias = bias_s[rs, t]
            for g in range(GROUP):
                s = lax.dot_general(
                    kt,
                    q_ref[:, g * HEAD_DIM : (g + 1) * HEAD_DIM],
                    (((1,), (1,)), ((), ())),
                    preferred_element_type=jnp.float32,
                )
                s = s + bias
                blk = jnp.max(s.reshape(TILE // BLOCK, BLOCK // 8, 8, SHARD), axis=1)
                bm_s[g, pl.ds(t * (TILE // BLOCK), TILE // BLOCK)] = blk
                m_old = m_s[g]
                m_new = jnp.maximum(m_old, jnp.max(blk, axis=0))
                e = jnp.exp2((s.reshape(TILE // 8, 8, SHARD) - m_new[None]) * EXP2_SCALE)
                l_s[g] = l_s[g] * jnp.exp2((m_old - m_new) * EXP2_SCALE) + jnp.sum(e, axis=0)
                m_s[g] = m_new
            return 0

        lax.fori_loop(t_lo, t_hi, step, 0)

        for g in range(GROUP):
            m = m_s[g]
            top = jnp.max(m, axis=0, keepdims=True)
            total = jnp.sum(l_s[g] * jnp.exp2((m - top) * EXP2_SCALE), axis=0, keepdims=True)
            bm = jnp.max(bm_s[g], axis=1)
            p = jnp.exp2((bm - top) * EXP2_SCALE) * (1.0 / total)
            for i in range(2):
                best = jnp.max(p[:, i * BLOCK : (i + 1) * BLOCK], axis=1, keepdims=True)
                col = half * 8 + h * 2 + i
                acc_s[...] += jnp.where(lane == col, best, 0.0)

    @pl.when(h == LOCAL_KV - 1)
    def _():
        raw = acc_s[...]
        norm = raw / jnp.sum(raw, axis=0, keepdims=True)
        out_ref[...] = norm.T[:16, :]


def attention_targets(scalars, q, q_recv, k_all):
    kw = GROUP * HEAD_DIM
    return pl.pallas_call(
        attention_kernel,
        out_shape=jax.ShapeDtypeStruct((16, NUM_BLOCKS), jnp.float32),
        grid_spec=pltpu.PrefetchScalarGridSpec(
            num_scalar_prefetch=1,
            grid=(LOCAL_KV,),
            in_specs=[
                pl.BlockSpec((SHARD, kw), lambda h, sc: (0, sc[2] * LOCAL_KV + h)),
                pl.BlockSpec((SHARD, kw), lambda h, sc: (0, h)),
                pl.BlockSpec((16 * SHARD, HEAD_DIM), lambda h, sc: (0, h)),
            ],
            out_specs=pl.BlockSpec((16, NUM_BLOCKS), lambda h, sc: (0, 0)),
            scratch_shapes=[
                pltpu.VMEM((2, 8, TILE, SHARD), jnp.float32),
                pltpu.VMEM((GROUP, 8, SHARD), jnp.float32),
                pltpu.VMEM((GROUP, 8, SHARD), jnp.float32),
                pltpu.VMEM((GROUP, NUM_BLOCKS, 8, SHARD), jnp.float32),
                pltpu.VMEM((NUM_BLOCKS, 128), jnp.float32),
            ],
        ),
        compiler_params=pltpu.CompilerParams(
            dimension_semantics=("arbitrary",), vmem_limit_bytes=32 * 1024 * 1024
        ),
        cost_estimate=pl.CostEstimate(
            flops=2 * 32 * 128 * 128 * 3072, bytes_accessed=4 << 20, transcendentals=12 << 20
        ),
        name="attention_targets",
    )(scalars, q, q_recv, k_all)


def spread(x, axes, n):
    return lax.all_to_all(
        jnp.broadcast_to(x[None], (n, *x.shape)), axes, split_axis=0, concat_axis=0, tiled=True
    )


def ordered(own, other, index):
    return jnp.where(index == 0, jnp.stack([own, other]), jnp.stack([other, own]))


def shards(queries, keys, doc_ids, gate_query_weight, gate_key_weight):
    xl, y = lax.axis_index("xl"), lax.axis_index("y")
    co, xh = lax.axis_index("co"), lax.axis_index("xh")
    gate_scale = 1.0 / GATE_DIM**0.5
    q, k, doc = queries[0], keys[0], doc_ids[0]
    half_kw, half_qw = k.shape[1] // 2, q.shape[1] // 2

    with jax.named_scope("keys"):
        k_mine = lax.dynamic_slice_in_dim(k, xl * half_kw, half_kw, 1)
        k_other = lax.dynamic_slice_in_dim(k, (1 - xl) * half_kw, half_kw, 1)
        k_recv = lax.ppermute(k_other, "xl", SWAP)
        k_all = lax.all_gather(jnp.concatenate([k_mine, k_recv]), "y", axis=0, tiled=True)
        q_other = lax.dynamic_slice_in_dim(q, (1 - xl) * half_qw, half_qw, 1)
        q_recv = lax.ppermute(q_other, "xl", SWAP)

    with jax.named_scope("pool"):
        pool_q = (
            jnp.sum(q.reshape(2, BLOCK, -1), axis=1, dtype=jnp.float32) / BLOCK
        ).astype(jnp.bfloat16)
        pool_k = jnp.max(k.reshape(2, BLOCK, -1), axis=1)
        mine = jnp.concatenate([pool_q.reshape(2, 16, -1), pool_k.reshape(2, 16, -1)], axis=2)
        pooled = lax.all_to_all(
            mine.transpose(1, 0, 2), CTX_AXES, split_axis=0, concat_axis=0, tiled=True
        ).reshape(NUM_BLOCKS, -1)
    rows_q = gate_query_weight.shape[0]
    rows_k = gate_key_weight.shape[0]
    pooled_q, pooled_k = pooled[:, :rows_q], pooled[:, rows_q:]

    with jax.named_scope("gates"):
        part = jnp.concatenate(
            [
                jnp.dot(pooled_q, gate_query_weight, preferred_element_type=jnp.float32),
                jnp.dot(pooled_k, gate_key_weight, preferred_element_type=jnp.float32),
            ],
            axis=1,
        )
        parts = lax.all_to_all(
            part.reshape(16, 2, -1), CTX_AXES, split_axis=0, concat_axis=0, tiled=True
        )
        gates_mine = jnp.sum(parts, axis=0).astype(jnp.bfloat16)
        gates = spread(gates_mine, CTX_AXES, 16).reshape(NUM_BLOCKS, -1)
        gw = gate_query_weight.shape[1]
        gq = gates[:, :gw].reshape(NUM_BLOCKS, KV_HEADS, GATE_DIM)
        gk = gates[:, gw:].reshape(NUM_BLOCKS, KV_HEADS, GATE_DIM)
        logits = (
            jnp.einsum("ahe,bhe->hab", gq, gk, preferred_element_type=jnp.float32) * gate_scale
        )
        block = jnp.arange(NUM_BLOCKS, dtype=jnp.int32)
        causal = block[None, :] <= block[:, None]
        masked = jnp.where(causal, logits, NEG_FILL)
        peak = jnp.max(masked, axis=-1, keepdims=True)
        weights = jnp.where(causal, jnp.exp(masked - peak), 0.0)
        gate_prob = weights / jnp.sum(weights, axis=-1, keepdims=True)

    with jax.named_scope("pooled_all"):
        hq, hk = rows_q // 2, rows_k // 2

        def half_rows(index):
            return jnp.concatenate(
                [
                    lax.dynamic_slice_in_dim(pooled_q, index * hq, hq, 1),
                    lax.dynamic_slice_in_dim(pooled_k, index * hk, hk, 1),
                ],
                axis=1,
            )

        pair = ordered(half_rows(co), lax.ppermute(half_rows(1 - co), "co", SWAP), co)
        quad = ordered(pair, lax.ppermute(pair, "xh", SWAP), xh)
        pooled_all = lax.all_gather(
            quad.reshape(4 * NUM_BLOCKS, -1), "z", axis=0, tiled=True
        )

    with jax.named_scope("targets"):
        scalars = jnp.stack(
            [
                jnp.sum((doc < 1).astype(jnp.int32)),
                jnp.sum((doc < 2).astype(jnp.int32)),
                xl.astype(jnp.int32),
                y.astype(jnp.int32),
            ]
        )
        mine = attention_targets(scalars, q, q_recv, k_all)
        target = spread(mine, CTX_AXES, 16)
        target = target.reshape(2, 8, 2, LOCAL_KV, 2, NUM_BLOCKS).transpose(0, 3, 2, 1, 4, 5)
        target = target.reshape(KV_HEADS, NUM_BLOCKS, NUM_BLOCKS)

    with jax.named_scope("gate_grads"):
        score_grad = jnp.where(causal, gate_prob - target, 0.0)
        grad_gate_q = (
            jnp.einsum(
                "hab,bhe->hae",
                score_grad,
                gk.astype(jnp.float32),
                precision=lax.Precision.HIGHEST,
            )
            * gate_scale
        ).astype(jnp.bfloat16)
        grad_gate_k = (
            jnp.einsum(
                "hab,ahe->hbe",
                score_grad,
                gq.astype(jnp.float32),
                precision=lax.Precision.HIGHEST,
            )
            * gate_scale
        ).astype(jnp.bfloat16)
        both = jnp.concatenate([grad_gate_q, grad_gate_k], axis=1)
        both = jnp.broadcast_to(both[:, None], (8, 4, 2 * NUM_BLOCKS, GATE_DIM))
        both = lax.all_to_all(
            both.reshape(32, 2 * NUM_BLOCKS, GATE_DIM),
            SEQ_AXES,
            split_axis=0,
            concat_axis=0,
            tiled=True,
        )

    with jax.named_scope("weight_grads"):
        all_q = both[:, :NUM_BLOCKS].reshape(-1, GATE_DIM)
        all_k = both[:, NUM_BLOCKS:].reshape(-1, GATE_DIM)
        piece = jnp.concatenate(
            [
                jnp.dot(pooled_all[:, :hq].T, all_q, preferred_element_type=jnp.float32),
                jnp.dot(pooled_all[:, hq:].T, all_k, preferred_element_type=jnp.float32),
            ]
        ).astype(jnp.bfloat16)
        pieces = spread(piece, "z", 8)
        own = pieces.transpose(1, 0, 2).reshape(hq + hk, -1)
        other = lax.ppermute(own, "co", SWAP)
        out_q = ordered(own[:hq], other[:hq], co).reshape(rows_q, -1)
        out_k = ordered(own[hq:], other[hq:], co).reshape(rows_k, -1)
    return out_q, out_k


def solution(mesh):
    split = Mesh(mesh.devices.reshape(8, 2, 2, 2, 8), (*SEQ_AXES, *CTX_AXES))
    in_specs = (
        P(SEQ_AXES, CTX_AXES, None),
        P(SEQ_AXES, CTX_AXES, None),
        P(SEQ_AXES, None),
        P(CTX_AXES, None),
        P(CTX_AXES, None),
    )
    out_specs = (P(CTX_AXES, None), P(CTX_AXES, None))
    return jax.shard_map(
        shards, mesh=split, in_specs=in_specs, out_specs=out_specs, check_vma=False
    )
```

time: 523 us -> 203 us (0.39)
  blocking collectives: 445 us -> 40.4 us
  starting transfers between devices: 16.3 us -> 70.7 us
  waiting for transfers between devices: 7.35 us -> 35.9 us
  Pallas kernels: 0 us -> 16.1 us
    psum x2 -> x0, blocking collectives: 240 us -> none  [the longest x1 193 us: shards(): summed_q, summed_k = lax.psum((grad_q, grad_k), 'seq')]
    all_gather x2 -> x1, blocking collectives: 152 us -> 22.1 us  [shards(): lax.all_gather(quad.reshape(4 * NUM_BLOCKS, -1), 'z', axis=0, tiled=True)]
    unnamed x1 -> x0, blocking collectives: 53.3 us -> none
    all_to_all x2 -> x5, starting transfers between devices: 16.2 us -> 46.3 us  [the longest x2 17.7 us: spread(): lax.all_to_all(jnp.broadcast_to(x[None], (n, *x.shape)), axes, split_axis...]
    ppermute x0 -> x5, starting transfers between devices: none -> 24.3 us  [the longest x1 10.2 us: shards(): other = lax.ppermute(own, 'co', SWAP)]
    all_to_all x2 -> x5, waiting for transfers between devices: 7.32 us -> 30.7 us  [the longest x2 17.3 us: spread(): lax.all_to_all(jnp.broadcast_to(x[None], (n, *x.shape)), axes, split_axis...]
    all_to_all x0 -> x1, blocking collectives: none -> 18.3 us  [spread(): lax.all_to_all(jnp.broadcast_to(x[None], (n, *x.shape)), axes, split_axis...]
    pallas_call x0 -> x1, Pallas kernels: none -> 16.1 us  [attention_targets(): pl.pallas_call(attention_kernel, out_shape=jax.ShapeDtypeStruct((16, NUM_...]
  transfers between devices with their start and end apart: 3 -> 11, of which waited for: 1 -> 8; matrix products, arithmetic and copies ran while one was open for 2% -> 6% of each run, Pallas kernels for 0% -> 0%
where the time goes in v1:
time: 203 us; the launch traced here: 202 us
  starting transfers between devices  70.7 us (35%)
  blocking collectives  40.4 us (20%)
  waiting for transfers between devices  35.9 us (18%)
  Pallas kernels  16.1 us (8%)
  between operations  14.4 us (7%)
  local copies, waits for them, and re-layouts  13.2 us (7%)
  other arithmetic  8.29 us (4%)
  matrix products  2.64 us (1%)
    all_gather x1, blocking collectives, shards(): lax.all_gather(quad.reshape(4 * NUM_BLOCKS, -1), 'z', axis=0, tiled=True)  22.1 us
    all_to_all x1, blocking collectives, spread(): lax.all_to_all(jnp.broadcast_to(x[None], (n, *x.shape)), axes, split_axis...  18.3 us
    all_to_all x2, starting transfers between devices, spread(): lax.all_to_all(jnp.broadcast_to(x[None], (n, *x.shape)), axes, split_axis...  17.7 us
    all_to_all x1, starting transfers between devices, shards(): lax.all_to_all(both.reshape(32, 2 * NUM_BLOCKS, GATE_DIM), SEQ_AXES, spli...  17.3 us
    all_to_all x2, waiting for transfers between devices, spread(): lax.all_to_all(jnp.broadcast_to(x[None], (n, *x.shape)), axes, split_axis...  17.3 us
    pallas_call x1, Pallas kernels, attention_targets(): pl.pallas_call(attention_kernel, out_shape=jax.ShapeDtypeStruct((16, NUM_...  16.1 us
    ppermute x1, starting transfers between devices, shards(): other = lax.ppermute(own, 'co', SWAP)  10.2 us
    all_to_all x1, starting transfers between devices, shards(): lax.all_to_all(mine.transpose(1, 0, 2), CTX_AXES, split_axis=0, concat_ax...  7.83 us
  transfers between devices with their start and end apart: 11, of which 8 were waited for; matrix products, arithmetic and copies ran while one was open for 6% of the time, Pallas kernels for 0%

profile of v1, /device:TPU:1, one launch (start us, length us, event | category | flops | bytes accessed | tf_op | source)
XLA Modules:
  0.0 201.8 jit_solution(10669908956327253635)
XLA Ops:
  7.2 1.1 dynamic-slice_bitcast_fusion.2
  8.3 3.9 %collective-permute-start.3 = (bf16[128,512]{1,0:T(8,128)(2,1)S(1)}, bf16[128,512]{1,0:T(8,128)(2,1)S(1)}, u32[]{:S(2)}, u32[]{:S(2)}) collective-permute-start(bf16[128,512]{1,0:T(8,128)(2,1)S(1)} %get-tuple-element.7), channel_id=1, source_target_pairs={{0,8},{8,0},{1,9},{9,1},{2,10},{10,2},{3,11},{11,3},{4,12},{12,4},... | collective-permute-start | bytes 393224 | tf_op jit(solution)/shard_map/keys/ppermute | solution.py:159
  12.3 1.0 reduce_max.18
  13.4 2.0 convert_reduce_fusion
  15.4 0.7 pad_maximum_fusion.1
  16.2 0.7 maximum_bitcast_fusion
  16.9 7.8 %all-to-all-start = ((bf16[16,2,576]{2,1,0:T(2,128)(2,1)}), bf16[16,2,576]{2,1,0:T(2,128)(2,1)S(1)}, u32[]{:S(2)}, u32[]{:S(2)}) async-start(bf16[16,2,576]{2,1,0:T(2,128)(2,1)} %maximum_bitcast_fusion), calls=%async_computation | async-start | bytes 81920 | tf_op jit(solution)/shard_map/pool/all_to_all | solution.py:170
  24.7 7.4 %all-to-all-done = bf16[16,2,576]{2,1,0:T(2,128)(2,1)S(1)} async-done(((bf16[16,2,576]{2,1,0:T(2,128)(2,1)}), bf16[16,2,576]{2,1,0:T(2,128)(2,1)S(1)}, u32[]{:S(2)}, u32[]{:S(2)}) %all-to-all-start) | async-done | bytes 36896 | tf_op jit(solution)/shard_map/pool/all_to_all | solution.py:170
  32.1 1.1 fusion.21
  33.2 0.3 fusion.23
  33.5 0.8 reshape.158
  34.4 3.5 %all-to-all-start.1 = ((f32[16,2,2048]{2,1,0:T(2,128)}), f32[16,2,2048]{2,1,0:T(2,128)S(1)}, u32[]{:S(2)}, u32[]{:S(2)}) async-start(f32[16,2,2048]{2,1,0:T(2,128)} %reshape.158), calls=%async_computation.1 | async-start | bytes 524288 | tf_op jit(solution)/shard_map/gates/all_to_all | solution.py:185
  37.9 1.1 dynamic-slice_bitcast_fusion
  39.0 3.2 %collective-permute-start.2 = (bf16[128,4096]{1,0:T(8,128)(2,1)}, bf16[128,4096]{1,0:T(8,128)(2,1)}, u32[]{:S(2)}, u32[]{:S(2)}) collective-permute-start(bf16[128,4096]{1,0:T(8,128)(2,1)} %dynamic-slice_bitcast_fusion), channel_id=1, source_target_pairs={{0,8},{8,0},{1,9},{9,1},{2,10},{10,2},{3,11},{11,3},{4,12},{12,4},... | collective-permute-start | bytes 3145736 | tf_op jit(solution)/shard_map/keys/ppermute | solution.py:162
  42.1 6.0 %all-to-all-done.1 = f32[16,2,2048]{2,1,0:T(2,128)S(1)} async-done(((f32[16,2,2048]{2,1,0:T(2,128)}), f32[16,2,2048]{2,1,0:T(2,128)S(1)}, u32[]{:S(2)}, u32[]{:S(2)}) %all-to-all-start.1) | async-done | bytes 262176 | tf_op jit(solution)/shard_map/gates/all_to_all | solution.py:185
  48.3 0.7 broadcast_in_dim.47
  49.0 5.8 %all-to-all-start.2 = ((bf16[16,2,2048]{2,1,0:T(2,128)(2,1)}), bf16[16,2,2048]{2,1,0:T(2,128)(2,1)S(1)}, u32[]{:S(2)}, u32[]{:S(2)}) async-start(bf16[16,2,2048]{2,1,0:T(2,128)(2,1)} %broadcast_in_dim.47), calls=%async_computation.2 | async-start | bytes 262144 | tf_op jit(solution)/shard_map/gates/all_to_all | solution.py:140
  54.8 0.7 fusion.19
  55.5 1.3 pad_add_fusion.sc
  56.9 10.1 %all-to-all-done.2 = bf16[16,2,2048]{2,1,0:T(2,128)(2,1)S(1)} async-done(((bf16[16,2,2048]{2,1,0:T(2,128)(2,1)}), bf16[16,2,2048]{2,1,0:T(2,128)(2,1)S(1)}, u32[]{:S(2)}, u32[]{:S(2)}) %all-to-all-start.2) | async-done | bytes 131104 | tf_op jit(solution)/shard_map/gates/all_to_all | solution.py:140
  67.0 1.8 all-gather.2.cloned.1.call-done.k_ref
  68.9 1.6 copy-done.2
  70.4 16.1 %attention_targets.1 = f32[16,32]{1,0:T(8,128)S(1)} custom-call(s32[4]{0:T(128)S(1)} %pad_add_fusion.sc, bf16[128,8192]{1,0:T(8,128)(2,1)S(1)} %bitcast.69, bf16[128,4096]{1,0:T(8,128)(2,1)} %collective-permute-done.2.q_recv, bf16[2048,512]{1,0:T(8,128)(2,1)S(1)} %copy-done.2), custom_call_target="tpu_custom_call" | custom-call | flops 3221225472 | bytes 4194304 | tf_op jit(solution)/shard_map/targets/attention_targets/pallas_call | solution.py:109
  86.6 0.7 reshape.169
  87.3 11.9 %all-to-all-start.3 = ((f32[16,1,512]{2,1,0:T(1,128)}), f32[16,1,512]{2,1,0:T(1,128)S(1)}, u32[]{:S(2)}, u32[]{:S(2)}) async-start(f32[16,1,512]{2,1,0:T(1,128)} %reshape.169), calls=%async_computation.3 | async-start | bytes 65536 | tf_op jit(solution)/shard_map/targets/all_to_all | solution.py:140
  99.4 7.1 %all-to-all-done.3 = f32[16,1,512]{2,1,0:T(1,128)S(1)} async-done(((f32[16,1,512]{2,1,0:T(1,128)}), f32[16,1,512]{2,1,0:T(1,128)S(1)}, u32[]{:S(2)}, u32[]{:S(2)}) %all-to-all-start.3) | async-done | bytes 32800 | tf_op jit(solution)/shard_map/targets/all_to_all | solution.py:140
  106.6 0.5 broadcast.35
  107.1 0.7 reduce.2
  108.4 0.3 fusion.5
  108.7 0.9 broadcast_in_dim.51
  109.6 17.3 %all-to-all-start.4 = ((bf16[32,64,128]{2,1,0:T(8,128)(2,1)}), bf16[32,64,128]{2,1,0:T(8,128)(2,1)S(1)}, u32[]{:S(2)}, u32[]{:S(2)}) async-start(bf16[32,64,128]{2,1,0:T(8,128)(2,1)} %bitcast.21), calls=%async_computation.4 | async-start | bytes 1048576 | tf_op jit(solution)/shard_map/gate_grads/all_to_all | solution.py:257
  127.1 2.1 %collective-permute-start = (bf16[32,288]{1,0:T(8,128)(2,1)S(1)}, bf16[32,288]{1,0:T(8,128)(2,1)S(1)}, u32[]{:S(2)}, u32[]{:S(2)}) collective-permute-start(bf16[32,288]{1,0:T(8,128)(2,1)S(1)} %pad_maximum_fusion.5), channel_id=1, source_target_pairs={{0,16},{16,0},{1,17},{17,1},{2,18},{18,2},{3,19},{19,3},{4,20},{20... | collective-permute-start | bytes 55304 | tf_op jit(solution)/shard_map/pooled_all/ppermute | solution.py:215
  129.2 0.9 collective-permute-done
  130.2 4.8 %collective-permute-start.1 = (bf16[2,32,288]{2,1,0:T(8,128)(2,1)S(1)}, bf16[2,32,288]{2,1,0:T(8,128)(2,1)S(1)}, u32[]{:S(2)}, u32[]{:S(2)}) collective-permute-start(bf16[2,32,288]{2,1,0:T(8,128)(2,1)S(1)} %maximum_select_fusion.4), channel_id=1, source_target_pairs={{0,32},{32,0},{1,33},{33,1},{2,34},{34,2},{3,35},{35,3},{4,36},{36... | collective-permute-start | bytes 110600 | tf_op jit(solution)/shard_map/pooled_all/ppermute | solution.py:216
  135.0 1.9 collective-permute-done.1
  137.0 22.1 %all_gather.6 = bf16[1024,288]{1,0:T(8,128)(2,1)S(1)} all-gather(bf16[128,288]{1,0:T(8,128)(2,1)S(1)} %bitcast.80), channel_id=1, replica_groups=mesh['z'=8,'xh'=2,'co'=2,'xl'=2,'y'=8] {'z'}, dimensions={0}, use_global_device_ids=true | all-gather | bytes 663552 | tf_op jit(solution)/shard_map/pooled_all/all_gather | solution.py:217
  159.1 0.2 convolution_convert_fusion.1
  159.3 0.4 convolution_convert_fusion
  159.8 18.3 %all_to_all.30 = bf16[8,288,128]{2,1,0:T(8,128)(2,1)S(1)} all-to-all(bf16[8,288,128]{2,1,0:T(8,128)(2,1)S(1)} %broadcast_in_dim.52), channel_id=1, replica_groups=mesh['z'=8,'xh'=2,'co'=2,'xl'=2,'y'=8] {'z'}, dimensions={0} | all-to-all | bytes 1179648 | tf_op jit(solution)/shard_map/weight_grads/all_to_all | solution.py:140
  178.1 0.9 copy_bitcast_fusion
  179.0 10.2 %collective-permute-start.4 = (bf16[288,1024]{1,0:T(8,128)(2,1)}, bf16[288,1024]{1,0:T(8,128)(2,1)S(1)}, u32[]{:S(2)}, u32[]{:S(2)}) collective-permute-start(bf16[288,1024]{1,0:T(8,128)(2,1)} %copy_bitcast_fusion), channel_id=1, source_target_pairs={{0,16},{16,0},{1,17},{17,1},{2,18},{18,2},{3,19},{19,3},{4,20},{20... | collective-permute-start | bytes 1769480 | tf_op jit(solution)/shard_map/weight_grads/ppermute | solution.py:276
  189.3 0.4 copy.66
  189.7 0.8 copy.73
  190.5 0.6 collective-permute-done.4
  191.3 0.6 copy-done.3
  192.1 1.3 copy.69
  193.4 0.8 slice_bitcast_fusion
  194.2 0.7 maximum_select_fusion.1
  (53 shorter events, 2.0 us)
Async XLA Ops:
  7.2 26.0 %copy-start = (bf16[512,1024]{1,0:T(8,128)(2,1)S(1)}, bf16[512,1024]{1,0:T(8,128)(2,1)}, u32[]{:S(2)}) copy-start(bf16[512,1024]{1,0:T(8,128)(2,1)} %param.8) | copy-start | bytes 3145732
  7.2 61.7 %all-gather.2.cloned.1.call-start = ((), (), s32[]{:S(2)}) async-start(), calls=%async_computation.6 | async-start | bytes 2359296 | tf_op jit(solution)/shard_map/keys/all_gather | solution.py:160
  8.3 7.1 %collective-permute-start.3 = (bf16[128,512]{1,0:T(8,128)(2,1)S(1)}, bf16[128,512]{1,0:T(8,128)(2,1)S(1)}, u32[]{:S(2)}, u32[]{:S(2)}) collective-permute-start(bf16[128,512]{1,0:T(8,128)(2,1)S(1)} %get-tuple-element.7), channel_id=1, source_target_pairs={{0,8},{8,0},{1,9},{9,1},{2,10},{10,2},{3,11},{11,3},{4,12},{12,4},... | collective-permute-start | bytes 393224 | tf_op jit(solution)/shard_map/keys/ppermute | solution.py:159
  15.4 22.5 %copy-start.1 = (bf16[1,128,8192]{2,1,0:T(8,128)(2,1)S(1)}, bf16[1,128,8192]{2,1,0:T(8,128)(2,1)}, u32[]{:S(2)}) copy-start(bf16[1,128,8192]{2,1,0:T(8,128)(2,1)} %param.5) | copy-start | bytes 6291460
  16.9 15.2 %all-to-all-start = ((bf16[16,2,576]{2,1,0:T(2,128)(2,1)}), bf16[16,2,576]{2,1,0:T(2,128)(2,1)S(1)}, u32[]{:S(2)}, u32[]{:S(2)}) async-start(bf16[16,2,576]{2,1,0:T(2,128)(2,1)} %maximum_bitcast_fusion), calls=%async_computation | async-start | bytes 81920 | tf_op jit(solution)/shard_map/pool/all_to_all | solution.py:170
  32.1 24.8 %copy-start.4 = (bf16[32,576]{1,0:T(8,128)(2,1)}, bf16[32,576]{1,0:T(8,128)(2,1)S(1)}, u32[]{:S(2)}) copy-start(bf16[32,576]{1,0:T(8,128)(2,1)S(1)} %reshape.157) | copy-start | bytes 110596
  33.5 21.3 %copy-start.6 = (s32[1,2048]{1,0:T(1,128)S(1)}, s32[1,2048]{1,0:T(1,128)}, u32[]{:S(2)}) copy-start(s32[1,2048]{1,0:T(1,128)} %param.7) | copy-start | bytes 24580
  34.4 13.8 %all-to-all-start.1 = ((f32[16,2,2048]{2,1,0:T(2,128)}), f32[16,2,2048]{2,1,0:T(2,128)S(1)}, u32[]{:S(2)}, u32[]{:S(2)}) async-start(f32[16,2,2048]{2,1,0:T(2,128)} %reshape.158), calls=%async_computation.1 | async-start | bytes 524288 | tf_op jit(solution)/shard_map/gates/all_to_all | solution.py:185
  39.0 28.1 %collective-permute-start.2 = (bf16[128,4096]{1,0:T(8,128)(2,1)}, bf16[128,4096]{1,0:T(8,128)(2,1)}, u32[]{:S(2)}, u32[]{:S(2)}) collective-permute-start(bf16[128,4096]{1,0:T(8,128)(2,1)} %dynamic-slice_bitcast_fusion), channel_id=1, source_target_pairs={{0,8},{8,0},{1,9},{9,1},{2,10},{10,2},{3,11},{11,3},{4,12},{12,4},... | collective-permute-start | bytes 3145736 | tf_op jit(solution)/shard_map/keys/ppermute | solution.py:162
  49.0 17.9 %all-to-all-start.2 = ((bf16[16,2,2048]{2,1,0:T(2,128)(2,1)}), bf16[16,2,2048]{2,1,0:T(2,128)(2,1)S(1)}, u32[]{:S(2)}, u32[]{:S(2)}) async-start(bf16[16,2,2048]{2,1,0:T(2,128)(2,1)} %broadcast_in_dim.47), calls=%async_computation.2 | async-start | bytes 262144 | tf_op jit(solution)/shard_map/gates/all_to_all | solution.py:140
  68.9 1.6 copy-start.2
  87.3 19.3 %all-to-all-start.3 = ((f32[16,1,512]{2,1,0:T(1,128)}), f32[16,1,512]{2,1,0:T(1,128)S(1)}, u32[]{:S(2)}, u32[]{:S(2)}) async-start(f32[16,1,512]{2,1,0:T(1,128)} %reshape.169), calls=%async_computation.3 | async-start | bytes 65536 | tf_op jit(solution)/shard_map/targets/all_to_all | solution.py:140
  107.8 19.1 %slice-start = ((bf16[32,576]{1,0:T(8,128)(2,1)}), bf16[32,64]{1,0:T(8,128)(2,1)S(1)}, s32[]{:S(2)}) async-start(bf16[32,576]{1,0:T(8,128)(2,1)} %copy-done.4), calls=%async_computation.7 | async-start | bytes 16384 | tf_op jit(solution)/shard_map/slice | solution.py:175
  107.9 19.1 %slice-start.1 = ((bf16[32,576]{1,0:T(8,128)(2,1)}), bf16[32,512]{1,0:T(8,128)(2,1)S(1)}, s32[]{:S(2)}) async-start(bf16[32,576]{1,0:T(8,128)(2,1)} %copy-done.4), calls=%async_computation.8 | async-start | bytes 65536 | tf_op jit(solution)/shard_map/slice | solution.py:175
  109.6 49.4 %all-to-all-start.4 = ((bf16[32,64,128]{2,1,0:T(8,128)(2,1)}), bf16[32,64,128]{2,1,0:T(8,128)(2,1)S(1)}, u32[]{:S(2)}, u32[]{:S(2)}) async-start(bf16[32,64,128]{2,1,0:T(8,128)(2,1)} %bitcast.21), calls=%async_computation.4 | async-start | bytes 1048576 | tf_op jit(solution)/shard_map/gate_grads/all_to_all | solution.py:257
  127.1 3.1 %collective-permute-start = (bf16[32,288]{1,0:T(8,128)(2,1)S(1)}, bf16[32,288]{1,0:T(8,128)(2,1)S(1)}, u32[]{:S(2)}, u32[]{:S(2)}) collective-permute-start(bf16[32,288]{1,0:T(8,128)(2,1)S(1)} %pad_maximum_fusion.5), channel_id=1, source_target_pairs={{0,16},{16,0},{1,17},{17,1},{2,18},{18,2},{3,19},{19,3},{4,20},{20... | collective-permute-start | bytes 55304 | tf_op jit(solution)/shard_map/pooled_all/ppermute | solution.py:215
  130.2 6.7 %collective-permute-start.1 = (bf16[2,32,288]{2,1,0:T(8,128)(2,1)S(1)}, bf16[2,32,288]{2,1,0:T(8,128)(2,1)S(1)}, u32[]{:S(2)}, u32[]{:S(2)}) collective-permute-start(bf16[2,32,288]{2,1,0:T(8,128)(2,1)S(1)} %maximum_select_fusion.4), channel_id=1, source_target_pairs={{0,32},{32,0},{1,33},{33,1},{2,34},{34,2},{3,35},{35,3},{4,36},{36... | collective-permute-start | bytes 110600 | tf_op jit(solution)/shard_map/pooled_all/ppermute | solution.py:216
  179.0 12.1 %collective-permute-start.4 = (bf16[288,1024]{1,0:T(8,128)(2,1)}, bf16[288,1024]{1,0:T(8,128)(2,1)S(1)}, u32[]{:S(2)}, u32[]{:S(2)}) collective-permute-start(bf16[288,1024]{1,0:T(8,128)(2,1)} %copy_bitcast_fusion), channel_id=1, source_target_pairs={{0,16},{16,0},{1,17},{17,1},{2,18},{18,2},{3,19},{19,3},{4,20},{20... | collective-permute-start | bytes 1769480 | tf_op jit(solution)/shard_map/weight_grads/ppermute | solution.py:276
  191.1 0.8 copy-start.3
  191.9 2.3 %copy-start.5 = (bf16[1,32,1024]{2,1,0:T(8,128)(2,1)S(1)}, bf16[1,32,1024]{2,1,0:T(8,128)(2,1)}, u32[]{:S(2)}) copy-start(bf16[1,32,1024]{2,1,0:T(8,128)(2,1)} %copy.73) | copy-start | bytes 196612
Sparse Core Ops, SparseCore 0:
  16.3 52.5 all-gather.1

commit v2 on v1

--- a/solution.py
+++ b/solution.py
@@ -15,7 +15,8 @@
 GATE_DIM = 128
 BLOCK = 64
 SHARD = 128
-TILE = 256
+PANEL = 1024
+FOLDED = [0, 4, 2, 6, 1, 5, 3, 7]
 LOCAL_KV = 4
 NUM_BLOCKS = 32
 SEQ_AXES = ("z", "xh", "co")
@@ -25,86 +26,119 @@
 EXP2_SCALE = math.log2(math.e) / math.sqrt(HEAD_DIM)
 
 
-def attention_kernel(sc, q_own, q_recv, k_ref, out_ref, bias_s, m_s, l_s, bm_s, acc_s):
+def attention_kernel(
+    sc, q_own, q_recv, k_ref, after, out_ref, bias_s, k_s, q_s, s0, s1, s2, m_s, l_s, bm_s, acc_s
+):
     h = pl.program_id(0)
     n0, n1, xl, y = sc[0], sc[1], sc[2], sc[3]
-    lane = lax.broadcasted_iota(jnp.int32, (NUM_BLOCKS, 128), 1)
+    slots = (s0, s1, s2)
+    sub = lax.broadcasted_iota(jnp.int32, (8, SHARD), 0)
+    lane = lax.broadcasted_iota(jnp.int32, (NUM_BLOCKS // 2, 128), 1)
+    left = lane < BLOCK
+
+    def fold(first, second, span):
+        low = (sub & span) == 0
+        kept = jnp.where(low, first, second)
+        moved = jnp.where(low, second, first)
+        if span == 4:
+            return jnp.maximum(kept, pltpu.roll(moved, 4, 0))
+        turned = jnp.where(low, pltpu.roll(moved, 8 - span, 0), pltpu.roll(moved, span, 0))
+        return jnp.maximum(kept, turned)
+
+    panels = ((0, 0), (1, 0), (1, 1))
 
     @pl.when(h == 0)
     def _():
         acc_s[...] = jnp.zeros_like(acc_s)
-
-    for rs, q_ref in enumerate((q_own, q_recv)):
-        half = xl if rs == 0 else 1 - xl
-        rank = half * 8 + y
-        row0 = rank * SHARD
-        first = jnp.where(row0 >= n1, n1, jnp.where(row0 >= n0, n0, 0))
-        t_lo = first // TILE
-        t_hi = rank // 2 + 1
-
-        @pl.when(h == 0)
-        def _():
-            rowpos = row0 + lax.broadcasted_iota(jnp.int32, (TILE, SHARD), 1)
+        for at, (half, panel) in enumerate(panels):
+            rowpos = (half * 8 + y) * SHARD + lax.broadcasted_iota(jnp.int32, (PANEL, SHARD), 1)
             rowstart = jnp.where(rowpos >= n1, n1, jnp.where(rowpos >= n0, n0, 0))
-
-            def fill(t, _):
-                kpos = t * TILE + lax.broadcasted_iota(jnp.int32, (TILE, SHARD), 0)
-                seen = (kpos <= rowpos) & (kpos >= rowstart)
-                bias_s[rs, t] = jnp.where(seen, 0.0, NEG_FILL)
-                return 0
-
-            lax.fori_loop(t_lo, t_hi, fill, 0)
-
-        m_s[...] = jnp.full_like(m_s, NEG_FILL)
-        l_s[...] = jnp.zeros_like(l_s)
-        bm_s[...] = jnp.full_like(bm_s, NEG_FILL)
-
-        def step(t, _):
-            parts = []
-            for o in range(2):
-                j = 2 * t + o
-                pos = (j % 8) * 2 + jnp.where(j // 8 != xl, 1, 0)
-                parts.append(k_ref[pl.ds(pl.multiple_of(pos * SHARD, SHARD), SHARD), :])
-            kt = jnp.concatenate(parts, axis=0)
-            bias = bias_s[rs, t]
-            for g in range(GROUP):
-                s = lax.dot_general(
-                    kt,
-                    q_ref[:, g * HEAD_DIM : (g + 1) * HEAD_DIM],
-                    (((1,), (1,)), ((), ())),
-                    preferred_element_type=jnp.float32,
-                )
-                s = s + bias
-                blk = jnp.max(s.reshape(TILE // BLOCK, BLOCK // 8, 8, SHARD), axis=1)
-                bm_s[g, pl.ds(t * (TILE // BLOCK), TILE // BLOCK)] = blk
-                m_old = m_s[g]
-                m_new = jnp.maximum(m_old, jnp.max(blk, axis=0))
-                e = jnp.exp2((s.reshape(TILE // 8, 8, SHARD) - m_new[None]) * EXP2_SCALE)
-                l_s[g] = l_s[g] * jnp.exp2((m_old - m_new) * EXP2_SCALE) + jnp.sum(e, axis=0)
-                m_s[g] = m_new
-            return 0
-
-        lax.fori_loop(t_lo, t_hi, step, 0)
-
+            kpos = panel * PANEL + lax.broadcasted_iota(jnp.int32, (PANEL, SHARD), 0)
+            seen = (kpos <= rowpos) & (kpos >= rowstart)
+            bias_s[at] = jnp.where(seen, 0.0, NEG_FILL)
+
+    for j in range(16):
+        pos = (j % 8) * 2 + jnp.where(xl == j // 8, 0, 1)
+        shard = k_ref[pl.ds(pl.multiple_of(pos * SHARD, SHARD), SHARD), :]
+        k_s[j * SHARD : (j + 1) * SHARD, :HEAD_DIM] = shard
+        k_s[j * SHARD : (j + 1) * SHARD, HEAD_DIM:] = shard
+    for g in range(GROUP):
+        rows = slice(g * SHARD, (g + 1) * SHARD)
+        own = q_own[:, g * HEAD_DIM : (g + 1) * HEAD_DIM].astype(jnp.float32)
+        recv = q_recv[:, g * HEAD_DIM : (g + 1) * HEAD_DIM].astype(jnp.float32)
+        for half in range(2):
+            scaled = jnp.where(xl == half, own, recv) * EXP2_SCALE
+            high = scaled.astype(jnp.bfloat16)
+            q_s[half, rows, :HEAD_DIM] = high
+            q_s[half, rows, HEAD_DIM:] = (scaled - high.astype(jnp.float32)).astype(jnp.bfloat16)
+
+    def scores(item):
+        pair, at = divmod(item, 3)
+        half, panel = panels[at]
+        slots[at][...] = lax.dot_general(
+            k_s[panel * PANEL : (panel + 1) * PANEL, :],
+            q_s[half, pair * 2 * SHARD : (pair + 1) * 2 * SHARD, :],
+            (((1,), (1,)), ((), ())),
+            preferred_element_type=jnp.float32,
+        )
+
+    def absorb(item):
+        pair, at = divmod(item, 3)
+        half, panel = panels[at]
+        for o in range(2):
+            cols = slice(o * SHARD, (o + 1) * SHARD)
+            g = pair * 2 + o
+            blks = []
+            for b in range(PANEL // BLOCK):
+                rows = slice(b * BLOCK, (b + 1) * BLOCK)
+                s = slots[at][rows, cols] + bias_s[at, rows, :]
+                slots[at][rows, cols] = s
+                blks.append(jnp.max(s.reshape(BLOCK // 8, 8, SHARD), axis=0))
+            top = functools.reduce(jnp.maximum, blks)
+            for w in range(PANEL // BLOCK // 8):
+                v = [blks[w * 8 + i] for i in FOLDED]
+                for span in (4, 2, 1):
+                    v = [fold(v[2 * i], v[2 * i + 1], span) for i in range(len(v) // 2)]
+                bm_s[half, g, panel * 2 + w] = v[0]
+            if panel == 1:
+                m_old = m_s[half, g]
+                top = jnp.maximum(m_old, top)
+            e = jnp.exp2(slots[at][:, cols].reshape(PANEL // 8, 8, SHARD) - top[None])
+            total = jnp.sum(e, axis=0)
+            if panel == 1:
+                total = total + l_s[half, g] * jnp.exp2(m_old - top)
+            l_s[half, g] = total
+            m_s[half, g] = top
+
+    scores(0)
+    for item in range(3 * GROUP // 2):
+        if item + 1 < 3 * GROUP // 2:
+            scores(item + 1)
+        absorb(item)
+
+    for half in range(2):
         for g in range(GROUP):
-            m = m_s[g]
+            m = m_s[half, g]
             top = jnp.max(m, axis=0, keepdims=True)
-            total = jnp.sum(l_s[g] * jnp.exp2((m - top) * EXP2_SCALE), axis=0, keepdims=True)
-            bm = jnp.max(bm_s[g], axis=1)
-            p = jnp.exp2((bm - top) * EXP2_SCALE) * (1.0 / total)
-            for i in range(2):
-                best = jnp.max(p[:, i * BLOCK : (i + 1) * BLOCK], axis=1, keepdims=True)
-                col = half * 8 + h * 2 + i
-                acc_s[...] += jnp.where(lane == col, best, 0.0)
+            total = jnp.sum(l_s[half, g] * jnp.exp2(m - top), axis=0, keepdims=True)
+            lse = top + jnp.log2(total)
+            for panel in range(half + 1):
+                bm = bm_s[half, g, panel * 2 : panel * 2 + 2].reshape(NUM_BLOCKS // 2, SHARD)
+                gap = bm - lse
+                for i in range(2):
+                    held = jnp.where(left if i == 0 else ~left, gap, NEG_FILL)
+                    best = jnp.exp2(jnp.max(held, axis=1, keepdims=True))
+                    col = half * 8 + h * 2 + i
+                    acc_s[panel] += jnp.where(lane == col, best, 0.0)
 
     @pl.when(h == LOCAL_KV - 1)
     def _():
-        raw = acc_s[...]
+        raw = acc_s[...].reshape(NUM_BLOCKS, 128)
         norm = raw / jnp.sum(raw, axis=0, keepdims=True)
         out_ref[...] = norm.T[:16, :]
 
 
-def attention_targets(scalars, q, q_recv, k_all):
+def attention_targets(scalars, q, q_recv, k_all, after):
     kw = GROUP * HEAD_DIM
     return pl.pallas_call(
         attention_kernel,
@@ -116,14 +150,18 @@
                 pl.BlockSpec((SHARD, kw), lambda h, sc: (0, sc[2] * LOCAL_KV + h)),
                 pl.BlockSpec((SHARD, kw), lambda h, sc: (0, h)),
                 pl.BlockSpec((16 * SHARD, HEAD_DIM), lambda h, sc: (0, h)),
+                pl.BlockSpec(memory_space=pl.ANY),
             ],
             out_specs=pl.BlockSpec((16, NUM_BLOCKS), lambda h, sc: (0, 0)),
             scratch_shapes=[
-                pltpu.VMEM((2, 8, TILE, SHARD), jnp.float32),
-                pltpu.VMEM((GROUP, 8, SHARD), jnp.float32),
-                pltpu.VMEM((GROUP, 8, SHARD), jnp.float32),
-                pltpu.VMEM((GROUP, NUM_BLOCKS, 8, SHARD), jnp.float32),
-                pltpu.VMEM((NUM_BLOCKS, 128), jnp.float32),
+                pltpu.VMEM((3, PANEL, SHARD), jnp.float32),
+                pltpu.VMEM((2 * PANEL, 2 * HEAD_DIM), jnp.bfloat16),
+                pltpu.VMEM((2, GROUP * SHARD, 2 * HEAD_DIM), jnp.bfloat16),
+                *[pltpu.VMEM((PANEL, 2 * SHARD), jnp.float32) for _ in range(3)],
+                pltpu.VMEM((2, GROUP, 8, SHARD), jnp.float32),
+                pltpu.VMEM((2, GROUP, 8, SHARD), jnp.float32),
+                pltpu.VMEM((2, GROUP, 4, 8, SHARD), jnp.float32),
+                pltpu.VMEM((2, NUM_BLOCKS // 2, 128), jnp.float32),
             ],
         ),
         compiler_params=pltpu.CompilerParams(
@@ -133,7 +171,32 @@
             flops=2 * 32 * 128 * 128 * 3072, bytes_accessed=4 << 20, transcendentals=12 << 20
         ),
         name="attention_targets",
-    )(scalars, q, q_recv, k_all)
+    )(scalars, q, q_recv, k_all, after)
+
+
+def assemble_kernel(sc, own, other, out_q, out_k):
+    hq, hk = out_q.shape[0] // 2, out_k.shape[0] // 2
+    for ref, core in ((own, sc[0]), (other, 1 - sc[0])):
+        for z in range(KV_HEADS):
+            cols = slice(z * GATE_DIM, (z + 1) * GATE_DIM)
+            out_q[pl.ds(pl.multiple_of(core * hq, hq), hq), cols] = ref[z, :hq, :]
+            out_k[pl.ds(pl.multiple_of(core * hk, hk), hk), cols] = ref[z, hq:, :]
+
+
+def assembled(co, own, other, rows_q, rows_k):
+    width = KV_HEADS * GATE_DIM
+    return pl.pallas_call(
+        assemble_kernel,
+        out_shape=(
+            jax.ShapeDtypeStruct((rows_q, width), jnp.bfloat16),
+            jax.ShapeDtypeStruct((rows_k, width), jnp.bfloat16),
+        ),
+        in_specs=[pl.BlockSpec(memory_space=pltpu.SMEM)]
+        + [pl.BlockSpec(memory_space=pltpu.VMEM)] * 2,
+        out_specs=(pl.BlockSpec(memory_space=pltpu.VMEM),) * 2,
+        compiler_params=pltpu.CompilerParams(vmem_limit_bytes=8 * 1024 * 1024),
+        name="assembled",
+    )(co.astype(jnp.int32).reshape(1), own, other)
 
 
 def spread(x, axes, n):
@@ -201,22 +264,10 @@
         gate_prob = weights / jnp.sum(weights, axis=-1, keepdims=True)
 
     with jax.named_scope("pooled_all"):
-        hq, hk = rows_q // 2, rows_k // 2
-
-        def half_rows(index):
-            return jnp.concatenate(
-                [
-                    lax.dynamic_slice_in_dim(pooled_q, index * hq, hq, 1),
-                    lax.dynamic_slice_in_dim(pooled_k, index * hk, hk, 1),
-                ],
-                axis=1,
-            )
-
-        pair = ordered(half_rows(co), lax.ppermute(half_rows(1 - co), "co", SWAP), co)
+        pair = ordered(pooled, lax.ppermute(pooled, "co", SWAP), co)
         quad = ordered(pair, lax.ppermute(pair, "xh", SWAP), xh)
-        pooled_all = lax.all_gather(
-            quad.reshape(4 * NUM_BLOCKS, -1), "z", axis=0, tiled=True
-        )
+        quad = quad.reshape(4 * NUM_BLOCKS, -1)
+        pooled_all = lax.all_gather(quad, "z", axis=0, tiled=True)
 
     with jax.named_scope("targets"):
         scalars = jnp.stack(
@@ -227,7 +278,7 @@
                 y.astype(jnp.int32),
             ]
         )
-        mine = attention_targets(scalars, q, q_recv, k_all)
+        mine = attention_targets(scalars, q, q_recv, k_all, quad)
         target = spread(mine, CTX_AXES, 16)
         target = target.reshape(2, 8, 2, LOCAL_KV, 2, NUM_BLOCKS).transpose(0, 3, 2, 1, 4, 5)
         target = target.reshape(KV_HEADS, NUM_BLOCKS, NUM_BLOCKS)
@@ -265,17 +316,17 @@
     with jax.named_scope("weight_grads"):
         all_q = both[:, :NUM_BLOCKS].reshape(-1, GATE_DIM)
         all_k = both[:, NUM_BLOCKS:].reshape(-1, GATE_DIM)
+        hq, hk = rows_q // 2, rows_k // 2
+        grad_q = jnp.dot(pooled_all[:, :rows_q].T, all_q, preferred_element_type=jnp.float32)
+        grad_k = jnp.dot(pooled_all[:, rows_q:].T, all_k, preferred_element_type=jnp.float32)
         piece = jnp.concatenate(
             [
-                jnp.dot(pooled_all[:, :hq].T, all_q, preferred_element_type=jnp.float32),
-                jnp.dot(pooled_all[:, hq:].T, all_k, preferred_element_type=jnp.float32),
+                lax.dynamic_slice_in_dim(grad_q, co * hq, hq, 0),
+                lax.dynamic_slice_in_dim(grad_k, co * hk, hk, 0),
             ]
         ).astype(jnp.bfloat16)
         pieces = spread(piece, "z", 8)
-        own = pieces.transpose(1, 0, 2).reshape(hq + hk, -1)
-        other = lax.ppermute(own, "co", SWAP)
-        out_q = ordered(own[:hq], other[:hq], co).reshape(rows_q, -1)
-        out_k = ordered(own[hq:], other[hq:], co).reshape(rows_k, -1)
+        out_q, out_k = assembled(co, pieces, lax.ppermute(pieces, "co", SWAP), rows_q, rows_k)
     return out_q, out_k
 
 

time: 203 us -> 183 us (0.901)
  blocking collectives: 40.4 us -> 22.7 us
  starting transfers between devices: 70.7 us -> 60.5 us
  Pallas kernels: 16.1 us -> 20 us
  waiting for transfers between devices: 35.9 us -> 39.5 us
  local copies, waits for them, and re-layouts: 13.2 us -> 10.3 us
  other arithmetic: 8.29 us -> 10.9 us
    all_gather x1 -> x0, blocking collectives: 22.1 us -> none  [shards(): lax.all_gather(quad.reshape(4 * NUM_BLOCKS, -1), 'z', axis=0, tiled=True)]
    all_to_all x1, waiting for transfers between devices: 0.01 us -> 17 us  [shards(): lax.all_to_all(both.reshape(32, 2 * NUM_BLOCKS, GATE_DIM), SEQ_AXES, spli...]
    all_to_all x2, waiting for transfers between devices: 17.3 us -> 7.15 us  [spread(): lax.all_to_all(jnp.broadcast_to(x[None], (n, *x.shape)), axes, split_axis...]
    all_to_all x1, waiting for transfers between devices: 6.05 us -> 0.01 us  [shards(): lax.all_to_all(part.reshape(16, 2, -1), CTX_AXES, split_axis=0, concat_ax...]
    all_to_all x2, starting transfers between devices: 17.7 us -> 12.4 us  [spread(): lax.all_to_all(jnp.broadcast_to(x[None], (n, *x.shape)), axes, split_axis...]
    ppermute x1, waiting for transfers between devices: 1.9 us -> 6.27 us  [shards(): quad = ordered(pair, lax.ppermute(pair, 'xh', SWAP), xh)]
    all_to_all x1, blocking collectives: 18.3 us -> 22.7 us  [spread(): lax.all_to_all(jnp.broadcast_to(x[None], (n, *x.shape)), axes, split_axis...]
    ppermute x2, starting transfers between devices: 12.4 us -> 9.23 us  [the longest x1 5.86 us: shards(): pair = ordered(pooled, lax.ppermute(pooled, 'co', SWAP), co)]
  transfers between devices with their start and end apart: 11 -> 12, of which waited for: 8 -> 5; matrix products, arithmetic and copies ran while one was open for 6% -> 9% of each run, Pallas kernels for 0% -> 10%
where the time goes in v2:
time: 183 us; the launch traced here: 182 us
  starting transfers between devices  60.5 us (33%)
  waiting for transfers between devices  39.5 us (22%)
  blocking collectives  22.7 us (12%)
  Pallas kernels  20 us (11%)
  between operations  14.4 us (8%)
  other arithmetic  10.9 us (6%)
  local copies, waits for them, and re-layouts  10.3 us (6%)
  matrix products  4.04 us (2%)
    all_to_all x1, blocking collectives, spread(): lax.all_to_all(jnp.broadcast_to(x[None], (n, *x.shape)), axes, split_axis...  22.7 us
    pallas_call x1, Pallas kernels, attention_targets(): pl.pallas_call(attention_kernel, out_shape=jax.ShapeDtypeStruct((16, NUM_...  18.7 us
    all_to_all x1, waiting for transfers between devices, shards(): lax.all_to_all(both.reshape(32, 2 * NUM_BLOCKS, GATE_DIM), SEQ_AXES, spli...  17 us
    all_to_all x1, starting transfers between devices, shards(): lax.all_to_all(both.reshape(32, 2 * NUM_BLOCKS, GATE_DIM), SEQ_AXES, spli...  16.3 us
    all_to_all x2, starting transfers between devices, spread(): lax.all_to_all(jnp.broadcast_to(x[None], (n, *x.shape)), axes, split_axis...  12.4 us
    all_to_all x1, starting transfers between devices, shards(): lax.all_to_all(mine.transpose(1, 0, 2), CTX_AXES, split_axis=0, concat_ax...  7.94 us
    all_to_all x1, waiting for transfers between devices, shards(): lax.all_to_all(mine.transpose(1, 0, 2), CTX_AXES, split_axis=0, concat_ax...  7.35 us
    all_to_all x2, waiting for transfers between devices, spread(): lax.all_to_all(jnp.broadcast_to(x[None], (n, *x.shape)), axes, split_axis...  7.15 us
  transfers between devices with their start and end apart: 12, of which 5 were waited for; matrix products, arithmetic and copies ran while one was open for 9% of the time, Pallas kernels for 10%

profile of v2, /device:TPU:1, one launch (start us, length us, event | category | flops | bytes accessed | tf_op | source)
XLA Modules:
  0.0 182.4 jit_solution(9545823903885640162)
XLA Ops:
  7.2 1.1 dynamic-slice_bitcast_fusion.2
  8.3 4.0 %collective-permute-start.3 = (bf16[128,512]{1,0:T(8,128)(2,1)S(1)}, bf16[128,512]{1,0:T(8,128)(2,1)}, u32[]{:S(2)}, u32[]{:S(2)}) collective-permute-start(bf16[128,512]{1,0:T(8,128)(2,1)S(1)} %get-tuple-element.7), channel_id=1, source_target_pairs={{0,8},{8,0},{1,9},{9,1},{2,10},{10,2},{3,11},{11,3},{4,12},{12,4},... | collective-permute-start | bytes 393224 | tf_op jit(solution)/shard_map/keys/ppermute | solution.py:222
  12.3 1.0 reduce_max.18
  13.4 2.0 %convert_reduce_fusion = f32[2,8192]{1,0:T(2,128)S(1)} fusion(bf16[2,64,8192]{2,1,0:T(8,128)(2,1)} %bitcast.51), kind=kLoop, calls=%fused_computation.1 | loop fusion | flops 2080768 | bytes 2162688 | tf_op jit(solution)/shard_map/pool/reduce_sum | solution.py:229
  15.4 1.8 pad_maximum_fusion.1
  17.3 0.7 maximum_bitcast_fusion
  18.0 7.9 %all-to-all-start = ((bf16[16,2,576]{2,1,0:T(2,128)(2,1)}), bf16[16,2,576]{2,1,0:T(2,128)(2,1)S(1)}, u32[]{:S(2)}, u32[]{:S(2)}) async-start(bf16[16,2,576]{2,1,0:T(2,128)(2,1)} %maximum_bitcast_fusion), calls=%async_computation | async-start | bytes 81920 | tf_op jit(solution)/shard_map/pool/all_to_all | solution.py:233
  25.9 7.4 %all-to-all-done = bf16[16,2,576]{2,1,0:T(2,128)(2,1)S(1)} async-done(((bf16[16,2,576]{2,1,0:T(2,128)(2,1)}), bf16[16,2,576]{2,1,0:T(2,128)(2,1)S(1)}, u32[]{:S(2)}, u32[]{:S(2)}) %all-to-all-start) | async-done | bytes 36896 | tf_op jit(solution)/shard_map/pool/all_to_all | solution.py:233
  33.3 0.1 fusion.23
  33.5 0.3 fusion.19
  33.8 0.9 reshape.150
  34.6 3.5 %all-to-all-start.1 = ((f32[16,2,2048]{2,1,0:T(2,128)}), f32[16,2,2048]{2,1,0:T(2,128)S(1)}, u32[]{:S(2)}, u32[]{:S(2)}) async-start(f32[16,2,2048]{2,1,0:T(2,128)} %reshape.150), calls=%async_computation.1 | async-start | bytes 524288 | tf_op jit(solution)/shard_map/gates/all_to_all | solution.py:248
  38.2 1.1 dynamic-slice_bitcast_fusion
  39.2 3.2 %collective-permute-start.2 = (bf16[128,4096]{1,0:T(8,128)(2,1)}, bf16[128,4096]{1,0:T(8,128)(2,1)}, u32[]{:S(2)}, u32[]{:S(2)}) collective-permute-start(bf16[128,4096]{1,0:T(8,128)(2,1)} %dynamic-slice_bitcast_fusion), channel_id=1, source_target_pairs={{0,8},{8,0},{1,9},{9,1},{2,10},{10,2},{3,11},{11,3},{4,12},{12,4},... | collective-permute-start | bytes 3145736 | tf_op jit(solution)/shard_map/keys/ppermute | solution.py:225
  42.5 0.7 fusion.21
  43.1 5.9 %collective-permute-start = (bf16[32,576]{1,0:T(8,128)(2,1)S(1)}, bf16[32,576]{1,0:T(8,128)(2,1)S(1)}, u32[]{:S(2)}, u32[]{:S(2)}) collective-permute-start(bf16[32,576]{1,0:T(8,128)(2,1)S(1)} %reshape.148), channel_id=1, source_target_pairs={{0,16},{16,0},{1,17},{17,1},{2,18},{18,2},{3,19},{19,3},{4,20},{20... | collective-permute-start | bytes 110600 | tf_op jit(solution)/shard_map/pooled_all/ppermute | solution.py:267
  49.0 1.3 pad_add_fusion.sc
  50.3 0.7 reshape.149
  51.0 0.7 stack.45
  51.7 0.1 reduce_sum.46
  51.7 0.7 broadcast_in_dim.47
  52.5 6.5 %all-to-all-start.2 = ((bf16[16,2,2048]{2,1,0:T(2,128)(2,1)}), bf16[16,2,2048]{2,1,0:T(2,128)(2,1)S(1)}, u32[]{:S(2)}, u32[]{:S(2)}) async-start(bf16[16,2,2048]{2,1,0:T(2,128)(2,1)} %broadcast_in_dim.47), calls=%async_computation.2 | async-start | bytes 262144 | tf_op jit(solution)/shard_map/gates/all_to_all | solution.py:203
  59.0 0.9 maximum_select_fusion.2
  59.9 3.9 %collective-permute-start.1 = (bf16[2,32,576]{2,1,0:T(8,128)(2,1)S(1)}, bf16[2,32,576]{2,1,0:T(8,128)(2,1)S(1)}, u32[]{:S(2)}, u32[]{:S(2)}) collective-permute-start(bf16[2,32,576]{2,1,0:T(8,128)(2,1)S(1)} %maximum_select_fusion.2), channel_id=1, source_target_pairs={{0,32},{32,0},{1,33},{33,1},{2,34},{34,2},{3,35},{35,3},{4,36},{36... | collective-permute-start | bytes 221192 | tf_op jit(solution)/shard_map/pooled_all/ppermute | solution.py:268
  63.9 0.9 maximum_select_fusion.1
  64.7 6.3 %collective-permute-done.1 = bf16[2,32,576]{2,1,0:T(8,128)(2,1)S(1)} collective-permute-done((bf16[2,32,576]{2,1,0:T(8,128)(2,1)S(1)}, bf16[2,32,576]{2,1,0:T(8,128)(2,1)S(1)}, u32[]{:S(2)}, u32[]{:S(2)}) %collective-permute-start.1) | collective-permute-done | bytes 73760 | tf_op jit(solution)/shard_map/pooled_all/ppermute | solution.py:268
  71.0 0.7 maximum_select_fusion
  71.9 0.9 copy-done.2
  72.8 1.6 copy-done.3
  74.4 18.7 %attention_targets.1 = f32[16,32]{1,0:T(8,128)S(1)} custom-call(s32[4]{0:T(128)S(1)} %pad_add_fusion.sc, bf16[128,8192]{1,0:T(8,128)(2,1)S(1)} %bitcast.52, bf16[128,4096]{1,0:T(8,128)(2,1)} %collective-permute-done.2.q_recv, bf16[2048,512]{1,0:T(8,128)(2,1)S(1)} %copy-done.3, bf16[128,576]{1,0:T(8,128)(2,1)S(1)} %bitcast.54), custom_call_target="tpu_custom_call" | custom-call | flops 3221225472 | bytes 4194304 | tf_op jit(solution)/shard_map/targets/attention_targets/pallas_call | solution.py:143
  93.1 0.7 reshape.160
  93.8 5.9 %all-to-all-start.3 = ((f32[16,1,512]{2,1,0:T(1,128)}), f32[16,1,512]{2,1,0:T(1,128)S(1)}, u32[]{:S(2)}, u32[]{:S(2)}) async-start(f32[16,1,512]{2,1,0:T(1,128)} %reshape.160), calls=%async_computation.3 | async-start | bytes 65536 | tf_op jit(solution)/shard_map/targets/all_to_all | solution.py:203
  99.7 0.2 fusion.26
  99.9 7.1 %all-to-all-done.3 = f32[16,1,512]{2,1,0:T(1,128)S(1)} async-done(((f32[16,1,512]{2,1,0:T(1,128)}), f32[16,1,512]{2,1,0:T(1,128)S(1)}, u32[]{:S(2)}, u32[]{:S(2)}) %all-to-all-start.3) | async-done | bytes 32800 | tf_op jit(solution)/shard_map/targets/all_to_all | solution.py:203
  107.1 0.5 broadcast.29
  107.6 0.7 reduce.2
  108.5 0.1 copy.21
  108.6 0.2 fusion.6
  108.9 0.3 fusion.5
  109.2 0.9 broadcast_in_dim.51
  110.1 16.3 %all-to-all-start.4 = ((bf16[32,64,128]{2,1,0:T(8,128)(2,1)}), bf16[32,64,128]{2,1,0:T(8,128)(2,1)S(1)}, u32[]{:S(2)}, u32[]{:S(2)}) async-start(bf16[32,64,128]{2,1,0:T(8,128)(2,1)} %bitcast.20), calls=%async_computation.4 | async-start | bytes 1048576 | tf_op jit(solution)/shard_map/gate_grads/all_to_all | solution.py:308
  126.4 17.0 %all-to-all-done.4 = bf16[32,64,128]{2,1,0:T(8,128)(2,1)S(1)} async-done(((bf16[32,64,128]{2,1,0:T(8,128)(2,1)}), bf16[32,64,128]{2,1,0:T(8,128)(2,1)S(1)}, u32[]{:S(2)}, u32[]{:S(2)}) %all-to-all-start.4) | async-done | bytes 524320 | tf_op jit(solution)/shard_map/gate_grads/all_to_all | solution.py:308
  143.5 1.2 fusion.9
  144.7 1.7 fusion.7
  146.5 22.7 %all_to_all.30.own = bf16[8,288,128]{2,1,0:T(8,128)(2,1)S(1)} all-to-all(bf16[8,288,128]{2,1,0:T(8,128)(2,1)S(1)} %broadcast_in_dim.52), channel_id=1, replica_groups=mesh['z'=8,'xh'=2,'co'=2,'xl'=2,'y'=8] {'z'}, dimensions={0} | all-to-all | bytes 1179648 | tf_op jit(solution)/shard_map/weight_grads/all_to_all | solution.py:203
  169.2 3.4 %collective-permute-start.4 = (bf16[8,288,128]{2,1,0:T(8,128)(2,1)S(1)}, bf16[8,288,128]{2,1,0:T(8,128)(2,1)S(1)}, u32[]{:S(2)}, u32[]{:S(2)}) collective-permute-start(bf16[8,288,128]{2,1,0:T(8,128)(2,1)S(1)} %all_to_all.30.own), channel_id=1, source_target_pairs={{0,16},{16,0},{1,17},{17,1},{2,18},{18,2},{3,19},{19,3},{4,20},{20... | collective-permute-start | bytes 1769480 | tf_op jit(solution)/shard_map/weight_grads/ppermute | solution.py:329
  172.6 1.6 collective-permute-done.4.other
  174.2 1.3 assembled.1
  (39 shorter events, 0.8 us)
Async XLA Ops:
  7.2 26.3 %copy-start = (bf16[512,1024]{1,0:T(8,128)(2,1)S(1)}, bf16[512,1024]{1,0:T(8,128)(2,1)}, u32[]{:S(2)}) copy-start(bf16[512,1024]{1,0:T(8,128)(2,1)} %param.8) | copy-start | bytes 3145732
  7.2 26.1 %copy-start.4 = (bf16[64,1024]{1,0:T(8,128)(2,1)S(1)}, bf16[64,1024]{1,0:T(8,128)(2,1)}, u32[]{:S(2)}) copy-start(bf16[64,1024]{1,0:T(8,128)(2,1)} %param.9) | copy-start | bytes 393220
  7.2 64.7 %all-gather.5.cloned.1.call-start = ((), (), s32[]{:S(2)}) async-start(), calls=%async_computation.7 | async-start | bytes 2359296 | tf_op jit(solution)/shard_map/keys/all_gather | solution.py:223
  8.3 7.1 %collective-permute-start.3 = (bf16[128,512]{1,0:T(8,128)(2,1)S(1)}, bf16[128,512]{1,0:T(8,128)(2,1)}, u32[]{:S(2)}, u32[]{:S(2)}) collective-permute-start(bf16[128,512]{1,0:T(8,128)(2,1)S(1)} %get-tuple-element.7), channel_id=1, source_target_pairs={{0,8},{8,0},{1,9},{9,1},{2,10},{10,2},{3,11},{11,3},{4,12},{12,4},... | collective-permute-start | bytes 393224 | tf_op jit(solution)/shard_map/keys/ppermute | solution.py:222
  15.4 22.8 %copy-start.1 = (bf16[1,128,8192]{2,1,0:T(8,128)(2,1)S(1)}, bf16[1,128,8192]{2,1,0:T(8,128)(2,1)}, u32[]{:S(2)}) copy-start(bf16[1,128,8192]{2,1,0:T(8,128)(2,1)} %param.5) | copy-start | bytes 6291460
  18.0 15.3 %all-to-all-start = ((bf16[16,2,576]{2,1,0:T(2,128)(2,1)}), bf16[16,2,576]{2,1,0:T(2,128)(2,1)S(1)}, u32[]{:S(2)}, u32[]{:S(2)}) async-start(bf16[16,2,576]{2,1,0:T(2,128)(2,1)} %maximum_bitcast_fusion), calls=%async_computation | async-start | bytes 81920 | tf_op jit(solution)/shard_map/pool/all_to_all | solution.py:233
  33.7 8.7 %copy-start.5 = (s32[1,2048]{1,0:T(1,128)S(1)}, s32[1,2048]{1,0:T(1,128)}, u32[]{:S(2)}) copy-start(s32[1,2048]{1,0:T(1,128)} %param.7) | copy-start | bytes 24580
  34.6 17.0 %all-to-all-start.1 = ((f32[16,2,2048]{2,1,0:T(2,128)}), f32[16,2,2048]{2,1,0:T(2,128)S(1)}, u32[]{:S(2)}, u32[]{:S(2)}) async-start(f32[16,2,2048]{2,1,0:T(2,128)} %reshape.150), calls=%async_computation.1 | async-start | bytes 524288 | tf_op jit(solution)/shard_map/gates/all_to_all | solution.py:248
  39.2 32.6 %collective-permute-start.2 = (bf16[128,4096]{1,0:T(8,128)(2,1)}, bf16[128,4096]{1,0:T(8,128)(2,1)}, u32[]{:S(2)}, u32[]{:S(2)}) collective-permute-start(bf16[128,4096]{1,0:T(8,128)(2,1)} %dynamic-slice_bitcast_fusion), channel_id=1, source_target_pairs={{0,8},{8,0},{1,9},{9,1},{2,10},{10,2},{3,11},{11,3},{4,12},{12,4},... | collective-permute-start | bytes 3145736 | tf_op jit(solution)/shard_map/keys/ppermute | solution.py:225
  43.1 15.9 %collective-permute-start = (bf16[32,576]{1,0:T(8,128)(2,1)S(1)}, bf16[32,576]{1,0:T(8,128)(2,1)S(1)}, u32[]{:S(2)}, u32[]{:S(2)}) collective-permute-start(bf16[32,576]{1,0:T(8,128)(2,1)S(1)} %reshape.148), channel_id=1, source_target_pairs={{0,16},{16,0},{1,17},{17,1},{2,18},{18,2},{3,19},{19,3},{4,20},{20... | collective-permute-start | bytes 110600 | tf_op jit(solution)/shard_map/pooled_all/ppermute | solution.py:267
  52.5 19.3 %all-to-all-start.2 = ((bf16[16,2,2048]{2,1,0:T(2,128)(2,1)}), bf16[16,2,2048]{2,1,0:T(2,128)(2,1)S(1)}, u32[]{:S(2)}, u32[]{:S(2)}) async-start(bf16[16,2,2048]{2,1,0:T(2,128)(2,1)} %broadcast_in_dim.47), calls=%async_computation.2 | async-start | bytes 262144 | tf_op jit(solution)/shard_map/gates/all_to_all | solution.py:203
  59.0 84.5 %all-gather.3.cloned.1.call-start = ((), (), s32[]{:S(2)}) async-start(), calls=%async_computation.6 | async-start | bytes 1474560 | tf_op jit(solution)/shard_map/pooled_all/all_gather | solution.py:270
  59.9 11.1 %collective-permute-start.1 = (bf16[2,32,576]{2,1,0:T(8,128)(2,1)S(1)}, bf16[2,32,576]{2,1,0:T(8,128)(2,1)S(1)}, u32[]{:S(2)}, u32[]{:S(2)}) collective-permute-start(bf16[2,32,576]{2,1,0:T(8,128)(2,1)S(1)} %maximum_select_fusion.2), channel_id=1, source_target_pairs={{0,32},{32,0},{1,33},{33,1},{2,34},{34,2},{3,35},{35,3},{4,36},{36... | collective-permute-start | bytes 221192 | tf_op jit(solution)/shard_map/pooled_all/ppermute | solution.py:268
  71.9 0.9 copy-start.2
  72.8 1.6 copy-start.3
  93.8 13.3 %all-to-all-start.3 = ((f32[16,1,512]{2,1,0:T(1,128)}), f32[16,1,512]{2,1,0:T(1,128)S(1)}, u32[]{:S(2)}, u32[]{:S(2)}) async-start(f32[16,1,512]{2,1,0:T(1,128)} %reshape.160), calls=%async_computation.3 | async-start | bytes 65536 | tf_op jit(solution)/shard_map/targets/all_to_all | solution.py:203
  110.1 33.3 %all-to-all-start.4 = ((bf16[32,64,128]{2,1,0:T(8,128)(2,1)}), bf16[32,64,128]{2,1,0:T(8,128)(2,1)S(1)}, u32[]{:S(2)}, u32[]{:S(2)}) async-start(bf16[32,64,128]{2,1,0:T(8,128)(2,1)} %bitcast.20), calls=%async_computation.4 | async-start | bytes 1048576 | tf_op jit(solution)/shard_map/gate_grads/all_to_all | solution.py:308
  169.2 5.0 %collective-permute-start.4 = (bf16[8,288,128]{2,1,0:T(8,128)(2,1)S(1)}, bf16[8,288,128]{2,1,0:T(8,128)(2,1)S(1)}, u32[]{:S(2)}, u32[]{:S(2)}) collective-permute-start(bf16[8,288,128]{2,1,0:T(8,128)(2,1)S(1)} %all_to_all.30.own), channel_id=1, source_target_pairs={{0,16},{16,0},{1,17},{17,1},{2,18},{18,2},{3,19},{19,3},{4,20},{20... | collective-permute-start | bytes 1769480 | tf_op jit(solution)/shard_map/weight_grads/ppermute | solution.py:329
Sparse Core Ops, SparseCore 0:
  17.4 53.0 all-gather.4
  72.6 41.3 all-gather.2

commit v3 on v2

--- a/solution.py
+++ b/solution.py
@@ -1,4 +1,3 @@
-import functools
 import math
 
 import jax
@@ -26,6 +25,12 @@
 EXP2_SCALE = math.log2(math.e) / math.sqrt(HEAD_DIM)
 
 
+def tree(op, parts):
+    while len(parts) > 1:
+        parts = [op(a, b) for a, b in zip(parts[::2], parts[1::2], strict=True)]
+    return parts[0]
+
+
 def attention_kernel(
     sc, q_own, q_recv, k_ref, after, out_ref, bias_s, k_s, q_s, s0, s1, s2, m_s, l_s, bm_s, acc_s
 ):
@@ -94,7 +99,7 @@
                 s = slots[at][rows, cols] + bias_s[at, rows, :]
                 slots[at][rows, cols] = s
                 blks.append(jnp.max(s.reshape(BLOCK // 8, 8, SHARD), axis=0))
-            top = functools.reduce(jnp.maximum, blks)
+            top = tree(jnp.maximum, blks)
             for w in range(PANEL // BLOCK // 8):
                 v = [blks[w * 8 + i] for i in FOLDED]
                 for span in (4, 2, 1):
@@ -104,7 +109,7 @@
                 m_old = m_s[half, g]
                 top = jnp.maximum(m_old, top)
             e = jnp.exp2(slots[at][:, cols].reshape(PANEL // 8, 8, SHARD) - top[None])
-            total = jnp.sum(e, axis=0)
+            total = tree(jnp.add, [e[b] for b in range(PANEL // 8)])
             if panel == 1:
                 total = total + l_s[half, g] * jnp.exp2(m_old - top)
             l_s[half, g] = total
@@ -135,14 +140,16 @@
     def _():
         raw = acc_s[...].reshape(NUM_BLOCKS, 128)
         norm = raw / jnp.sum(raw, axis=0, keepdims=True)
-        out_ref[...] = norm.T[:16, :]
+        mine = norm.T[:16, :]
+        for to in range(16):
+            out_ref[to * 16 : (to + 1) * 16, :] = mine
 
 
 def attention_targets(scalars, q, q_recv, k_all, after):
     kw = GROUP * HEAD_DIM
     return pl.pallas_call(
         attention_kernel,
-        out_shape=jax.ShapeDtypeStruct((16, NUM_BLOCKS), jnp.float32),
+        out_shape=jax.ShapeDtypeStruct((256, NUM_BLOCKS), jnp.float32),
         grid_spec=pltpu.PrefetchScalarGridSpec(
             num_scalar_prefetch=1,
             grid=(LOCAL_KV,),
@@ -152,7 +159,7 @@
                 pl.BlockSpec((16 * SHARD, HEAD_DIM), lambda h, sc: (0, h)),
                 pl.BlockSpec(memory_space=pl.ANY),
             ],
-            out_specs=pl.BlockSpec((16, NUM_BLOCKS), lambda h, sc: (0, 0)),
+            out_specs=pl.BlockSpec((256, NUM_BLOCKS), lambda h, sc: (0, 0)),
             scratch_shapes=[
                 pltpu.VMEM((3, PANEL, SHARD), jnp.float32),
                 pltpu.VMEM((2 * PANEL, 2 * HEAD_DIM), jnp.bfloat16),
@@ -174,13 +181,85 @@
     )(scalars, q, q_recv, k_all, after)
 
 
+def gate_grads_kernel(target, prob, gq, gk, out_ref):
+    left = lax.broadcasted_iota(jnp.int32, (NUM_BLOCKS, GATE_DIM), 1) < GATE_DIM // 2
+    row = lax.broadcasted_iota(jnp.int32, (NUM_BLOCKS, NUM_BLOCKS), 0)
+    causal = lax.broadcasted_iota(jnp.int32, (NUM_BLOCKS, NUM_BLOCKS), 1) <= row
+    scale = 1.0 / GATE_DIM**0.5
+
+    def product(grad, other):
+        high = grad.astype(jnp.bfloat16)
+        low = (grad - high.astype(jnp.float32)).astype(jnp.bfloat16)
+        total = jnp.dot(high, other, preferred_element_type=jnp.float32)
+        total = total + jnp.dot(low, other, preferred_element_type=jnp.float32)
+        return (total * scale).astype(jnp.bfloat16).astype(jnp.float32)
+
+    for head in range(KV_HEADS):
+        cols = slice(head * GATE_DIM, (head + 1) * GATE_DIM)
+        x, h = divmod(head, LOCAL_KV)
+        rows = [(x * 8 + y) * 16 + half * 8 + h * 2 for half in range(2) for y in range(8)]
+        mine = jnp.concatenate([target[r : r + 2, :] for r in rows], axis=0)
+        grad = jnp.where(causal, prob[head] - mine, 0.0)
+        of_q = product(grad, gk[:, cols])
+        of_k = product(grad.T, gq[:, cols])
+        half = GATE_DIM // 2
+        first = jnp.where(left, of_q, pltpu.roll(of_k, half, 1)).astype(jnp.bfloat16)
+        second = jnp.where(left, pltpu.roll(of_q, half, 1), of_k).astype(jnp.bfloat16)
+        for to in range(4):
+            at = (head * 4 + to) * NUM_BLOCKS
+            out_ref[at : at + NUM_BLOCKS, :] = first if to % 2 == 0 else second
+
+
+def weight_grads_kernel(pooled, grads, out_ref):
+    depth = 4 * NUM_BLOCKS
+    rows = pooled.shape[0] // 8
+    total = jnp.zeros((rows, GATE_DIM), jnp.float32)
+    for z in range(8):
+        total = total + jnp.dot(
+            pooled[z * rows : (z + 1) * rows, :],
+            grads[z * depth : (z + 1) * depth, :],
+            preferred_element_type=jnp.float32,
+        )
+    rows_k = rows // 9
+    hq, hk = rows_k * 4, rows_k // 2
+    of_q, of_k = total[: 2 * hq], total[2 * hq :]
+    left = lax.broadcasted_iota(jnp.int32, (hq, GATE_DIM), 1) < GATE_DIM // 2
+    half = GATE_DIM // 2
+    top = jnp.where(left, of_q[:hq], pltpu.roll(of_q[hq:], half, 1)).astype(jnp.bfloat16)
+    low = jnp.where(left[:hk], pltpu.roll(of_k[:hk], half, 1), of_k[hk:]).astype(jnp.bfloat16)
+    for z in range(8):
+        out_ref[z, :hq, :] = top
+        out_ref[z, hq:, :] = low
+
+
 def assemble_kernel(sc, own, other, out_q, out_k):
     hq, hk = out_q.shape[0] // 2, out_k.shape[0] // 2
-    for ref, core in ((own, sc[0]), (other, 1 - sc[0])):
-        for z in range(KV_HEADS):
-            cols = slice(z * GATE_DIM, (z + 1) * GATE_DIM)
-            out_q[pl.ds(pl.multiple_of(core * hq, hq), hq), cols] = ref[z, :hq, :]
-            out_k[pl.ds(pl.multiple_of(core * hk, hk), hk), cols] = ref[z, hq:, :]
+    half = GATE_DIM // 2
+    left = lax.broadcasted_iota(jnp.int32, (hq + hk, GATE_DIM), 1) < half
+    first = sc[0] == 0
+    for z in range(KV_HEADS):
+        cols = slice(z * GATE_DIM, (z + 1) * GATE_DIM)
+        mine, theirs = own[z].astype(jnp.float32), other[z].astype(jnp.float32)
+        core0 = jnp.where(first, mine, theirs)
+        core1 = jnp.where(first, theirs, mine)
+        upper = jnp.where(left, core0, pltpu.roll(core1, half, 1)).astype(jnp.bfloat16)
+        lower = jnp.where(left, pltpu.roll(core0, half, 1), core1).astype(jnp.bfloat16)
+        out_q[:hq, cols] = upper[:hq]
+        out_q[hq:, cols] = lower[:hq]
+        out_k[:hk, cols] = upper[hq:]
+        out_k[hk:, cols] = lower[hq:]
+
+
+def in_vmem(kernel, out_shape, name, mib, *args):
+    spec = pl.BlockSpec(memory_space=pltpu.VMEM)
+    return pl.pallas_call(
+        kernel,
+        out_shape=out_shape,
+        in_specs=[spec] * len(args),
+        out_specs=spec,
+        compiler_params=pltpu.CompilerParams(vmem_limit_bytes=mib * 1024 * 1024),
+        name=name,
+    )(*args)
 
 
 def assembled(co, own, other, rows_q, rows_k):
@@ -266,7 +345,7 @@
     with jax.named_scope("pooled_all"):
         pair = ordered(pooled, lax.ppermute(pooled, "co", SWAP), co)
         quad = ordered(pair, lax.ppermute(pair, "xh", SWAP), xh)
-        quad = quad.reshape(4 * NUM_BLOCKS, -1)
+        quad = quad.reshape(4 * NUM_BLOCKS, -1).T
         pooled_all = lax.all_gather(quad, "z", axis=0, tiled=True)
 
     with jax.named_scope("targets"):
@@ -279,53 +358,31 @@
             ]
         )
         mine = attention_targets(scalars, q, q_recv, k_all, quad)
-        target = spread(mine, CTX_AXES, 16)
-        target = target.reshape(2, 8, 2, LOCAL_KV, 2, NUM_BLOCKS).transpose(0, 3, 2, 1, 4, 5)
-        target = target.reshape(KV_HEADS, NUM_BLOCKS, NUM_BLOCKS)
+        target = lax.all_to_all(mine, CTX_AXES, split_axis=0, concat_axis=0, tiled=True)
 
     with jax.named_scope("gate_grads"):
-        score_grad = jnp.where(causal, gate_prob - target, 0.0)
-        grad_gate_q = (
-            jnp.einsum(
-                "hab,bhe->hae",
-                score_grad,
-                gk.astype(jnp.float32),
-                precision=lax.Precision.HIGHEST,
-            )
-            * gate_scale
-        ).astype(jnp.bfloat16)
-        grad_gate_k = (
-            jnp.einsum(
-                "hab,ahe->hbe",
-                score_grad,
-                gq.astype(jnp.float32),
-                precision=lax.Precision.HIGHEST,
-            )
-            * gate_scale
-        ).astype(jnp.bfloat16)
-        both = jnp.concatenate([grad_gate_q, grad_gate_k], axis=1)
-        both = jnp.broadcast_to(both[:, None], (8, 4, 2 * NUM_BLOCKS, GATE_DIM))
-        both = lax.all_to_all(
-            both.reshape(32, 2 * NUM_BLOCKS, GATE_DIM),
-            SEQ_AXES,
-            split_axis=0,
-            concat_axis=0,
-            tiled=True,
-        )
+        grads = in_vmem(
+            gate_grads_kernel,
+            jax.ShapeDtypeStruct((32 * NUM_BLOCKS, GATE_DIM), jnp.bfloat16),
+            "gate_grads",
+            16,
+            target,
+            gate_prob,
+            gates[:, :gw],
+            gates[:, gw:],
+        )
+        grads = lax.all_to_all(grads, SEQ_AXES, split_axis=0, concat_axis=0, tiled=True)
 
     with jax.named_scope("weight_grads"):
-        all_q = both[:, :NUM_BLOCKS].reshape(-1, GATE_DIM)
-        all_k = both[:, NUM_BLOCKS:].reshape(-1, GATE_DIM)
-        hq, hk = rows_q // 2, rows_k // 2
-        grad_q = jnp.dot(pooled_all[:, :rows_q].T, all_q, preferred_element_type=jnp.float32)
-        grad_k = jnp.dot(pooled_all[:, rows_q:].T, all_k, preferred_element_type=jnp.float32)
-        piece = jnp.concatenate(
-            [
-                lax.dynamic_slice_in_dim(grad_q, co * hq, hq, 0),
-                lax.dynamic_slice_in_dim(grad_k, co * hk, hk, 0),
-            ]
-        ).astype(jnp.bfloat16)
-        pieces = spread(piece, "z", 8)
+        pieces = in_vmem(
+            weight_grads_kernel,
+            jax.ShapeDtypeStruct((8, (rows_q + rows_k) // 2, GATE_DIM), jnp.bfloat16),
+            "weight_grads",
+            16,
+            pooled_all,
+            grads,
+        )
+        pieces = lax.all_to_all(pieces, "z", split_axis=0, concat_axis=0, tiled=True)
         out_q, out_k = assembled(co, pieces, lax.ppermute(pieces, "co", SWAP), rows_q, rows_k)
     return out_q, out_k
 

time: 183 us -> 179 us (0.978)
  other arithmetic: 10.9 us -> 8.24 us
  local copies, waits for them, and re-layouts: 10.3 us -> 12.8 us
  matrix products: 4.04 us -> 1.67 us
    all_to_all x2 -> x1, starting transfers between devices: 12.4 us -> 6.31 us  [spread(): lax.all_to_all(jnp.broadcast_to(x[None], (n, *x.shape)), axes, split_axis...]
    all_to_all x1 -> x2, starting transfers between devices: 16.3 us -> 20.7 us  [the longest x1 17.2 us: shards(): lax.all_to_all(grads, SEQ_AXES, split_axis=0, concat_axis=0, tiled=True)]
    all_to_all x1, waiting for transfers between devices: 7.35 us -> 3 us  [shards(): lax.all_to_all(mine.transpose(1, 0, 2), CTX_AXES, split_axis=0, concat_ax...]
    dot_general x4 -> x0, matrix products: 3.41 us -> none  [the longest x1 1.71 us: shards(): jnp.dot(pooled_all[:, :rows_q].T, all_q, preferred_element_type=jnp.float32)]
    all_to_all x1 -> x2, waiting for transfers between devices: 17 us -> 19.9 us  [the longest x1 12.9 us: shards(): lax.all_to_all(grads, SEQ_AXES, split_axis=0, concat_axis=0, tiled=True)]
    ppermute x1, waiting for transfers between devices: 0.01 us -> 2.34 us  [shards(): k_recv = lax.ppermute(k_other, 'xl', SWAP)]
    all_to_all x2 -> x1, waiting for transfers between devices: 7.15 us -> 5.31 us  [spread(): lax.all_to_all(jnp.broadcast_to(x[None], (n, *x.shape)), axes, split_axis...]
    unnamed x15 -> x17, local copies, waits for them, and re-layouts: 3.36 us -> 4.62 us
  transfers between devices with their start and end apart: 12 -> 12, of which waited for: 5 -> 7; matrix products, arithmetic and copies ran while one was open for 9% -> 10% of each run, Pallas kernels for 10% -> 11%
where the time goes in v3:
time: 179 us; the launch traced here: 178 us
  starting transfers between devices  59.2 us (33%)
  waiting for transfers between devices  39.1 us (22%)
  blocking collectives  21.2 us (12%)
  Pallas kernels  21.1 us (12%)
  between operations  14.3 us (8%)
  local copies, waits for them, and re-layouts  12.8 us (7%)
  other arithmetic  8.24 us (5%)
    all_to_all x1, blocking collectives, shards(): lax.all_to_all(pieces, 'z', split_axis=0, concat_axis=0, tiled=True)  21.2 us
    pallas_call x1, Pallas kernels, attention_targets(): pl.pallas_call(attention_kernel, out_shape=jax.ShapeDtypeStruct((256, NUM...  17.9 us
    all_to_all x1, starting transfers between devices, shards(): lax.all_to_all(grads, SEQ_AXES, split_axis=0, concat_axis=0, tiled=True)  17.2 us
    all_to_all x1, waiting for transfers between devices, shards(): lax.all_to_all(grads, SEQ_AXES, split_axis=0, concat_axis=0, tiled=True)  12.9 us
    all_to_all x1, starting transfers between devices, shards(): lax.all_to_all(mine.transpose(1, 0, 2), CTX_AXES, split_axis=0, concat_ax...  8.64 us
    all_to_all x1, waiting for transfers between devices, shards(): lax.all_to_all(mine, CTX_AXES, split_axis=0, concat_axis=0, tiled=True)  6.98 us
    ppermute x1, waiting for transfers between devices, shards(): quad = ordered(pair, lax.ppermute(pair, 'xh', SWAP), xh)  6.9 us
    all_to_all x1, starting transfers between devices, spread(): lax.all_to_all(jnp.broadcast_to(x[None], (n, *x.shape)), axes, split_axis...  6.31 us
  transfers between devices with their start and end apart: 12, of which 7 were waited for; matrix products, arithmetic and copies ran while one was open for 10% of the time, Pallas kernels for 11%

profile of v3, /device:TPU:1, one launch (start us, length us, event | category | flops | bytes accessed | tf_op | source)
XLA Modules:
  0.0 177.6 jit_solution(10406125163937222339)
XLA Ops:
  7.3 1.1 dynamic-slice_bitcast_fusion.2
  8.4 3.9 %collective-permute-start.3 = (bf16[128,512]{1,0:T(8,128)(2,1)S(1)}, bf16[128,512]{1,0:T(8,128)(2,1)S(1)}, u32[]{:S(2)}, u32[]{:S(2)}) collective-permute-start(bf16[128,512]{1,0:T(8,128)(2,1)S(1)} %get-tuple-element.5), channel_id=1, source_target_pairs={{0,8},{8,0},{1,9},{9,1},{2,10},{10,2},{3,11},{11,3},{4,12},{12,4},... | collective-permute-start | bytes 393224 | tf_op jit(solution)/shard_map/keys/ppermute | solution.py:301
  12.4 2.3 %collective-permute-done.3 = bf16[128,512]{1,0:T(8,128)(2,1)S(1)} collective-permute-done((bf16[128,512]{1,0:T(8,128)(2,1)S(1)}, bf16[128,512]{1,0:T(8,128)(2,1)S(1)}, u32[]{:S(2)}, u32[]{:S(2)}) %collective-permute-start.3) | collective-permute-done | bytes 131104 | tf_op jit(solution)/shard_map/keys/ppermute | solution.py:301
  14.7 0.7 pad_maximum_fusion
  15.4 2.0 %convert_reduce_fusion = f32[2,8192]{1,0:T(2,128)S(1)} fusion(bf16[2,64,8192]{2,1,0:T(8,128)(2,1)} %bitcast.50), kind=kLoop, calls=%fused_computation.2 | loop fusion | flops 2080768 | bytes 2162688 | tf_op jit(solution)/shard_map/pool/reduce_sum | solution.py:308
  17.7 0.6 copy.19
  18.3 8.6 %all-to-all-start = ((bf16[16,2,576]{2,1,0:T(2,128)(2,1)}), bf16[16,2,576]{2,1,0:T(2,128)(2,1)S(1)}, u32[]{:S(2)}, u32[]{:S(2)}) async-start(bf16[16,2,576]{2,1,0:T(2,128)(2,1)} %copy.19), calls=%async_computation | async-start | bytes 81920 | tf_op jit(solution)/shard_map/pool/all_to_all | solution.py:312
  27.0 1.1 dynamic-slice_bitcast_fusion
  28.1 3.3 %collective-permute-start.2 = (bf16[128,4096]{1,0:T(8,128)(2,1)}, bf16[128,4096]{1,0:T(8,128)(2,1)}, u32[]{:S(2)}, u32[]{:S(2)}) collective-permute-start(bf16[128,4096]{1,0:T(8,128)(2,1)} %dynamic-slice_bitcast_fusion), channel_id=1, source_target_pairs={{0,8},{8,0},{1,9},{9,1},{2,10},{10,2},{3,11},{11,3},{4,12},{12,4},... | collective-permute-start | bytes 3145736 | tf_op jit(solution)/shard_map/keys/ppermute | solution.py:304
  31.4 3.0 %all-to-all-done = bf16[16,2,576]{2,1,0:T(2,128)(2,1)S(1)} async-done(((bf16[16,2,576]{2,1,0:T(2,128)(2,1)}), bf16[16,2,576]{2,1,0:T(2,128)(2,1)S(1)}, u32[]{:S(2)}, u32[]{:S(2)}) %all-to-all-start) | async-done | bytes 36896 | tf_op jit(solution)/shard_map/pool/all_to_all | solution.py:312
  34.4 5.4 %collective-permute-start = (bf16[32,576]{1,0:T(8,128)(2,1)S(1)}, bf16[32,576]{1,0:T(8,128)(2,1)S(1)}, u32[]{:S(2)}, u32[]{:S(2)}) collective-permute-start(bf16[32,576]{1,0:T(8,128)(2,1)S(1)} %reshape.120), channel_id=1, source_target_pairs={{0,16},{16,0},{1,17},{17,1},{2,18},{18,2},{3,19},{19,3},{4,20},{20... | collective-permute-start | bytes 110600 | tf_op jit(solution)/shard_map/pooled_all/ppermute | solution.py:346
  39.8 1.1 fusion.15
  40.9 0.3 fusion.11
  41.2 0.9 reshape.122
  42.1 3.5 %all-to-all-start.2 = ((f32[16,2,2048]{2,1,0:T(2,128)}), f32[16,2,2048]{2,1,0:T(2,128)S(1)}, u32[]{:S(2)}, u32[]{:S(2)}) async-start(f32[16,2,2048]{2,1,0:T(2,128)} %reshape.122), calls=%async_computation.2 | async-start | bytes 524288 | tf_op jit(solution)/shard_map/gates/all_to_all | solution.py:327
  45.6 0.6 stack.45
  46.3 0.7 reshape.121
  47.0 0.9 maximum_select_fusion.2
  47.8 3.9 %collective-permute-start.1 = (bf16[2,32,576]{2,1,0:T(8,128)(2,1)S(1)}, bf16[2,32,576]{2,1,0:T(8,128)(2,1)S(1)}, u32[]{:S(2)}, u32[]{:S(2)}) collective-permute-start(bf16[2,32,576]{2,1,0:T(8,128)(2,1)S(1)} %maximum_select_fusion.2), channel_id=1, source_target_pairs={{0,32},{32,0},{1,33},{33,1},{2,34},{34,2},{3,35},{35,3},{4,36},{36... | collective-permute-start | bytes 221192 | tf_op jit(solution)/shard_map/pooled_all/ppermute | solution.py:347
  51.8 0.9 maximum_select_fusion.1
  52.6 6.9 %collective-permute-done.1 = bf16[2,32,576]{2,1,0:T(8,128)(2,1)S(1)} collective-permute-done((bf16[2,32,576]{2,1,0:T(8,128)(2,1)S(1)}, bf16[2,32,576]{2,1,0:T(8,128)(2,1)S(1)}, u32[]{:S(2)}, u32[]{:S(2)}) %collective-permute-start.1) | collective-permute-done | bytes 73760 | tf_op jit(solution)/shard_map/pooled_all/ppermute | solution.py:347
  59.5 0.7 maximum_select_fusion
  60.2 1.7 copy.20
  62.0 0.1 reduce_sum.48
  62.1 0.7 broadcast_in_dim.25
  62.8 6.3 %all-to-all-start.3 = ((bf16[16,2,2048]{2,1,0:T(2,128)(2,1)}), bf16[16,2,2048]{2,1,0:T(2,128)(2,1)S(1)}, u32[]{:S(2)}, u32[]{:S(2)}) async-start(bf16[16,2,2048]{2,1,0:T(2,128)(2,1)} %broadcast_in_dim.25), calls=%async_computation.3 | async-start | bytes 262144 | tf_op jit(solution)/shard_map/gates/all_to_all | solution.py:282
  69.1 0.7 fusion.13
  69.8 1.4 pad_add_fusion.sc
  71.2 5.3 %all-to-all-done.3 = bf16[16,2,2048]{2,1,0:T(2,128)(2,1)S(1)} async-done(((bf16[16,2,2048]{2,1,0:T(2,128)(2,1)}), bf16[16,2,2048]{2,1,0:T(2,128)(2,1)S(1)}, u32[]{:S(2)}, u32[]{:S(2)}) %all-to-all-start.3) | async-done | bytes 131104 | tf_op jit(solution)/shard_map/gates/all_to_all | solution.py:282
  76.7 0.9 copy-done.3
  77.6 1.6 copy-done.4
  79.2 17.9 %attention_targets.1 = f32[256,32]{1,0:T(8,128)S(1)} custom-call(s32[4]{0:T(128)S(1)} %pad_add_fusion.sc, bf16[128,8192]{1,0:T(8,128)(2,1)S(1)} %bitcast.51, bf16[128,4096]{1,0:T(8,128)(2,1)} %collective-permute-done.2.q_recv, bf16[2048,512]{1,0:T(8,128)(2,1)S(1)} %copy-done.4, bf16[576,128]{1,0:T(8,128)(2,1)S(1)} %bitcast.54), custom_call_target="tpu_custom_call" | custom-call | flops 3221225472 | bytes 4194304 | tf_op jit(solution)/shard_map/targets/attention_targets/pallas_call | solution.py:150
  97.1 0.7 reshape.127
  97.8 3.5 %all-to-all-start.1 = ((f32[16,1,512]{2,1,0:T(1,128)}), f32[16,1,512]{2,1,0:T(1,128)S(1)}, u32[]{:S(2)}, u32[]{:S(2)}) async-start(f32[16,1,512]{2,1,0:T(1,128)} %reshape.127), calls=%async_computation.1 | async-start | bytes 65536 | tf_op jit(solution)/shard_map/targets/all_to_all | solution.py:361
  101.3 0.3 fusion.3.prob
  101.6 7.0 %all-to-all-done.1 = f32[16,1,512]{2,1,0:T(1,128)S(1)} async-done(((f32[16,1,512]{2,1,0:T(1,128)}), f32[16,1,512]{2,1,0:T(1,128)S(1)}, u32[]{:S(2)}, u32[]{:S(2)}) %all-to-all-start.1) | async-done | bytes 32800 | tf_op jit(solution)/shard_map/targets/all_to_all | solution.py:361
  108.6 0.5 broadcast.21
  109.1 0.7 reduce.2
  109.9 0.1 reshape.128
  110.0 1.1 gate_grads.1
  111.0 17.2 %all-to-all-start.4 = ((bf16[32,32,128]{2,1,0:T(8,128)(2,1)}), bf16[32,32,128]{2,1,0:T(8,128)(2,1)S(1)}, u32[]{:S(2)}, u32[]{:S(2)}) async-start(bf16[32,32,128]{2,1,0:T(8,128)(2,1)} %bitcast.19), calls=%async_computation.4 | async-start | bytes 524288 | tf_op jit(solution)/shard_map/gate_grads/all_to_all | solution.py:374
  128.2 12.9 %all-to-all-done.4 = bf16[32,32,128]{2,1,0:T(8,128)(2,1)S(1)} async-done(((bf16[32,32,128]{2,1,0:T(8,128)(2,1)}), bf16[32,32,128]{2,1,0:T(8,128)(2,1)S(1)}, u32[]{:S(2)}, u32[]{:S(2)}) %all-to-all-start.4) | async-done | bytes 262176 | tf_op jit(solution)/shard_map/gate_grads/all_to_all | solution.py:374
  141.2 1.3 copy-done.2
  142.4 0.5 weight_grads.1
  143.0 21.2 %all_to_all.42.own = bf16[8,288,128]{2,1,0:T(8,128)(2,1)S(1)} all-to-all(bf16[8,288,128]{2,1,0:T(8,128)(2,1)S(1)} %weight_grads.1), channel_id=1, replica_groups=mesh['z'=8,'xh'=2,'co'=2,'xl'=2,'y'=8] {'z'}, dimensions={0} | all-to-all | bytes 1179648 | tf_op jit(solution)/shard_map/weight_grads/all_to_all | solution.py:385
  164.2 3.4 %collective-permute-start.4 = (bf16[8,288,128]{2,1,0:T(8,128)(2,1)S(1)}, bf16[8,288,128]{2,1,0:T(8,128)(2,1)S(1)}, u32[]{:S(2)}, u32[]{:S(2)}) collective-permute-start(bf16[8,288,128]{2,1,0:T(8,128)(2,1)S(1)} %all_to_all.42.own), channel_id=1, source_target_pairs={{0,16},{16,0},{1,17},{17,1},{2,18},{18,2},{3,19},{19,3},{4,20},{20... | collective-permute-start | bytes 1769480 | tf_op jit(solution)/shard_map/weight_grads/ppermute | solution.py:386
  167.6 1.6 collective-permute-done.4.other
  169.2 1.6 assembled.1
  (30 shorter events, 0.5 us)
Async XLA Ops:
  7.2 33.7 %copy-start = (bf16[512,1024]{1,0:T(8,128)(2,1)S(1)}, bf16[512,1024]{1,0:T(8,128)(2,1)}, u32[]{:S(2)}) copy-start(bf16[512,1024]{1,0:T(8,128)(2,1)} %param.8) | copy-start | bytes 3145732
  7.2 10.3 %copy-start.5 = (bf16[1,128,1024]{2,1,0:T(8,128)(2,1)S(1)}, bf16[1,128,1024]{2,1,0:T(8,128)(2,1)}, u32[]{:S(2)}) copy-start(bf16[1,128,1024]{2,1,0:T(8,128)(2,1)} %param.6) | copy-start | bytes 786436
  7.2 69.5 %all-gather.5.cloned.1.call-start = ((), (), s32[]{:S(2)}) async-start(), calls=%async_computation.7 | async-start | bytes 2359296 | tf_op jit(solution)/shard_map/keys/all_gather | solution.py:302
  7.2 19.8 %copy-start.1 = (bf16[1,128,8192]{2,1,0:T(8,128)(2,1)S(1)}, bf16[1,128,8192]{2,1,0:T(8,128)(2,1)}, u32[]{:S(2)}) copy-start(bf16[1,128,8192]{2,1,0:T(8,128)(2,1)} %param.5) | copy-start | bytes 6291460
  8.4 6.3 %collective-permute-start.3 = (bf16[128,512]{1,0:T(8,128)(2,1)S(1)}, bf16[128,512]{1,0:T(8,128)(2,1)S(1)}, u32[]{:S(2)}, u32[]{:S(2)}) collective-permute-start(bf16[128,512]{1,0:T(8,128)(2,1)S(1)} %get-tuple-element.5), channel_id=1, source_target_pairs={{0,8},{8,0},{1,9},{9,1},{2,10},{10,2},{3,11},{11,3},{4,12},{12,4},... | collective-permute-start | bytes 393224 | tf_op jit(solution)/shard_map/keys/ppermute | solution.py:301
  18.3 16.0 %all-to-all-start = ((bf16[16,2,576]{2,1,0:T(2,128)(2,1)}), bf16[16,2,576]{2,1,0:T(2,128)(2,1)S(1)}, u32[]{:S(2)}, u32[]{:S(2)}) async-start(bf16[16,2,576]{2,1,0:T(2,128)(2,1)} %copy.19), calls=%async_computation | async-start | bytes 81920 | tf_op jit(solution)/shard_map/pool/all_to_all | solution.py:312
  28.1 48.6 %collective-permute-start.2 = (bf16[128,4096]{1,0:T(8,128)(2,1)}, bf16[128,4096]{1,0:T(8,128)(2,1)}, u32[]{:S(2)}, u32[]{:S(2)}) collective-permute-start(bf16[128,4096]{1,0:T(8,128)(2,1)} %dynamic-slice_bitcast_fusion), channel_id=1, source_target_pairs={{0,8},{8,0},{1,9},{9,1},{2,10},{10,2},{3,11},{11,3},{4,12},{12,4},... | collective-permute-start | bytes 3145736 | tf_op jit(solution)/shard_map/keys/ppermute | solution.py:304
  34.4 12.6 %collective-permute-start = (bf16[32,576]{1,0:T(8,128)(2,1)S(1)}, bf16[32,576]{1,0:T(8,128)(2,1)S(1)}, u32[]{:S(2)}, u32[]{:S(2)}) collective-permute-start(bf16[32,576]{1,0:T(8,128)(2,1)S(1)} %reshape.120), channel_id=1, source_target_pairs={{0,16},{16,0},{1,17},{17,1},{2,18},{18,2},{3,19},{19,3},{4,20},{20... | collective-permute-start | bytes 110600 | tf_op jit(solution)/shard_map/pooled_all/ppermute | solution.py:346
  40.9 28.2 %copy-start.6 = (s32[1,2048]{1,0:T(1,128)S(1)}, s32[1,2048]{1,0:T(1,128)}, u32[]{:S(2)}) copy-start(s32[1,2048]{1,0:T(1,128)} %param.7) | copy-start | bytes 24580
  42.1 19.9 %all-to-all-start.2 = ((f32[16,2,2048]{2,1,0:T(2,128)}), f32[16,2,2048]{2,1,0:T(2,128)S(1)}, u32[]{:S(2)}, u32[]{:S(2)}) async-start(f32[16,2,2048]{2,1,0:T(2,128)} %reshape.122), calls=%async_computation.2 | async-start | bytes 524288 | tf_op jit(solution)/shard_map/gates/all_to_all | solution.py:327
  45.6 82.6 %all-gather.3.cloned.1.call-start = ((), (), s32[]{:S(2)}) async-start(), calls=%async_computation.6 | async-start | bytes 1327104 | tf_op jit(solution)/shard_map/pooled_all/all_gather | solution.py:349
  47.8 11.7 %collective-permute-start.1 = (bf16[2,32,576]{2,1,0:T(8,128)(2,1)S(1)}, bf16[2,32,576]{2,1,0:T(8,128)(2,1)S(1)}, u32[]{:S(2)}, u32[]{:S(2)}) collective-permute-start(bf16[2,32,576]{2,1,0:T(8,128)(2,1)S(1)} %maximum_select_fusion.2), channel_id=1, source_target_pairs={{0,32},{32,0},{1,33},{33,1},{2,34},{34,2},{3,35},{35,3},{4,36},{36... | collective-permute-start | bytes 221192 | tf_op jit(solution)/shard_map/pooled_all/ppermute | solution.py:347
  62.8 13.7 %all-to-all-start.3 = ((bf16[16,2,2048]{2,1,0:T(2,128)(2,1)}), bf16[16,2,2048]{2,1,0:T(2,128)(2,1)S(1)}, u32[]{:S(2)}, u32[]{:S(2)}) async-start(bf16[16,2,2048]{2,1,0:T(2,128)(2,1)} %broadcast_in_dim.25), calls=%async_computation.3 | async-start | bytes 262144 | tf_op jit(solution)/shard_map/gates/all_to_all | solution.py:282
  76.7 0.9 copy-start.3
  77.6 1.6 copy-start.4
  97.8 10.8 %all-to-all-start.1 = ((f32[16,1,512]{2,1,0:T(1,128)}), f32[16,1,512]{2,1,0:T(1,128)S(1)}, u32[]{:S(2)}, u32[]{:S(2)}) async-start(f32[16,1,512]{2,1,0:T(1,128)} %reshape.127), calls=%async_computation.1 | async-start | bytes 65536 | tf_op jit(solution)/shard_map/targets/all_to_all | solution.py:361
  111.0 30.1 %all-to-all-start.4 = ((bf16[32,32,128]{2,1,0:T(8,128)(2,1)}), bf16[32,32,128]{2,1,0:T(8,128)(2,1)S(1)}, u32[]{:S(2)}, u32[]{:S(2)}) async-start(bf16[32,32,128]{2,1,0:T(8,128)(2,1)} %bitcast.19), calls=%async_computation.4 | async-start | bytes 524288 | tf_op jit(solution)/shard_map/gate_grads/all_to_all | solution.py:374
  141.2 1.3 copy-start.2
  164.2 5.0 %collective-permute-start.4 = (bf16[8,288,128]{2,1,0:T(8,128)(2,1)S(1)}, bf16[8,288,128]{2,1,0:T(8,128)(2,1)S(1)}, u32[]{:S(2)}, u32[]{:S(2)}) collective-permute-start(bf16[8,288,128]{2,1,0:T(8,128)(2,1)S(1)} %all_to_all.42.own), channel_id=1, source_target_pairs={{0,16},{16,0},{1,17},{17,1},{2,18},{18,2},{3,19},{19,3},{4,20},{20... | collective-permute-start | bytes 1769480 | tf_op jit(solution)/shard_map/weight_grads/ppermute | solution.py:386
Sparse Core Ops, SparseCore 0:
  15.6 51.3 all-gather.4
  69.1 40.4 all-gather.2

commit v4 on v3

--- a/solution.py
+++ b/solution.py
@@ -32,7 +32,7 @@
 
 
 def attention_kernel(
-    sc, q_own, q_recv, k_ref, after, out_ref, bias_s, k_s, q_s, s0, s1, s2, m_s, l_s, bm_s, acc_s
+    sc, q_own, q_recv, k_ref, gates, after, out_ref, bias_s, k_s, q_s, s0, s1, s2, m_s, l_s, bm_s, acc_s
 ):
     h = pl.program_id(0)
     n0, n1, xl, y = sc[0], sc[1], sc[2], sc[3]
@@ -140,16 +140,19 @@
     def _():
         raw = acc_s[...].reshape(NUM_BLOCKS, 128)
         norm = raw / jnp.sum(raw, axis=0, keepdims=True)
-        mine = norm.T[:16, :]
+        high = norm.astype(jnp.bfloat16).astype(jnp.float32)
+        parts = jnp.concatenate([high, norm - high, jnp.zeros((64, 128), jnp.float32)], axis=0)
+        mine = parts.T[:16, :].astype(jnp.bfloat16)
         for to in range(16):
-            out_ref[to * 16 : (to + 1) * 16, :] = mine
-
-
-def attention_targets(scalars, q, q_recv, k_all, after):
+            out_ref[to * 48 : to * 48 + 32, :] = gates[...]
+            out_ref[to * 48 + 32 : to * 48 + 48, :] = mine
+
+
+def attention_targets(scalars, q, q_recv, k_all, gates, after):
     kw = GROUP * HEAD_DIM
     return pl.pallas_call(
         attention_kernel,
-        out_shape=jax.ShapeDtypeStruct((256, NUM_BLOCKS), jnp.float32),
+        out_shape=jax.ShapeDtypeStruct((16 * 48, 128), jnp.bfloat16),
         grid_spec=pltpu.PrefetchScalarGridSpec(
             num_scalar_prefetch=1,
             grid=(LOCAL_KV,),
@@ -157,9 +160,10 @@
                 pl.BlockSpec((SHARD, kw), lambda h, sc: (0, sc[2] * LOCAL_KV + h)),
                 pl.BlockSpec((SHARD, kw), lambda h, sc: (0, h)),
                 pl.BlockSpec((16 * SHARD, HEAD_DIM), lambda h, sc: (0, h)),
+                pl.BlockSpec((32, 128), lambda h, sc: (0, 0)),
                 pl.BlockSpec(memory_space=pl.ANY),
             ],
-            out_specs=pl.BlockSpec((256, NUM_BLOCKS), lambda h, sc: (0, 0)),
+            out_specs=pl.BlockSpec((16 * 48, 128), lambda h, sc: (0, 0)),
             scratch_shapes=[
                 pltpu.VMEM((3, PANEL, SHARD), jnp.float32),
                 pltpu.VMEM((2 * PANEL, 2 * HEAD_DIM), jnp.bfloat16),
@@ -172,16 +176,16 @@
             ],
         ),
         compiler_params=pltpu.CompilerParams(
-            dimension_semantics=("arbitrary",), vmem_limit_bytes=32 * 1024 * 1024
+            dimension_semantics=("arbitrary",), vmem_limit_bytes=56 * 1024 * 1024
         ),
         cost_estimate=pl.CostEstimate(
             flops=2 * 32 * 128 * 128 * 3072, bytes_accessed=4 << 20, transcendentals=12 << 20
         ),
         name="attention_targets",
-    )(scalars, q, q_recv, k_all, after)
-
-
-def gate_grads_kernel(target, prob, gq, gk, out_ref):
+    )(scalars, q, q_recv, k_all, gates, after)
+
+
+def gate_grads_kernel(target, gates, out_ref):
     left = lax.broadcasted_iota(jnp.int32, (NUM_BLOCKS, GATE_DIM), 1) < GATE_DIM // 2
     row = lax.broadcasted_iota(jnp.int32, (NUM_BLOCKS, NUM_BLOCKS), 0)
     causal = lax.broadcasted_iota(jnp.int32, (NUM_BLOCKS, NUM_BLOCKS), 1) <= row
@@ -195,13 +199,17 @@
         return (total * scale).astype(jnp.bfloat16).astype(jnp.float32)
 
     for head in range(KV_HEADS):
-        cols = slice(head * GATE_DIM, (head + 1) * GATE_DIM)
-        x, h = divmod(head, LOCAL_KV)
-        rows = [(x * 8 + y) * 16 + half * 8 + h * 2 for half in range(2) for y in range(8)]
-        mine = jnp.concatenate([target[r : r + 2, :] for r in rows], axis=0)
-        grad = jnp.where(causal, prob[head] - mine, 0.0)
-        of_q = product(grad, gk[:, cols])
-        of_k = product(grad.T, gq[:, cols])
+        gq, gk = gates[head], gates[KV_HEADS + head]
+        logits = lax.dot_general(
+            gq, gk, (((1,), (1,)), ((), ())), preferred_element_type=jnp.float32
+        )
+        logits = jnp.where(causal, logits * scale, NEG_FILL)
+        weights = jnp.exp(logits - jnp.max(logits, axis=1, keepdims=True))
+        weights = jnp.where(causal, weights, 0.0)
+        prob = weights / jnp.sum(weights, axis=1, keepdims=True)
+        grad = jnp.where(causal, prob - target[head], 0.0)
+        of_q = product(grad, gk)
+        of_k = product(grad.T, gq)
         half = GATE_DIM // 2
         first = jnp.where(left, of_q, pltpu.roll(of_k, half, 1)).astype(jnp.bfloat16)
         second = jnp.where(left, pltpu.roll(of_q, half, 1), of_k).astype(jnp.bfloat16)
@@ -278,12 +286,6 @@
     )(co.astype(jnp.int32).reshape(1), own, other)
 
 
-def spread(x, axes, n):
-    return lax.all_to_all(
-        jnp.broadcast_to(x[None], (n, *x.shape)), axes, split_axis=0, concat_axis=0, tiled=True
-    )
-
-
 def ordered(own, other, index):
     return jnp.where(index == 0, jnp.stack([own, other]), jnp.stack([other, own]))
 
@@ -291,7 +293,6 @@
 def shards(queries, keys, doc_ids, gate_query_weight, gate_key_weight):
     xl, y = lax.axis_index("xl"), lax.axis_index("y")
     co, xh = lax.axis_index("co"), lax.axis_index("xh")
-    gate_scale = 1.0 / GATE_DIM**0.5
     q, k, doc = queries[0], keys[0], doc_ids[0]
     half_kw, half_qw = k.shape[1] // 2, q.shape[1] // 2
 
@@ -328,19 +329,7 @@
             part.reshape(16, 2, -1), CTX_AXES, split_axis=0, concat_axis=0, tiled=True
         )
         gates_mine = jnp.sum(parts, axis=0).astype(jnp.bfloat16)
-        gates = spread(gates_mine, CTX_AXES, 16).reshape(NUM_BLOCKS, -1)
-        gw = gate_query_weight.shape[1]
-        gq = gates[:, :gw].reshape(NUM_BLOCKS, KV_HEADS, GATE_DIM)
-        gk = gates[:, gw:].reshape(NUM_BLOCKS, KV_HEADS, GATE_DIM)
-        logits = (
-            jnp.einsum("ahe,bhe->hab", gq, gk, preferred_element_type=jnp.float32) * gate_scale
-        )
-        block = jnp.arange(NUM_BLOCKS, dtype=jnp.int32)
-        causal = block[None, :] <= block[:, None]
-        masked = jnp.where(causal, logits, NEG_FILL)
-        peak = jnp.max(masked, axis=-1, keepdims=True)
-        weights = jnp.where(causal, jnp.exp(masked - peak), 0.0)
-        gate_prob = weights / jnp.sum(weights, axis=-1, keepdims=True)
+        gates_mine = gates_mine.reshape(2, 16, GATE_DIM).transpose(1, 0, 2).reshape(32, GATE_DIM)
 
     with jax.named_scope("pooled_all"):
         pair = ordered(pooled, lax.ppermute(pooled, "co", SWAP), co)
@@ -357,19 +346,22 @@
                 y.astype(jnp.int32),
             ]
         )
-        mine = attention_targets(scalars, q, q_recv, k_all, quad)
-        target = lax.all_to_all(mine, CTX_AXES, split_axis=0, concat_axis=0, tiled=True)
+        mine = attention_targets(scalars, q, q_recv, k_all, gates_mine, quad)
+        both = lax.all_to_all(mine, CTX_AXES, split_axis=0, concat_axis=0, tiled=True)
+        both = both.reshape(16, 48, 128)
 
     with jax.named_scope("gate_grads"):
+        gates = both[:, :32].reshape(16, 16, 2, GATE_DIM).transpose(1, 0, 2, 3)
+        target = both[:, 32:, :NUM_BLOCKS].astype(jnp.float32)
+        target = target + both[:, 32:, NUM_BLOCKS : 2 * NUM_BLOCKS].astype(jnp.float32)
+        target = target.reshape(2, 8, 2, LOCAL_KV, 2, NUM_BLOCKS).transpose(0, 3, 2, 1, 4, 5)
         grads = in_vmem(
             gate_grads_kernel,
             jax.ShapeDtypeStruct((32 * NUM_BLOCKS, GATE_DIM), jnp.bfloat16),
             "gate_grads",
             16,
-            target,
-            gate_prob,
-            gates[:, :gw],
-            gates[:, gw:],
+            target.reshape(KV_HEADS, NUM_BLOCKS, NUM_BLOCKS),
+            gates.reshape(16, NUM_BLOCKS, GATE_DIM),
         )
         grads = lax.all_to_all(grads, SEQ_AXES, split_axis=0, concat_axis=0, tiled=True)
 

time: 179 us -> 169 us (0.944)
  blocking collectives: 21.2 us -> 34.6 us
  starting transfers between devices: 59.2 us -> 48.2 us
  waiting for transfers between devices: 39.1 us -> 32 us
  local copies, waits for them, and re-layouts: 12.8 us -> 6.95 us
  Pallas kernels: 21.1 us -> 24.4 us
    all_to_all x0 -> x1, blocking collectives: none -> 13.4 us  [shards(): lax.all_to_all(mine, CTX_AXES, split_axis=0, concat_axis=0, tiled=True)]
    all_to_all x2 -> x0, waiting for transfers between devices: 12.3 us -> none  [the longest x1 6.98 us: shards(): lax.all_to_all(mine, CTX_AXES, split_axis=0, concat_axis=0, tiled=True)]
    all_to_all x2 -> x0, starting transfers between devices: 9.81 us -> none  [the longest x1 6.31 us: spread(): lax.all_to_all(jnp.broadcast_to(x[None], (n, *x.shape)), axes, split_axis...]
    ppermute x1, waiting for transfers between devices: 6.9 us -> 10.8 us  [shards(): quad = ordered(pair, lax.ppermute(pair, 'xh', SWAP), xh)]
    unnamed x17 -> x16, local copies, waits for them, and re-layouts: 4.62 us -> 1.98 us
    pallas_call x2, Pallas kernels: 1.58 us -> 4.11 us  [in_vmem(): pl.pallas_call(kernel, out_shape=out_shape, in_specs=[spec] * len(args),...]
    select_n x3, other arithmetic: 2.46 us -> 0.09 us  [ordered(): jnp.where(index == 0, jnp.stack([own, other]), jnp.stack([other, own]))]
  transfers between devices with their start and end apart: 12 -> 10, of which waited for: 7 -> 6; matrix products, arithmetic and copies ran while one was open for 10% -> 7% of each run, Pallas kernels for 11% -> 13%
where the time goes in v4:
time: 169 us; the launch traced here: 168 us
  starting transfers between devices  48.2 us (29%)
  blocking collectives  34.6 us (20%)
  waiting for transfers between devices  32 us (19%)
  Pallas kernels  24.4 us (14%)
  between operations  14.3 us (8%)
  other arithmetic  7.05 us (4%)
  local copies, waits for them, and re-layouts  6.95 us (4%)
    all_to_all x1, blocking collectives, shards(): lax.all_to_all(pieces, 'z', split_axis=0, concat_axis=0, tiled=True)  21.2 us
    pallas_call x1, Pallas kernels, attention_targets(): pl.pallas_call(attention_kernel, out_shape=jax.ShapeDtypeStruct((16 * 48,...  18.7 us
    all_to_all x1, starting transfers between devices, shards(): lax.all_to_all(grads, SEQ_AXES, split_axis=0, concat_axis=0, tiled=True)  16 us
    all_to_all x1, blocking collectives, shards(): lax.all_to_all(mine, CTX_AXES, split_axis=0, concat_axis=0, tiled=True)  13.4 us
    all_to_all x1, waiting for transfers between devices, shards(): lax.all_to_all(grads, SEQ_AXES, split_axis=0, concat_axis=0, tiled=True)  12.9 us
    ppermute x1, waiting for transfers between devices, shards(): quad = ordered(pair, lax.ppermute(pair, 'xh', SWAP), xh)  10.8 us
    all_to_all x1, starting transfers between devices, shards(): lax.all_to_all(mine.transpose(1, 0, 2), CTX_AXES, split_axis=0, concat_ax...  8.64 us
    ppermute x1, starting transfers between devices, shards(): pair = ordered(pooled, lax.ppermute(pooled, 'co', SWAP), co)  5.41 us
  transfers between devices with their start and end apart: 10, of which 6 were waited for; matrix products, arithmetic and copies ran while one was open for 7% of the time, Pallas kernels for 13%

profile of v4, /device:TPU:1, one launch (start us, length us, event | category | flops | bytes accessed | tf_op | source)
XLA Modules:
  0.0 167.9 jit_solution(2803408627495412068)
XLA Ops:
  7.2 0.0 copy-start
  7.2 0.0 all-gather.5.cloned.1.call-start
  7.2 0.0 copy-start.2
  7.3 1.1 dynamic-slice_bitcast_fusion.2
  8.4 3.9 %collective-permute-start.3 = (bf16[128,512]{1,0:T(8,128)(2,1)S(1)}, bf16[128,512]{1,0:T(8,128)(2,1)S(1)}, u32[]{:S(2)}, u32[]{:S(2)}) collective-permute-start(bf16[128,512]{1,0:T(8,128)(2,1)S(1)} %get-tuple-element.5), channel_id=1, source_target_pairs={{0,8},{8,0},{1,9},{9,1},{2,10},{10,2},{3,11},{11,3},{4,12},{12,4},... | collective-permute-start | bytes 393224 | tf_op jit(solution)/shard_map/keys/ppermute | solution.py:302
  12.4 2.3 %collective-permute-done.3 = bf16[128,512]{1,0:T(8,128)(2,1)S(1)} collective-permute-done((bf16[128,512]{1,0:T(8,128)(2,1)S(1)}, bf16[128,512]{1,0:T(8,128)(2,1)S(1)}, u32[]{:S(2)}, u32[]{:S(2)}) %collective-permute-start.3) | collective-permute-done | bytes 131104 | tf_op jit(solution)/shard_map/keys/ppermute | solution.py:302
  14.7 0.7 pad_maximum_fusion
  15.4 0.0 all-gather.5.cloned.1.call-update
  15.4 2.0 %convert_reduce_fusion = f32[2,8192]{1,0:T(2,128)S(1)} fusion(bf16[2,64,8192]{2,1,0:T(8,128)(2,1)} %bitcast.47), kind=kLoop, calls=%fused_computation | loop fusion | flops 2080768 | bytes 2162688 | tf_op jit(solution)/shard_map/pool/reduce_sum | solution.py:309
  17.5 0.6 copy.30
  18.1 0.1 reduce_max.9
  18.2 0.1 reshape.125
  18.3 0.8 maximum_bitcast_fusion
  19.1 0.6 copy.16
  19.7 8.6 %all-to-all-start = ((bf16[16,2,576]{2,1,0:T(2,128)(2,1)}), bf16[16,2,576]{2,1,0:T(2,128)(2,1)S(1)}, u32[]{:S(2)}, u32[]{:S(2)}) async-start(bf16[16,2,576]{2,1,0:T(2,128)(2,1)} %copy.16), calls=%async_computation | async-start | bytes 81920 | tf_op jit(solution)/shard_map/pool/all_to_all | solution.py:313
  28.4 1.0 dynamic-slice_bitcast_fusion
  29.4 3.3 %collective-permute-start.2 = (bf16[128,4096]{1,0:T(8,128)(2,1)}, bf16[128,4096]{1,0:T(8,128)(2,1)S(1)}, u32[]{:S(2)}, u32[]{:S(2)}) collective-permute-start(bf16[128,4096]{1,0:T(8,128)(2,1)} %dynamic-slice_bitcast_fusion), channel_id=1, source_target_pairs={{0,8},{8,0},{1,9},{9,1},{2,10},{10,2},{3,11},{11,3},{4,12},{12,4},... | collective-permute-start | bytes 3145736 | tf_op jit(solution)/shard_map/keys/ppermute | solution.py:305
  32.7 3.0 %all-to-all-done = bf16[16,2,576]{2,1,0:T(2,128)(2,1)S(1)} async-done(((bf16[16,2,576]{2,1,0:T(2,128)(2,1)}), bf16[16,2,576]{2,1,0:T(2,128)(2,1)S(1)}, u32[]{:S(2)}, u32[]{:S(2)}) %all-to-all-start) | async-done | bytes 36896 | tf_op jit(solution)/shard_map/pool/all_to_all | solution.py:313
  35.8 5.4 %collective-permute-start = (bf16[32,576]{1,0:T(8,128)(2,1)S(1)}, bf16[32,576]{1,0:T(8,128)(2,1)S(1)}, u32[]{:S(2)}, u32[]{:S(2)}) collective-permute-start(bf16[32,576]{1,0:T(8,128)(2,1)S(1)} %reshape.126), channel_id=1, source_target_pairs={{0,16},{16,0},{1,17},{17,1},{2,18},{18,2},{3,19},{19,3},{4,20},{20... | collective-permute-start | bytes 110600 | tf_op jit(solution)/shard_map/pooled_all/ppermute | solution.py:335
  41.2 0.3 fusion
  41.5 0.1 fusion.4
  41.7 0.8 reshape.128
  42.5 3.5 %all-to-all-start.1 = ((f32[16,2,2048]{2,1,0:T(2,128)}), f32[16,2,2048]{2,1,0:T(2,128)S(1)}, u32[]{:S(2)}, u32[]{:S(2)}) async-start(f32[16,2,2048]{2,1,0:T(2,128)} %reshape.128), calls=%async_computation.1 | async-start | bytes 524288 | tf_op jit(solution)/shard_map/gates/all_to_all | solution.py:328
  46.1 0.0 all-gather.3.cloned.1.call-start
  46.2 3.9 %collective-permute-start.1 = (bf16[2,32,576]{2,1,0:T(8,128)(2,1)S(1)}, bf16[2,32,576]{2,1,0:T(8,128)(2,1)S(1)}, u32[]{:S(2)}, u32[]{:S(2)}) collective-permute-start(bf16[2,32,576]{2,1,0:T(8,128)(2,1)S(1)} %maximum_select_fusion.2), channel_id=1, source_target_pairs={{0,32},{32,0},{1,33},{33,1},{2,34},{34,2},{3,35},{35,3},{4,36},{36... | collective-permute-start | bytes 221192 | tf_op jit(solution)/shard_map/pooled_all/ppermute | solution.py:336
  50.2 10.8 %collective-permute-done.1 = bf16[2,32,576]{2,1,0:T(8,128)(2,1)S(1)} collective-permute-done((bf16[2,32,576]{2,1,0:T(8,128)(2,1)S(1)}, bf16[2,32,576]{2,1,0:T(8,128)(2,1)S(1)}, u32[]{:S(2)}, u32[]{:S(2)}) %collective-permute-start.1) | collective-permute-done | bytes 73760 | tf_op jit(solution)/shard_map/pooled_all/ppermute | solution.py:336
  61.1 0.8 copy.17
  61.9 0.0 all-gather.3.cloned.1.call-update
  61.9 0.7 fusion.2
  62.6 1.9 %pad_add_fusion.sc = s32[4]{0:T(128)} fusion(s32[1]{0:T(128)} %bitcast.12, s32[1]{0:T(128)} %bitcast.11, s32[1]{0:T(128)} %bitcast.10, s32[1]{0:T(128)} %bitcast.9), kind=kLoop, calls=%fused_computation.21 | loop fusion | flops 12 | bytes 32 | tf_op jit(solution)/shard_map/targets/stack | solution.py:341
  64.5 0.7 reduce_sum.39
  65.2 1.2 all-gather.5.cloned.1.call-done.k_ref
  66.4 18.7 %attention_targets.1 = bf16[768,128]{1,0:T(8,128)(2,1)} custom-call(s32[4]{0:T(128)} %pad_add_fusion.sc, bf16[128,8192]{1,0:T(8,128)(2,1)} %bitcast.48, bf16[128,4096]{1,0:T(8,128)(2,1)} %copy-done.6, bf16[2048,512]{1,0:T(8,128)(2,1)} %all-gather.5.cloned.1.call-done.k_ref, bf16[32,128]{1,0:T(8,128)(2,1)} %bitcast.61, bf16[576,128]{1,0:T(8,128)(2,1)} %bitcast.52), custom_call_target="tpu_custom_call" | custom-call | flops 3221225472 | bytes 4194304 | tf_op jit(solution)/shard_map/targets/attention_targets/pallas_call | solution.py:153
  85.1 13.4 %all_to_all.35 = bf16[16,48,128]{2,1,0:T(8,128)(2,1)S(1)} all-to-all(bf16[16,48,128]{2,1,0:T(8,128)(2,1)} %bitcast.55), channel_id=1, replica_groups=mesh['z'=8,'xh'=2,'co'=2,'xl'=2,'y'=8] {'xl','y'}, dimensions={0} | all-to-all | bytes 393216 | tf_op jit(solution)/shard_map/targets/all_to_all | solution.py:350
  98.5 0.1 fusion.6
  98.6 0.1 copy.20
  98.7 0.1 copy.25
  98.8 0.1 copy.22
  98.9 3.6 %gate_grads.1 = bf16[1024,128]{1,0:T(8,128)(2,1)} custom-call(f32[8,32,32]{2,1,0:T(8,128)S(1)} %bitcast.45, bf16[16,32,128]{2,1,0:T(8,128)(2,1)S(1)} %bitcast.46), custom_call_target="tpu_custom_call" | custom-call | tf_op jit(solution)/shard_map/gate_grads/gate_grads/pallas_call | solution.py:263
  102.5 16.0 %all-to-all-start.3 = ((bf16[32,32,128]{2,1,0:T(8,128)(2,1)}), bf16[32,32,128]{2,1,0:T(8,128)(2,1)S(1)}, u32[]{:S(2)}, u32[]{:S(2)}) async-start(bf16[32,32,128]{2,1,0:T(8,128)(2,1)} %bitcast.27), calls=%async_computation.3 | async-start | bytes 524288 | tf_op jit(solution)/shard_map/gate_grads/all_to_all | solution.py:366
  118.5 0.0 all-gather.3.cloned.1.call-done.pooled
  118.5 12.9 %all-to-all-done.3 = bf16[32,32,128]{2,1,0:T(8,128)(2,1)S(1)} async-done(((bf16[32,32,128]{2,1,0:T(8,128)(2,1)}), bf16[32,32,128]{2,1,0:T(8,128)(2,1)S(1)}, u32[]{:S(2)}, u32[]{:S(2)}) %all-to-all-start.3) | async-done | bytes 262176 | tf_op jit(solution)/shard_map/gate_grads/all_to_all | solution.py:366
  131.4 1.3 copy-done.1
  132.7 0.5 weight_grads.1
  133.2 21.2 %all_to_all.36.own = bf16[8,288,128]{2,1,0:T(8,128)(2,1)S(1)} all-to-all(bf16[8,288,128]{2,1,0:T(8,128)(2,1)S(1)} %weight_grads.1), channel_id=1, replica_groups=mesh['z'=8,'xh'=2,'co'=2,'xl'=2,'y'=8] {'z'}, dimensions={0} | all-to-all | bytes 1179648 | tf_op jit(solution)/shard_map/weight_grads/all_to_all | solution.py:377
  154.4 3.4 %collective-permute-start.4 = (bf16[8,288,128]{2,1,0:T(8,128)(2,1)S(1)}, bf16[8,288,128]{2,1,0:T(8,128)(2,1)S(1)}, u32[]{:S(2)}, u32[]{:S(2)}) collective-permute-start(bf16[8,288,128]{2,1,0:T(8,128)(2,1)S(1)} %all_to_all.36.own), channel_id=1, source_target_pairs={{0,16},{16,0},{1,17},{17,1},{2,18},{18,2},{3,19},{19,3},{4,20},{20... | collective-permute-start | bytes 1769480 | tf_op jit(solution)/shard_map/weight_grads/ppermute | solution.py:378
  157.8 1.6 collective-permute-done.4.other
  159.4 1.6 assembled.1
  (24 shorter events, 0.3 us)
Async XLA Ops:
  7.2 34.0 %copy-start = (bf16[512,1024]{1,0:T(8,128)(2,1)S(1)}, bf16[512,1024]{1,0:T(8,128)(2,1)}, u32[]{:S(2)}) copy-start(bf16[512,1024]{1,0:T(8,128)(2,1)} %param.8) | copy-start | bytes 3145732
  7.2 11.0 %copy-start.3 = (bf16[1,128,1024]{2,1,0:T(8,128)(2,1)S(1)}, bf16[1,128,1024]{2,1,0:T(8,128)(2,1)}, u32[]{:S(2)}) copy-start(bf16[1,128,1024]{2,1,0:T(8,128)(2,1)} %param.6) | copy-start | bytes 786436
  7.2 59.2 %all-gather.5.cloned.1.call-start = ((), (), s32[]{:S(2)}) async-start(), calls=%async_computation.6 | async-start | bytes 2359296 | tf_op jit(solution)/shard_map/keys/all_gather | solution.py:303
  7.2 21.1 %copy-start.2 = (bf16[1,128,8192]{2,1,0:T(8,128)(2,1)S(1)}, bf16[1,128,8192]{2,1,0:T(8,128)(2,1)}, u32[]{:S(2)}) copy-start(bf16[1,128,8192]{2,1,0:T(8,128)(2,1)} %param.5) | copy-start | bytes 6291460
  8.4 6.3 %collective-permute-start.3 = (bf16[128,512]{1,0:T(8,128)(2,1)S(1)}, bf16[128,512]{1,0:T(8,128)(2,1)S(1)}, u32[]{:S(2)}, u32[]{:S(2)}) collective-permute-start(bf16[128,512]{1,0:T(8,128)(2,1)S(1)} %get-tuple-element.5), channel_id=1, source_target_pairs={{0,8},{8,0},{1,9},{9,1},{2,10},{10,2},{3,11},{11,3},{4,12},{12,4},... | collective-permute-start | bytes 393224 | tf_op jit(solution)/shard_map/keys/ppermute | solution.py:302
  17.5 24.0 %copy-start.4 = (bf16[64,1024]{1,0:T(8,128)(2,1)S(1)}, bf16[64,1024]{1,0:T(8,128)(2,1)}, u32[]{:S(2)}) copy-start(bf16[64,1024]{1,0:T(8,128)(2,1)} %param.9) | copy-start | bytes 393220
  19.7 16.0 %all-to-all-start = ((bf16[16,2,576]{2,1,0:T(2,128)(2,1)}), bf16[16,2,576]{2,1,0:T(2,128)(2,1)S(1)}, u32[]{:S(2)}, u32[]{:S(2)}) async-start(bf16[16,2,576]{2,1,0:T(2,128)(2,1)} %copy.16), calls=%async_computation | async-start | bytes 81920 | tf_op jit(solution)/shard_map/pool/all_to_all | solution.py:313
  29.4 35.8 %collective-permute-start.2 = (bf16[128,4096]{1,0:T(8,128)(2,1)}, bf16[128,4096]{1,0:T(8,128)(2,1)S(1)}, u32[]{:S(2)}, u32[]{:S(2)}) collective-permute-start(bf16[128,4096]{1,0:T(8,128)(2,1)} %dynamic-slice_bitcast_fusion), channel_id=1, source_target_pairs={{0,8},{8,0},{1,9},{9,1},{2,10},{10,2},{3,11},{11,3},{4,12},{12,4},... | collective-permute-start | bytes 3145736 | tf_op jit(solution)/shard_map/keys/ppermute | solution.py:305
  35.8 26.1 %copy-start.5 = (s32[1,2048]{1,0:T(1,128)S(1)}, s32[1,2048]{1,0:T(1,128)}, u32[]{:S(2)}) copy-start(s32[1,2048]{1,0:T(1,128)} %param.7) | copy-start | bytes 24580
  35.8 10.4 %collective-permute-start = (bf16[32,576]{1,0:T(8,128)(2,1)S(1)}, bf16[32,576]{1,0:T(8,128)(2,1)S(1)}, u32[]{:S(2)}, u32[]{:S(2)}) collective-permute-start(bf16[32,576]{1,0:T(8,128)(2,1)S(1)} %reshape.126), channel_id=1, source_target_pairs={{0,16},{16,0},{1,17},{17,1},{2,18},{18,2},{3,19},{19,3},{4,20},{20... | collective-permute-start | bytes 110600 | tf_op jit(solution)/shard_map/pooled_all/ppermute | solution.py:335
  42.5 22.0 %all-to-all-start.1 = ((f32[16,2,2048]{2,1,0:T(2,128)}), f32[16,2,2048]{2,1,0:T(2,128)S(1)}, u32[]{:S(2)}, u32[]{:S(2)}) async-start(f32[16,2,2048]{2,1,0:T(2,128)} %reshape.128), calls=%async_computation.1 | async-start | bytes 524288 | tf_op jit(solution)/shard_map/gates/all_to_all | solution.py:328
  46.1 72.5 %all-gather.3.cloned.1.call-start = ((), (), s32[]{:S(2)}) async-start(), calls=%async_computation.5 | async-start | bytes 1327104 | tf_op jit(solution)/shard_map/pooled_all/all_gather | solution.py:338
  46.2 14.8 %collective-permute-start.1 = (bf16[2,32,576]{2,1,0:T(8,128)(2,1)S(1)}, bf16[2,32,576]{2,1,0:T(8,128)(2,1)S(1)}, u32[]{:S(2)}, u32[]{:S(2)}) collective-permute-start(bf16[2,32,576]{2,1,0:T(8,128)(2,1)S(1)} %maximum_select_fusion.2), channel_id=1, source_target_pairs={{0,32},{32,0},{1,33},{33,1},{2,34},{34,2},{3,35},{35,3},{4,36},{36... | collective-permute-start | bytes 221192 | tf_op jit(solution)/shard_map/pooled_all/ppermute | solution.py:336
  65.2 1.2 copy-start.6
  102.5 29.0 %all-to-all-start.3 = ((bf16[32,32,128]{2,1,0:T(8,128)(2,1)}), bf16[32,32,128]{2,1,0:T(8,128)(2,1)S(1)}, u32[]{:S(2)}, u32[]{:S(2)}) async-start(bf16[32,32,128]{2,1,0:T(8,128)(2,1)} %bitcast.27), calls=%async_computation.3 | async-start | bytes 524288 | tf_op jit(solution)/shard_map/gate_grads/all_to_all | solution.py:366
  131.4 1.3 copy-start.1
  154.4 5.0 %collective-permute-start.4 = (bf16[8,288,128]{2,1,0:T(8,128)(2,1)S(1)}, bf16[8,288,128]{2,1,0:T(8,128)(2,1)S(1)}, u32[]{:S(2)}, u32[]{:S(2)}) collective-permute-start(bf16[8,288,128]{2,1,0:T(8,128)(2,1)S(1)} %all_to_all.36.own), channel_id=1, source_target_pairs={{0,16},{16,0},{1,17},{17,1},{2,18},{18,2},{3,19},{19,3},{4,20},{20... | collective-permute-start | bytes 1769480 | tf_op jit(solution)/shard_map/weight_grads/ppermute | solution.py:378
Sparse Core Ops, SparseCore 0:
  15.6 50.8 all-gather.4
  68.5 40.8 all-gather.2

commit v5 on v4

--- a/solution.py
+++ b/solution.py
@@ -1,3 +1,4 @@
+import functools
 import math
 
 import jax
@@ -17,6 +18,7 @@
 PANEL = 1024
 FOLDED = [0, 4, 2, 6, 1, 5, 3, 7]
 LOCAL_KV = 4
+PART_KV = 2
 NUM_BLOCKS = 32
 SEQ_AXES = ("z", "xh", "co")
 CTX_AXES = ("xl", "y")
@@ -31,9 +33,12 @@
     return parts[0]
 
 
-def attention_kernel(
-    sc, q_own, q_recv, k_ref, gates, after, out_ref, bias_s, k_s, q_s, s0, s1, s2, m_s, l_s, bm_s, acc_s
-):
+def attention_kernel(part, sc, q_own, q_recv, k_ref, *refs):
+    if part == 0:
+        out_ref, *scratch = refs
+    else:
+        gates, before, _, out_ref, *scratch = refs
+    bias_s, k_s, q_s, s0, s1, s2, m_s, l_s, bm_s, acc_s = scratch
     h = pl.program_id(0)
     n0, n1, xl, y = sc[0], sc[1], sc[2], sc[3]
     slots = (s0, s1, s2)
@@ -54,7 +59,7 @@
 
     @pl.when(h == 0)
     def _():
-        acc_s[...] = jnp.zeros_like(acc_s)
+        acc_s[...] = jnp.zeros_like(acc_s) if part == 0 else before[...]
         for at, (half, panel) in enumerate(panels):
             rowpos = (half * 8 + y) * SHARD + lax.broadcasted_iota(jnp.int32, (PANEL, SHARD), 1)
             rowstart = jnp.where(rowpos >= n1, n1, jnp.where(rowpos >= n0, n0, 0))
@@ -133,11 +138,14 @@
                 for i in range(2):
                     held = jnp.where(left if i == 0 else ~left, gap, NEG_FILL)
                     best = jnp.exp2(jnp.max(held, axis=1, keepdims=True))
-                    col = half * 8 + h * 2 + i
+                    col = half * 8 + (part * PART_KV + h) * 2 + i
                     acc_s[panel] += jnp.where(lane == col, best, 0.0)
 
-    @pl.when(h == LOCAL_KV - 1)
+    @pl.when(h == PART_KV - 1)
     def _():
+        if part == 0:
+            out_ref[...] = acc_s[...]
+            return
         raw = acc_s[...].reshape(NUM_BLOCKS, 128)
         norm = raw / jnp.sum(raw, axis=0, keepdims=True)
         high = norm.astype(jnp.bfloat16).astype(jnp.float32)
@@ -148,22 +156,33 @@
             out_ref[to * 48 + 32 : to * 48 + 48, :] = mine
 
 
-def attention_targets(scalars, q, q_recv, k_all, gates, after):
+def attention_part(part, scalars, q, q_recv, keys, *rest):
     kw = GROUP * HEAD_DIM
+    sums = (2, NUM_BLOCKS // 2, 128)
+    if part == 0:
+        out, out_type = sums, jnp.float32
+        more = []
+    else:
+        out, out_type = (16 * 48, 128), jnp.bfloat16
+        more = [
+            pl.BlockSpec((32, 128), lambda h, sc: (0, 0)),
+            pl.BlockSpec(sums, lambda h, sc: (0, 0, 0)),
+            pl.BlockSpec(memory_space=pl.ANY),
+        ]
+    own = LOCAL_KV // PART_KV
     return pl.pallas_call(
-        attention_kernel,
-        out_shape=jax.ShapeDtypeStruct((16 * 48, 128), jnp.bfloat16),
+        functools.partial(attention_kernel, part),
+        out_shape=jax.ShapeDtypeStruct(out, out_type),
         grid_spec=pltpu.PrefetchScalarGridSpec(
             num_scalar_prefetch=1,
-            grid=(LOCAL_KV,),
+            grid=(PART_KV,),
             in_specs=[
-                pl.BlockSpec((SHARD, kw), lambda h, sc: (0, sc[2] * LOCAL_KV + h)),
+                pl.BlockSpec((SHARD, kw), lambda h, sc: (0, (sc[2] * own + part) * PART_KV + h)),
                 pl.BlockSpec((SHARD, kw), lambda h, sc: (0, h)),
                 pl.BlockSpec((16 * SHARD, HEAD_DIM), lambda h, sc: (0, h)),
-                pl.BlockSpec((32, 128), lambda h, sc: (0, 0)),
-                pl.BlockSpec(memory_space=pl.ANY),
+                *more,
             ],
-            out_specs=pl.BlockSpec((16 * 48, 128), lambda h, sc: (0, 0)),
+            out_specs=pl.BlockSpec(out, lambda h, sc: (0,) * len(out)),
             scratch_shapes=[
                 pltpu.VMEM((3, PANEL, SHARD), jnp.float32),
                 pltpu.VMEM((2 * PANEL, 2 * HEAD_DIM), jnp.bfloat16),
@@ -179,10 +198,10 @@
             dimension_semantics=("arbitrary",), vmem_limit_bytes=56 * 1024 * 1024
         ),
         cost_estimate=pl.CostEstimate(
-            flops=2 * 32 * 128 * 128 * 3072, bytes_accessed=4 << 20, transcendentals=12 << 20
+            flops=2 * 16 * 128 * 128 * 3072, bytes_accessed=2 << 20, transcendentals=6 << 20
         ),
-        name="attention_targets",
-    )(scalars, q, q_recv, k_all, gates, after)
+        name=f"attention_{part}",
+    )(scalars, q, q_recv, keys, *rest)
 
 
 def gate_grads_kernel(target, gates, out_ref):
@@ -198,23 +217,30 @@
         total = total + jnp.dot(low, other, preferred_element_type=jnp.float32)
         return (total * scale).astype(jnp.bfloat16).astype(jnp.float32)
 
-    for head in range(KV_HEADS):
-        gq, gk = gates[head], gates[KV_HEADS + head]
-        logits = lax.dot_general(
-            gq, gk, (((1,), (1,)), ((), ())), preferred_element_type=jnp.float32
-        )
-        logits = jnp.where(causal, logits * scale, NEG_FILL)
-        weights = jnp.exp(logits - jnp.max(logits, axis=1, keepdims=True))
-        weights = jnp.where(causal, weights, 0.0)
-        prob = weights / jnp.sum(weights, axis=1, keepdims=True)
-        grad = jnp.where(causal, prob - target[head], 0.0)
-        of_q = product(grad, gk)
-        of_k = product(grad.T, gq)
-        half = GATE_DIM // 2
-        first = jnp.where(left, of_q, pltpu.roll(of_k, half, 1)).astype(jnp.bfloat16)
-        second = jnp.where(left, pltpu.roll(of_q, half, 1), of_k).astype(jnp.bfloat16)
+    heads = range(KV_HEADS)
+    logits = [
+        lax.dot_general(
+            gates[g],
+            gates[KV_HEADS + g],
+            (((1,), (1,)), ((), ())),
+            preferred_element_type=jnp.float32,
+        )
+        for g in heads
+    ]
+    logits = jnp.where(causal[None], jnp.stack(logits) * scale, NEG_FILL)
+    weights = jnp.exp(logits - jnp.max(logits, axis=2, keepdims=True))
+    weights = jnp.where(causal[None], weights, 0.0)
+    prob = weights / jnp.sum(weights, axis=2, keepdims=True)
+    grad = jnp.where(causal[None], prob - target[...], 0.0)
+    turned = [grad[g].T for g in heads]
+    of_q = [product(grad[g], gates[KV_HEADS + g]) for g in heads]
+    of_k = [product(turned[g], gates[g]) for g in heads]
+    half = GATE_DIM // 2
+    for g in heads:
+        first = jnp.where(left, of_q[g], pltpu.roll(of_k[g], half, 1)).astype(jnp.bfloat16)
+        second = jnp.where(left, pltpu.roll(of_q[g], half, 1), of_k[g]).astype(jnp.bfloat16)
         for to in range(4):
-            at = (head * 4 + to) * NUM_BLOCKS
+            at = (g * 4 + to) * NUM_BLOCKS
             out_ref[at : at + NUM_BLOCKS, :] = first if to % 2 == 0 else second
 
 
@@ -300,9 +326,20 @@
         k_mine = lax.dynamic_slice_in_dim(k, xl * half_kw, half_kw, 1)
         k_other = lax.dynamic_slice_in_dim(k, (1 - xl) * half_kw, half_kw, 1)
         k_recv = lax.ppermute(k_other, "xl", SWAP)
-        k_all = lax.all_gather(jnp.concatenate([k_mine, k_recv]), "y", axis=0, tiled=True)
-        q_other = lax.dynamic_slice_in_dim(q, (1 - xl) * half_qw, half_qw, 1)
-        q_recv = lax.ppermute(q_other, "xl", SWAP)
+        kk = jnp.concatenate([k_mine, k_recv])
+        part_kw, part_qw = half_kw // 2, half_qw // 2
+        first = jnp.broadcast_to(kk[None, :, :part_kw], (8, kk.shape[0], part_kw))
+        first = lax.all_to_all(first, "y", split_axis=0, concat_axis=0, tiled=True)
+        second = lax.all_gather(kk[:, part_kw:], "y", axis=0, tiled=True)
+        keys_of = (first.reshape(-1, part_kw), second)
+        q_recv = [
+            lax.ppermute(
+                lax.dynamic_slice_in_dim(q, (1 - xl) * half_qw + part * part_qw, part_qw, 1),
+                "xl",
+                SWAP,
+            )
+            for part in range(2)
+        ]
 
     with jax.named_scope("pool"):
         pool_q = (
@@ -346,7 +383,8 @@
                 y.astype(jnp.int32),
             ]
         )
-        mine = attention_targets(scalars, q, q_recv, k_all, gates_mine, quad)
+        sums = attention_part(0, scalars, q, q_recv[0], keys_of[0])
+        mine = attention_part(1, scalars, q, q_recv[1], keys_of[1], gates_mine, sums, quad)
         both = lax.all_to_all(mine, CTX_AXES, split_axis=0, concat_axis=0, tiled=True)
         both = both.reshape(16, 48, 128)
 

time: 169 us -> 182 us (1.077)
  waiting for transfers between devices: 32 us -> 36 us
  starting transfers between devices: 48.2 us -> 52.1 us
  local copies, waits for them, and re-layouts: 6.95 us -> 9.42 us
  blocking collectives: 34.6 us -> 37 us
    all_to_all x1, waiting for transfers between devices: 0.01 us -> 6.1 us  [shards(): lax.all_to_all(part.reshape(16, 2, -1), CTX_AXES, split_axis=0, concat_ax...]
    all_to_all x0 -> x1, starting transfers between devices: none -> 4.25 us  [shards(): first = lax.all_to_all(first, 'y', split_axis=0, concat_axis=0, tiled=True)]
    pallas_call x1 -> x2, Pallas kernels: 18.7 us -> 21.4 us  [attention_part(): pl.pallas_call(functools.partial(attention_kernel, part), out_shape=jax.S...]
    all_to_all x1, blocking collectives: 13.4 us -> 15.8 us  [shards(): lax.all_to_all(mine, CTX_AXES, split_axis=0, concat_axis=0, tiled=True)]
    ppermute x1, waiting for transfers between devices: 2.34 us -> 0.01 us  [shards(): k_recv = lax.ppermute(k_other, 'xl', SWAP)]
    pallas_call x2, Pallas kernels: 4.11 us -> 1.85 us  [in_vmem(): pl.pallas_call(kernel, out_shape=out_shape, in_specs=[spec] * len(args),...]
    broadcast_in_dim x0 -> x1, local copies, waits for them, and re-layouts: none -> 1.94 us  [shards(): first = jnp.broadcast_to(kk[None, :, :part_kw], (8, kk.shape[0], part_kw))]
    ppermute x1 -> x2, starting transfers between devices: 3.26 us -> 4.43 us  [shards(): lax.ppermute(lax.dynamic_slice_in_dim(q, (1 - xl) * half_qw + part * part...]
  transfers between devices with their start and end apart: 10 -> 12, of which waited for: 6 -> 5; matrix products, arithmetic and copies ran while one was open for 7% -> 6% of each run, Pallas kernels for 13% -> 13%
where the time goes in v5:
time: 182 us
  starting transfers between devices  52.1 us (29%)
  blocking collectives  37 us (20%)
  waiting for transfers between devices  36 us (20%)
  Pallas kernels  24.9 us (14%)
  between operations  14.4 us (8%)
  local copies, waits for them, and re-layouts  9.42 us (5%)
  other arithmetic  7.41 us (4%)
    pallas_call x2, Pallas kernels, attention_part(): pl.pallas_call(functools.partial(attention_kernel, part), out_shape=jax.S...  21.4 us
    all_to_all x1, blocking collectives, shards(): lax.all_to_all(pieces, 'z', split_axis=0, concat_axis=0, tiled=True)  21.2 us
    all_to_all x1, blocking collectives, shards(): lax.all_to_all(mine, CTX_AXES, split_axis=0, concat_axis=0, tiled=True)  15.8 us
    all_to_all x1, starting transfers between devices, shards(): lax.all_to_all(grads, SEQ_AXES, split_axis=0, concat_axis=0, tiled=True)  14.6 us
    all_to_all x1, waiting for transfers between devices, shards(): lax.all_to_all(grads, SEQ_AXES, split_axis=0, concat_axis=0, tiled=True)  12.9 us
    ppermute x1, waiting for transfers between devices, shards(): quad = ordered(pair, lax.ppermute(pair, 'xh', SWAP), xh)  11.9 us
    all_to_all x1, starting transfers between devices, shards(): lax.all_to_all(mine.transpose(1, 0, 2), CTX_AXES, split_axis=0, concat_ax...  8.68 us
    all_to_all x1, waiting for transfers between devices, shards(): lax.all_to_all(part.reshape(16, 2, -1), CTX_AXES, split_axis=0, concat_ax...  6.1 us
  transfers between devices with their start and end apart: 12, of which 5 were waited for; matrix products, arithmetic and copies ran while one was open for 6% of the time, Pallas kernels for 13%

profile of v5, /device:TPU:1, one launch (start us, length us, event | category | flops | bytes accessed | tf_op | source)
XLA Modules:
  0.0 181.5 jit_solution(15651274570957752738)
XLA Ops:
  7.2 2.1 %convert_reduce_fusion = f32[2,8192]{1,0:T(2,128)S(1)} fusion(bf16[2,64,8192]{2,1,0:T(8,128)(2,1)} %bitcast.50), kind=kLoop, calls=%fused_computation | loop fusion | flops 2080768 | bytes 2162688 | tf_op jit(solution)/shard_map/pool/reduce_sum | solution.py:346
  9.4 0.1 reduce_max.9
  9.5 0.1 reshape.130
  9.6 0.6 copy.16
  10.2 8.7 %all-to-all-start = ((bf16[16,2,576]{2,1,0:T(2,128)(2,1)}), bf16[16,2,576]{2,1,0:T(2,128)(2,1)S(1)}, u32[]{:S(2)}, u32[]{:S(2)}) async-start(bf16[16,2,576]{2,1,0:T(2,128)(2,1)} %copy.16), calls=%async_computation | async-start | bytes 81920 | tf_op jit(solution)/shard_map/pool/all_to_all | solution.py:350
  18.9 0.7 dynamic-slice_bitcast_fusion.2
  19.6 3.3 %collective-permute-start.3 = (bf16[128,512]{1,0:T(8,128)(2,1)}, bf16[128,512]{1,0:T(8,128)(2,1)}, u32[]{:S(2)}, u32[]{:S(2)}) collective-permute-start(bf16[128,512]{1,0:T(8,128)(2,1)} %get-tuple-element.8), channel_id=1, source_target_pairs={{0,8},{8,0},{1,9},{9,1},{2,10},{10,2},{3,11},{11,3},{4,12},{12,4},... | collective-permute-start | bytes 393224 | tf_op jit(solution)/shard_map/keys/ppermute | solution.py:328
  22.9 3.4 %all-to-all-done = bf16[16,2,576]{2,1,0:T(2,128)(2,1)S(1)} async-done(((bf16[16,2,576]{2,1,0:T(2,128)(2,1)}), bf16[16,2,576]{2,1,0:T(2,128)(2,1)S(1)}, u32[]{:S(2)}, u32[]{:S(2)}) %all-to-all-start) | async-done | bytes 36896 | tf_op jit(solution)/shard_map/pool/all_to_all | solution.py:350
  26.3 0.3 fusion.1
  26.6 0.2 fusion.5
  26.8 0.8 reshape.133
  27.6 3.5 %all-to-all-start.1 = ((f32[16,2,2048]{2,1,0:T(2,128)}), f32[16,2,2048]{2,1,0:T(2,128)S(1)}, u32[]{:S(2)}, u32[]{:S(2)}) async-start(f32[16,2,2048]{2,1,0:T(2,128)} %reshape.133), calls=%async_computation.1 | async-start | bytes 524288 | tf_op jit(solution)/shard_map/gates/all_to_all | solution.py:365
  31.2 0.0 all-gather.5.cloned.1.call-start
  31.2 1.8 pad_maximum_fusion.1
  33.0 6.1 %all-to-all-done.1 = f32[16,2,2048]{2,1,0:T(2,128)S(1)} async-done(((f32[16,2,2048]{2,1,0:T(2,128)}), f32[16,2,2048]{2,1,0:T(2,128)S(1)}, u32[]{:S(2)}, u32[]{:S(2)}) %all-to-all-start.1) | async-done | bytes 262176 | tf_op jit(solution)/shard_map/gates/all_to_all | solution.py:365
  39.1 1.9 %broadcast_in_dim.2 = bf16[8,256,256]{2,1,0:T(8,128)(2,1)} broadcast(bf16[256,256]{1,0:T(8,128)(2,1)} %get-tuple-element.6), dimensions={1,2} | broadcast | bytes 1179648 | tf_op jit(solution)/shard_map/keys/broadcast_in_dim | solution.py:331
  41.1 4.2 %all-to-all-start.2 = ((bf16[8,256,256]{2,1,0:T(8,128)(2,1)}), bf16[8,256,256]{2,1,0:T(8,128)(2,1)}, u32[]{:S(2)}, u32[]{:S(2)}) async-start(bf16[8,256,256]{2,1,0:T(8,128)(2,1)} %broadcast_in_dim.2), calls=%async_computation.2 | async-start | bytes 2097152 | tf_op jit(solution)/shard_map/keys/all_to_all | solution.py:332
  45.4 0.0 all-gather.3.cloned.1.call-start
  45.4 5.8 %collective-permute-start = (bf16[32,576]{1,0:T(8,128)(2,1)S(1)}, bf16[32,576]{1,0:T(8,128)(2,1)S(1)}, u32[]{:S(2)}, u32[]{:S(2)}) collective-permute-start(bf16[32,576]{1,0:T(8,128)(2,1)S(1)} %reshape.131), channel_id=1, source_target_pairs={{0,16},{16,0},{1,17},{17,1},{2,18},{18,2},{3,19},{19,3},{4,20},{20... | collective-permute-start | bytes 110600 | tf_op jit(solution)/shard_map/pooled_all/ppermute | solution.py:372
  51.3 1.0 dynamic-slice_bitcast_fusion
  52.3 2.5 %collective-permute-start.4 = (bf16[128,2048]{1,0:T(8,128)(2,1)}, bf16[128,2048]{1,0:T(8,128)(2,1)S(1)}, u32[]{:S(2)}, u32[]{:S(2)}) collective-permute-start(bf16[128,2048]{1,0:T(8,128)(2,1)} %get-tuple-element.4), channel_id=1, source_target_pairs={{0,8},{8,0},{1,9},{9,1},{2,10},{10,2},{3,11},{11,3},{4,12},{12,4},... | collective-permute-start | bytes 1572872 | tf_op jit(solution)/shard_map/keys/ppermute | solution.py:336
  55.0 4.0 %collective-permute-start.1 = (bf16[2,32,576]{2,1,0:T(8,128)(2,1)S(1)}, bf16[2,32,576]{2,1,0:T(8,128)(2,1)S(1)}, u32[]{:S(2)}, u32[]{:S(2)}) collective-permute-start(bf16[2,32,576]{2,1,0:T(8,128)(2,1)S(1)} %maximum_select_fusion.2), channel_id=1, source_target_pairs={{0,32},{32,0},{1,33},{33,1},{2,34},{34,2},{3,35},{35,3},{4,36},{36... | collective-permute-start | bytes 221192 | tf_op jit(solution)/shard_map/pooled_all/ppermute | solution.py:373
  59.1 11.9 %collective-permute-done.1 = bf16[2,32,576]{2,1,0:T(8,128)(2,1)S(1)} collective-permute-done((bf16[2,32,576]{2,1,0:T(8,128)(2,1)S(1)}, bf16[2,32,576]{2,1,0:T(8,128)(2,1)S(1)}, u32[]{:S(2)}, u32[]{:S(2)}) %collective-permute-start.1) | collective-permute-done | bytes 73760 | tf_op jit(solution)/shard_map/pooled_all/ppermute | solution.py:373
  71.0 0.8 copy.17
  71.8 0.0 all-gather.3.cloned.1.call-update
  71.9 1.9 %collective-permute-start.2 = (bf16[128,2048]{1,0:T(8,128)(2,1)}, bf16[128,2048]{1,0:T(8,128)(2,1)S(1)}, u32[]{:S(2)}, u32[]{:S(2)}) collective-permute-start(bf16[128,2048]{1,0:T(8,128)(2,1)} %get-tuple-element.5), channel_id=1, source_target_pairs={{0,8},{8,0},{1,9},{9,1},{2,10},{10,2},{3,11},{11,3},{4,12},{12,4},... | collective-permute-start | bytes 1572872 | tf_op jit(solution)/shard_map/keys/ppermute | solution.py:336
  73.8 0.7 fusion.3
  74.5 1.9 %pad_add_fusion.sc = s32[4]{0:T(128)} fusion(s32[1]{0:T(128)} %bitcast.12, s32[1]{0:T(128)} %bitcast.11, s32[1]{0:T(128)} %bitcast.10, s32[1]{0:T(128)} %bitcast.9), kind=kLoop, calls=%fused_computation.25 | loop fusion | flops 12 | bytes 32 | tf_op jit(solution)/shard_map/targets/stack | solution.py:378
  76.4 0.7 reduce_sum.39
  77.1 0.8 copy-done.6
  77.8 10.7 %attention_0.1.refs_1_ = f32[2,16,128]{2,1,0:T(8,128)} custom-call(s32[4]{0:T(128)} %pad_add_fusion.sc, bf16[128,8192]{1,0:T(8,128)(2,1)} %bitcast.51, bf16[128,2048]{1,0:T(8,128)(2,1)} %copy-done.6, bf16[2048,256]{1,0:T(8,128)(2,1)} %bitcast.21.k_ref), custom_call_target="tpu_custom_call" | custom-call | flops 1610612736 | bytes 2097152 | tf_op jit(solution)/shard_map/targets/attention_0/pallas_call | solution.py:173
  88.5 0.8 copy-done.7
  89.3 10.8 %attention_1.1 = bf16[768,128]{1,0:T(8,128)(2,1)} custom-call(s32[4]{0:T(128)} %pad_add_fusion.sc, bf16[128,8192]{1,0:T(8,128)(2,1)} %bitcast.52, bf16[128,2048]{1,0:T(8,128)(2,1)} %copy-done.7, bf16[2048,256]{1,0:T(8,128)(2,1)} %all-gather.5.cloned.1.call-done.k_ref, bf16[32,128]{1,0:T(8,128)(2,1)} %bitcast.65, f32[2,16,128]{2,1,0:T(8,128)} %attention_0.1.refs_1_, ...), custom_call_target="tpu_custom_call" | custom-call | flops 1610612736 | bytes 2097152 | tf_op jit(solution)/shard_map/targets/attention_1/pallas_call | solution.py:173
  100.1 15.8 %all_to_all.40 = bf16[16,48,128]{2,1,0:T(8,128)(2,1)S(1)} all-to-all(bf16[16,48,128]{2,1,0:T(8,128)(2,1)} %bitcast.59), channel_id=1, replica_groups=mesh['z'=8,'xh'=2,'co'=2,'xl'=2,'y'=8] {'xl','y'}, dimensions={0} | all-to-all | bytes 393216 | tf_op jit(solution)/shard_map/targets/all_to_all | solution.py:388
  115.8 0.1 fusion.7
  116.0 0.1 copy.20
  116.1 0.1 copy.25
  116.1 0.1 copy.22
  116.2 1.3 gate_grads.1
  117.6 14.6 %all-to-all-start.4 = ((bf16[32,32,128]{2,1,0:T(8,128)(2,1)}), bf16[32,32,128]{2,1,0:T(8,128)(2,1)S(1)}, u32[]{:S(2)}, u32[]{:S(2)}) async-start(bf16[32,32,128]{2,1,0:T(8,128)(2,1)} %bitcast.29), calls=%async_computation.4 | async-start | bytes 524288 | tf_op jit(solution)/shard_map/gate_grads/all_to_all | solution.py:404
  132.1 0.0 all-gather.3.cloned.1.call-done.pooled
  132.2 12.9 %all-to-all-done.4 = bf16[32,32,128]{2,1,0:T(8,128)(2,1)S(1)} async-done(((bf16[32,32,128]{2,1,0:T(8,128)(2,1)}), bf16[32,32,128]{2,1,0:T(8,128)(2,1)S(1)}, u32[]{:S(2)}, u32[]{:S(2)}) %all-to-all-start.4) | async-done | bytes 262176 | tf_op jit(solution)/shard_map/gate_grads/all_to_all | solution.py:404
  145.1 1.3 copy-done.1
  146.3 0.5 weight_grads.1
  146.9 21.2 %all_to_all.41.own = bf16[8,288,128]{2,1,0:T(8,128)(2,1)S(1)} all-to-all(bf16[8,288,128]{2,1,0:T(8,128)(2,1)S(1)} %weight_grads.1), channel_id=1, replica_groups=mesh['z'=8,'xh'=2,'co'=2,'xl'=2,'y'=8] {'z'}, dimensions={0} | all-to-all | bytes 1179648 | tf_op jit(solution)/shard_map/weight_grads/all_to_all | solution.py:415
  168.1 3.4 %collective-permute-start.5 = (bf16[8,288,128]{2,1,0:T(8,128)(2,1)S(1)}, bf16[8,288,128]{2,1,0:T(8,128)(2,1)S(1)}, u32[]{:S(2)}, u32[]{:S(2)}) collective-permute-start(bf16[8,288,128]{2,1,0:T(8,128)(2,1)S(1)} %all_to_all.41.own), channel_id=1, source_target_pairs={{0,16},{16,0},{1,17},{17,1},{2,18},{18,2},{3,19},{19,3},{4,20},{20... | collective-permute-start | bytes 1769480 | tf_op jit(solution)/shard_map/weight_grads/ppermute | solution.py:416
  171.5 1.6 collective-permute-done.5.other
  173.1 1.6 assembled.1
  (32 shorter events, 0.4 us)
Async XLA Ops:
  7.2 19.1 %copy-start = (bf16[512,1024]{1,0:T(8,128)(2,1)S(1)}, bf16[512,1024]{1,0:T(8,128)(2,1)}, u32[]{:S(2)}) copy-start(bf16[512,1024]{1,0:T(8,128)(2,1)} %param.8) | copy-start | bytes 3145732
  7.2 2.2 %copy-start.3 = (bf16[1,128,1024]{2,1,0:T(8,128)(2,1)S(1)}, bf16[1,128,1024]{2,1,0:T(8,128)(2,1)}, u32[]{:S(2)}) copy-start(bf16[1,128,1024]{2,1,0:T(8,128)(2,1)} %param.6) | copy-start | bytes 786436
  7.2 19.4 %copy-start.4 = (bf16[64,1024]{1,0:T(8,128)(2,1)S(1)}, bf16[64,1024]{1,0:T(8,128)(2,1)}, u32[]{:S(2)}) copy-start(bf16[64,1024]{1,0:T(8,128)(2,1)} %param.9) | copy-start | bytes 393220
  10.2 16.0 %all-to-all-start = ((bf16[16,2,576]{2,1,0:T(2,128)(2,1)}), bf16[16,2,576]{2,1,0:T(2,128)(2,1)S(1)}, u32[]{:S(2)}, u32[]{:S(2)}) async-start(bf16[16,2,576]{2,1,0:T(2,128)(2,1)} %copy.16), calls=%async_computation | async-start | bytes 81920 | tf_op jit(solution)/shard_map/pool/all_to_all | solution.py:350
  19.6 11.6 %collective-permute-start.3 = (bf16[128,512]{1,0:T(8,128)(2,1)}, bf16[128,512]{1,0:T(8,128)(2,1)}, u32[]{:S(2)}, u32[]{:S(2)}) collective-permute-start(bf16[128,512]{1,0:T(8,128)(2,1)} %get-tuple-element.8), channel_id=1, source_target_pairs={{0,8},{8,0},{1,9},{9,1},{2,10},{10,2},{3,11},{11,3},{4,12},{12,4},... | collective-permute-start | bytes 393224 | tf_op jit(solution)/shard_map/keys/ppermute | solution.py:328
  27.6 11.5 %all-to-all-start.1 = ((f32[16,2,2048]{2,1,0:T(2,128)}), f32[16,2,2048]{2,1,0:T(2,128)S(1)}, u32[]{:S(2)}, u32[]{:S(2)}) async-start(f32[16,2,2048]{2,1,0:T(2,128)} %reshape.133), calls=%async_computation.1 | async-start | bytes 524288 | tf_op jit(solution)/shard_map/gates/all_to_all | solution.py:365
  31.2 20.1 %copy-start.2 = (bf16[1,128,8192]{2,1,0:T(8,128)(2,1)S(1)}, bf16[1,128,8192]{2,1,0:T(8,128)(2,1)}, u32[]{:S(2)}) copy-start(bf16[1,128,8192]{2,1,0:T(8,128)(2,1)} %param.5) | copy-start | bytes 6291460
  31.2 57.3 %all-gather.5.cloned.1.call-start = ((), (), s32[]{:S(2)}) async-start(), calls=%async_computation.7 | async-start | bytes 1179648 | tf_op jit(solution)/shard_map/keys/all_gather | solution.py:333
  41.1 36.0 %all-to-all-start.2 = ((bf16[8,256,256]{2,1,0:T(8,128)(2,1)}), bf16[8,256,256]{2,1,0:T(8,128)(2,1)}, u32[]{:S(2)}, u32[]{:S(2)}) async-start(bf16[8,256,256]{2,1,0:T(8,128)(2,1)} %broadcast_in_dim.2), calls=%async_computation.2 | async-start | bytes 2097152 | tf_op jit(solution)/shard_map/keys/all_to_all | solution.py:332
  45.3 28.5 %copy-start.5 = (s32[1,2048]{1,0:T(1,128)S(1)}, s32[1,2048]{1,0:T(1,128)}, u32[]{:S(2)}) copy-start(s32[1,2048]{1,0:T(1,128)} %param.7) | copy-start | bytes 24580
  45.4 86.8 %all-gather.3.cloned.1.call-start = ((), (), s32[]{:S(2)}) async-start(), calls=%async_computation.6 | async-start | bytes 1327104 | tf_op jit(solution)/shard_map/pooled_all/all_gather | solution.py:375
  45.4 9.5 %collective-permute-start = (bf16[32,576]{1,0:T(8,128)(2,1)S(1)}, bf16[32,576]{1,0:T(8,128)(2,1)S(1)}, u32[]{:S(2)}, u32[]{:S(2)}) collective-permute-start(bf16[32,576]{1,0:T(8,128)(2,1)S(1)} %reshape.131), channel_id=1, source_target_pairs={{0,16},{16,0},{1,17},{17,1},{2,18},{18,2},{3,19},{19,3},{4,20},{20... | collective-permute-start | bytes 110600 | tf_op jit(solution)/shard_map/pooled_all/ppermute | solution.py:372
  52.3 24.8 %collective-permute-start.4 = (bf16[128,2048]{1,0:T(8,128)(2,1)}, bf16[128,2048]{1,0:T(8,128)(2,1)S(1)}, u32[]{:S(2)}, u32[]{:S(2)}) collective-permute-start(bf16[128,2048]{1,0:T(8,128)(2,1)} %get-tuple-element.4), channel_id=1, source_target_pairs={{0,8},{8,0},{1,9},{9,1},{2,10},{10,2},{3,11},{11,3},{4,12},{12,4},... | collective-permute-start | bytes 1572872 | tf_op jit(solution)/shard_map/keys/ppermute | solution.py:336
  55.0 16.0 %collective-permute-start.1 = (bf16[2,32,576]{2,1,0:T(8,128)(2,1)S(1)}, bf16[2,32,576]{2,1,0:T(8,128)(2,1)S(1)}, u32[]{:S(2)}, u32[]{:S(2)}) collective-permute-start(bf16[2,32,576]{2,1,0:T(8,128)(2,1)S(1)} %maximum_select_fusion.2), channel_id=1, source_target_pairs={{0,32},{32,0},{1,33},{33,1},{2,34},{34,2},{3,35},{35,3},{4,36},{36... | collective-permute-start | bytes 221192 | tf_op jit(solution)/shard_map/pooled_all/ppermute | solution.py:373
  71.9 16.7 %collective-permute-start.2 = (bf16[128,2048]{1,0:T(8,128)(2,1)}, bf16[128,2048]{1,0:T(8,128)(2,1)S(1)}, u32[]{:S(2)}, u32[]{:S(2)}) collective-permute-start(bf16[128,2048]{1,0:T(8,128)(2,1)} %get-tuple-element.5), channel_id=1, source_target_pairs={{0,8},{8,0},{1,9},{9,1},{2,10},{10,2},{3,11},{11,3},{4,12},{12,4},... | collective-permute-start | bytes 1572872 | tf_op jit(solution)/shard_map/keys/ppermute | solution.py:336
  77.1 0.8 copy-start.6
  88.5 0.8 copy-start.7
  117.6 27.5 %all-to-all-start.4 = ((bf16[32,32,128]{2,1,0:T(8,128)(2,1)}), bf16[32,32,128]{2,1,0:T(8,128)(2,1)S(1)}, u32[]{:S(2)}, u32[]{:S(2)}) async-start(bf16[32,32,128]{2,1,0:T(8,128)(2,1)} %bitcast.29), calls=%async_computation.4 | async-start | bytes 524288 | tf_op jit(solution)/shard_map/gate_grads/all_to_all | solution.py:404
  145.1 1.3 copy-start.1
  168.1 5.0 %collective-permute-start.5 = (bf16[8,288,128]{2,1,0:T(8,128)(2,1)S(1)}, bf16[8,288,128]{2,1,0:T(8,128)(2,1)S(1)}, u32[]{:S(2)}, u32[]{:S(2)}) collective-permute-start(bf16[8,288,128]{2,1,0:T(8,128)(2,1)S(1)} %all_to_all.41.own), channel_id=1, source_target_pairs={{0,16},{16,0},{1,17},{17,1},{2,18},{18,2},{3,19},{19,3},{4,20},{20... | collective-permute-start | bytes 1769480 | tf_op jit(solution)/shard_map/weight_grads/ppermute | solution.py:416
Sparse Core Ops, SparseCore 0:
  34.1 51.0 all-gather.4
  87.2 40.5 all-gather.2

commit v6 on v4

--- a/solution.py
+++ b/solution.py
@@ -17,6 +17,7 @@
 PANEL = 1024
 FOLDED = [0, 4, 2, 6, 1, 5, 3, 7]
 LOCAL_KV = 4
+Z_STEP = 2
 NUM_BLOCKS = 32
 SEQ_AXES = ("z", "xh", "co")
 CTX_AXES = ("xl", "y")
@@ -198,36 +199,61 @@
         total = total + jnp.dot(low, other, preferred_element_type=jnp.float32)
         return (total * scale).astype(jnp.bfloat16).astype(jnp.float32)
 
-    for head in range(KV_HEADS):
-        gq, gk = gates[head], gates[KV_HEADS + head]
-        logits = lax.dot_general(
-            gq, gk, (((1,), (1,)), ((), ())), preferred_element_type=jnp.float32
-        )
-        logits = jnp.where(causal, logits * scale, NEG_FILL)
-        weights = jnp.exp(logits - jnp.max(logits, axis=1, keepdims=True))
-        weights = jnp.where(causal, weights, 0.0)
-        prob = weights / jnp.sum(weights, axis=1, keepdims=True)
-        grad = jnp.where(causal, prob - target[head], 0.0)
-        of_q = product(grad, gk)
-        of_k = product(grad.T, gq)
-        half = GATE_DIM // 2
-        first = jnp.where(left, of_q, pltpu.roll(of_k, half, 1)).astype(jnp.bfloat16)
-        second = jnp.where(left, pltpu.roll(of_q, half, 1), of_k).astype(jnp.bfloat16)
+    heads = range(KV_HEADS)
+    logits = [
+        lax.dot_general(
+            gates[g],
+            gates[KV_HEADS + g],
+            (((1,), (1,)), ((), ())),
+            preferred_element_type=jnp.float32,
+        )
+        for g in heads
+    ]
+    logits = jnp.where(causal[None], jnp.stack(logits) * scale, NEG_FILL)
+    weights = jnp.exp(logits - jnp.max(logits, axis=2, keepdims=True))
+    weights = jnp.where(causal[None], weights, 0.0)
+    prob = weights / jnp.sum(weights, axis=2, keepdims=True)
+    grad = jnp.where(causal[None], prob - target[...], 0.0)
+    turned = [grad[g].T for g in heads]
+    of_q = [product(grad[g], gates[KV_HEADS + g]) for g in heads]
+    of_k = [product(turned[g], gates[g]) for g in heads]
+    half = GATE_DIM // 2
+    for g in heads:
+        first = jnp.where(left, of_q[g], pltpu.roll(of_k[g], half, 1)).astype(jnp.bfloat16)
+        second = jnp.where(left, pltpu.roll(of_q[g], half, 1), of_k[g]).astype(jnp.bfloat16)
         for to in range(4):
-            at = (head * 4 + to) * NUM_BLOCKS
+            at = (g * 4 + to) * NUM_BLOCKS
             out_ref[at : at + NUM_BLOCKS, :] = first if to % 2 == 0 else second
 
 
-def weight_grads_kernel(pooled, grads, out_ref):
+def weight_grads_kernel(pooled, grads, out_ref, total_s):
+    step = pl.program_id(0)
     depth = 4 * NUM_BLOCKS
-    rows = pooled.shape[0] // 8
-    total = jnp.zeros((rows, GATE_DIM), jnp.float32)
-    for z in range(8):
-        total = total + jnp.dot(
+    rows = total_s.shape[0]
+    total = sum(
+        jnp.dot(
             pooled[z * rows : (z + 1) * rows, :],
             grads[z * depth : (z + 1) * depth, :],
             preferred_element_type=jnp.float32,
         )
+        for z in range(Z_STEP)
+    )
+
+    @pl.when(step == 0)
+    def _():
+        total_s[...] = total
+
+    @pl.when(step > 0)
+    def _():
+        total_s[...] += total
+
+    @pl.when(step == 8 // Z_STEP - 1)
+    def _():
+        pack_weight_grads(total_s[...], out_ref)
+
+
+def pack_weight_grads(total, out_ref):
+    rows = total.shape[0]
     rows_k = rows // 9
     hq, hk = rows_k * 4, rows_k // 2
     of_q, of_k = total[: 2 * hq], total[2 * hq :]
@@ -286,6 +312,24 @@
     )(co.astype(jnp.int32).reshape(1), own, other)
 
 
+def weight_grads(pooled_all, grads, rows):
+    return pl.pallas_call(
+        weight_grads_kernel,
+        out_shape=jax.ShapeDtypeStruct((8, rows // 2, GATE_DIM), jnp.bfloat16),
+        grid=(8 // Z_STEP,),
+        in_specs=[
+            pl.BlockSpec((Z_STEP * rows, 4 * NUM_BLOCKS), lambda i: (i, 0)),
+            pl.BlockSpec((Z_STEP * 4 * NUM_BLOCKS, GATE_DIM), lambda i: (i, 0)),
+        ],
+        out_specs=pl.BlockSpec((8, rows // 2, GATE_DIM), lambda i: (0, 0, 0)),
+        scratch_shapes=[pltpu.VMEM((rows, GATE_DIM), jnp.float32)],
+        compiler_params=pltpu.CompilerParams(
+            dimension_semantics=("arbitrary",), vmem_limit_bytes=56 * 1024 * 1024
+        ),
+        name="weight_grads",
+    )(pooled_all, grads)
+
+
 def ordered(own, other, index):
     return jnp.where(index == 0, jnp.stack([own, other]), jnp.stack([other, own]))
 
@@ -366,14 +410,7 @@
         grads = lax.all_to_all(grads, SEQ_AXES, split_axis=0, concat_axis=0, tiled=True)
 
     with jax.named_scope("weight_grads"):
-        pieces = in_vmem(
-            weight_grads_kernel,
-            jax.ShapeDtypeStruct((8, (rows_q + rows_k) // 2, GATE_DIM), jnp.bfloat16),
-            "weight_grads",
-            16,
-            pooled_all,
-            grads,
-        )
+        pieces = weight_grads(pooled_all, grads, rows_q + rows_k)
         pieces = lax.all_to_all(pieces, "z", split_axis=0, concat_axis=0, tiled=True)
         out_q, out_k = assembled(co, pieces, lax.ppermute(pieces, "co", SWAP), rows_q, rows_k)
     return out_q, out_k

time: 169 us -> 170 us (level)
    pallas_call x0 -> x1, Pallas kernels: none -> 3.64 us  [weight_grads(): pl.pallas_call(weight_grads_kernel, out_shape=jax.ShapeDtypeStruct((8, ro...]
    pallas_call x2 -> x1, Pallas kernels: 4.11 us -> 1.33 us  [in_vmem(): pl.pallas_call(kernel, out_shape=out_shape, in_specs=[spec] * len(args),...]
  transfers between devices with their start and end apart: 10 -> 10, of which waited for: 6 -> 6; matrix products, arithmetic and copies ran while one was open for 7% -> 7% of each run, Pallas kernels for 13% -> 12%
where the time goes in v6:
time: 170 us; the launch traced here: 169 us
  starting transfers between devices  47.7 us (28%)
  blocking collectives  35.7 us (21%)
  waiting for transfers between devices  32 us (19%)
  Pallas kernels  25.2 us (15%)
  between operations  14.3 us (8%)
  other arithmetic  7.05 us (4%)
  local copies, waits for them, and re-layouts  6.38 us (4%)
    all_to_all x1, blocking collectives, shards(): lax.all_to_all(pieces, 'z', split_axis=0, concat_axis=0, tiled=True)  22.2 us
    pallas_call x1, Pallas kernels, attention_targets(): pl.pallas_call(attention_kernel, out_shape=jax.ShapeDtypeStruct((16 * 48,...  18.7 us
    all_to_all x1, starting transfers between devices, shards(): lax.all_to_all(grads, SEQ_AXES, split_axis=0, concat_axis=0, tiled=True)  16 us
    all_to_all x1, blocking collectives, shards(): lax.all_to_all(mine, CTX_AXES, split_axis=0, concat_axis=0, tiled=True)  13.4 us
    all_to_all x1, waiting for transfers between devices, shards(): lax.all_to_all(grads, SEQ_AXES, split_axis=0, concat_axis=0, tiled=True)  12.9 us
    ppermute x1, waiting for transfers between devices, shards(): quad = ordered(pair, lax.ppermute(pair, 'xh', SWAP), xh)  10.8 us
    all_to_all x1, starting transfers between devices, shards(): lax.all_to_all(mine.transpose(1, 0, 2), CTX_AXES, split_axis=0, concat_ax...  8.64 us
    ppermute x1, starting transfers between devices, shards(): pair = ordered(pooled, lax.ppermute(pooled, 'co', SWAP), co)  5.41 us
  transfers between devices with their start and end apart: 10, of which 6 were waited for; matrix products, arithmetic and copies ran while one was open for 7% of the time, Pallas kernels for 12%

profile of v6, /device:TPU:1, one launch (start us, length us, event | category | flops | bytes accessed | tf_op | source)
XLA Modules:
  0.0 168.7 jit_solution(8202844236506118120)
XLA Ops:
  7.2 0.0 copy-start
  7.2 0.0 all-gather.5.cloned.1.call-start
  7.2 0.0 copy-start.1
  7.3 1.1 dynamic-slice_bitcast_fusion.2
  8.4 3.9 %collective-permute-start.3 = (bf16[128,512]{1,0:T(8,128)(2,1)S(1)}, bf16[128,512]{1,0:T(8,128)(2,1)S(1)}, u32[]{:S(2)}, u32[]{:S(2)}) collective-permute-start(bf16[128,512]{1,0:T(8,128)(2,1)S(1)} %get-tuple-element.5), channel_id=1, source_target_pairs={{0,8},{8,0},{1,9},{9,1},{2,10},{10,2},{3,11},{11,3},{4,12},{12,4},... | collective-permute-start | bytes 393224 | tf_op jit(solution)/shard_map/keys/ppermute | solution.py:346
  12.4 2.3 %collective-permute-done.3 = bf16[128,512]{1,0:T(8,128)(2,1)S(1)} collective-permute-done((bf16[128,512]{1,0:T(8,128)(2,1)S(1)}, bf16[128,512]{1,0:T(8,128)(2,1)S(1)}, u32[]{:S(2)}, u32[]{:S(2)}) %collective-permute-start.3) | collective-permute-done | bytes 131104 | tf_op jit(solution)/shard_map/keys/ppermute | solution.py:346
  14.7 0.7 pad_maximum_fusion
  15.4 0.0 all-gather.5.cloned.1.call-update
  15.4 2.0 %convert_reduce_fusion = f32[2,8192]{1,0:T(2,128)S(1)} fusion(bf16[2,64,8192]{2,1,0:T(8,128)(2,1)} %bitcast.46), kind=kLoop, calls=%fused_computation | loop fusion | flops 2080768 | bytes 2162688 | tf_op jit(solution)/shard_map/pool/reduce_sum | solution.py:353
  17.5 0.6 copy.30
  18.1 0.1 reduce_max.9
  18.2 0.1 reshape.125
  18.3 0.8 maximum_bitcast_fusion
  19.1 0.6 copy.16
  19.7 8.6 %all-to-all-start = ((bf16[16,2,576]{2,1,0:T(2,128)(2,1)}), bf16[16,2,576]{2,1,0:T(2,128)(2,1)S(1)}, u32[]{:S(2)}, u32[]{:S(2)}) async-start(bf16[16,2,576]{2,1,0:T(2,128)(2,1)} %copy.16), calls=%async_computation | async-start | bytes 81920 | tf_op jit(solution)/shard_map/pool/all_to_all | solution.py:357
  28.4 1.0 dynamic-slice_bitcast_fusion
  29.4 3.3 %collective-permute-start.2 = (bf16[128,4096]{1,0:T(8,128)(2,1)}, bf16[128,4096]{1,0:T(8,128)(2,1)S(1)}, u32[]{:S(2)}, u32[]{:S(2)}) collective-permute-start(bf16[128,4096]{1,0:T(8,128)(2,1)} %dynamic-slice_bitcast_fusion), channel_id=1, source_target_pairs={{0,8},{8,0},{1,9},{9,1},{2,10},{10,2},{3,11},{11,3},{4,12},{12,4},... | collective-permute-start | bytes 3145736 | tf_op jit(solution)/shard_map/keys/ppermute | solution.py:349
  32.7 3.0 %all-to-all-done = bf16[16,2,576]{2,1,0:T(2,128)(2,1)S(1)} async-done(((bf16[16,2,576]{2,1,0:T(2,128)(2,1)}), bf16[16,2,576]{2,1,0:T(2,128)(2,1)S(1)}, u32[]{:S(2)}, u32[]{:S(2)}) %all-to-all-start) | async-done | bytes 36896 | tf_op jit(solution)/shard_map/pool/all_to_all | solution.py:357
  35.8 5.4 %collective-permute-start = (bf16[32,576]{1,0:T(8,128)(2,1)S(1)}, bf16[32,576]{1,0:T(8,128)(2,1)S(1)}, u32[]{:S(2)}, u32[]{:S(2)}) collective-permute-start(bf16[32,576]{1,0:T(8,128)(2,1)S(1)} %reshape.126), channel_id=1, source_target_pairs={{0,16},{16,0},{1,17},{17,1},{2,18},{18,2},{3,19},{19,3},{4,20},{20... | collective-permute-start | bytes 110600 | tf_op jit(solution)/shard_map/pooled_all/ppermute | solution.py:379
  41.2 0.3 fusion
  41.5 0.1 fusion.4
  41.7 0.8 reshape.128
  42.5 3.5 %all-to-all-start.1 = ((f32[16,2,2048]{2,1,0:T(2,128)}), f32[16,2,2048]{2,1,0:T(2,128)S(1)}, u32[]{:S(2)}, u32[]{:S(2)}) async-start(f32[16,2,2048]{2,1,0:T(2,128)} %reshape.128), calls=%async_computation.1 | async-start | bytes 524288 | tf_op jit(solution)/shard_map/gates/all_to_all | solution.py:372
  46.1 0.0 all-gather.3.cloned.1.call-start
  46.2 3.9 %collective-permute-start.1 = (bf16[2,32,576]{2,1,0:T(8,128)(2,1)S(1)}, bf16[2,32,576]{2,1,0:T(8,128)(2,1)S(1)}, u32[]{:S(2)}, u32[]{:S(2)}) collective-permute-start(bf16[2,32,576]{2,1,0:T(8,128)(2,1)S(1)} %maximum_select_fusion.2), channel_id=1, source_target_pairs={{0,32},{32,0},{1,33},{33,1},{2,34},{34,2},{3,35},{35,3},{4,36},{36... | collective-permute-start | bytes 221192 | tf_op jit(solution)/shard_map/pooled_all/ppermute | solution.py:380
  50.2 10.8 %collective-permute-done.1 = bf16[2,32,576]{2,1,0:T(8,128)(2,1)S(1)} collective-permute-done((bf16[2,32,576]{2,1,0:T(8,128)(2,1)S(1)}, bf16[2,32,576]{2,1,0:T(8,128)(2,1)S(1)}, u32[]{:S(2)}, u32[]{:S(2)}) %collective-permute-start.1) | collective-permute-done | bytes 73760 | tf_op jit(solution)/shard_map/pooled_all/ppermute | solution.py:380
  61.1 0.8 copy.17
  61.9 0.0 all-gather.3.cloned.1.call-update
  61.9 0.7 fusion.2
  62.6 1.9 %pad_add_fusion.sc = s32[4]{0:T(128)} fusion(s32[1]{0:T(128)} %bitcast.12, s32[1]{0:T(128)} %bitcast.11, s32[1]{0:T(128)} %bitcast.10, s32[1]{0:T(128)} %bitcast.9), kind=kLoop, calls=%fused_computation.21 | loop fusion | flops 12 | bytes 32 | tf_op jit(solution)/shard_map/targets/stack | solution.py:385
  64.5 0.7 reduce_sum.39
  65.2 1.2 all-gather.5.cloned.1.call-done.k_ref
  66.4 18.7 %attention_targets.1 = bf16[768,128]{1,0:T(8,128)(2,1)} custom-call(s32[4]{0:T(128)} %pad_add_fusion.sc, bf16[128,8192]{1,0:T(8,128)(2,1)} %bitcast.47, bf16[128,4096]{1,0:T(8,128)(2,1)} %copy-done.6, bf16[2048,512]{1,0:T(8,128)(2,1)} %all-gather.5.cloned.1.call-done.k_ref, bf16[32,128]{1,0:T(8,128)(2,1)} %bitcast.61, bf16[576,128]{1,0:T(8,128)(2,1)} %bitcast.52), custom_call_target="tpu_custom_call" | custom-call | flops 3221225472 | bytes 4194304 | tf_op jit(solution)/shard_map/targets/attention_targets/pallas_call | solution.py:154
  85.1 13.4 %all_to_all.35 = bf16[16,48,128]{2,1,0:T(8,128)(2,1)S(1)} all-to-all(bf16[16,48,128]{2,1,0:T(8,128)(2,1)} %bitcast.55), channel_id=1, replica_groups=mesh['z'=8,'xh'=2,'co'=2,'xl'=2,'y'=8] {'xl','y'}, dimensions={0} | all-to-all | bytes 393216 | tf_op jit(solution)/shard_map/targets/all_to_all | solution.py:394
  98.5 0.1 fusion.6
  98.6 0.1 copy.20
  98.7 0.1 copy.25
  98.8 0.1 copy.22
  98.9 1.3 gate_grads.1
  100.2 16.0 %all-to-all-start.3 = ((bf16[32,32,128]{2,1,0:T(8,128)(2,1)}), bf16[32,32,128]{2,1,0:T(8,128)(2,1)S(1)}, u32[]{:S(2)}, u32[]{:S(2)}) async-start(bf16[32,32,128]{2,1,0:T(8,128)(2,1)} %bitcast.27), calls=%async_computation.3 | async-start | bytes 524288 | tf_op jit(solution)/shard_map/gate_grads/all_to_all | solution.py:410
  116.2 0.0 all-gather.3.cloned.1.call-done.pooled
  116.3 12.9 %all-to-all-done.3 = bf16[32,32,128]{2,1,0:T(8,128)(2,1)S(1)} async-done(((bf16[32,32,128]{2,1,0:T(8,128)(2,1)}), bf16[32,32,128]{2,1,0:T(8,128)(2,1)S(1)}, u32[]{:S(2)}, u32[]{:S(2)}) %all-to-all-start.3) | async-done | bytes 262176 | tf_op jit(solution)/shard_map/gate_grads/all_to_all | solution.py:410
  129.2 0.7 copy-done.3
  129.9 3.6 %weight_grads.1 = bf16[8,288,128]{2,1,0:T(8,128)(2,1)} custom-call(bf16[4608,128]{1,0:T(8,128)(2,1)} %all-gather.3.cloned.1.call-done.pooled, bf16[1024,128]{1,0:T(8,128)(2,1)} %bitcast.49), custom_call_target="tpu_custom_call" | custom-call | tf_op jit(solution)/shard_map/weight_grads/weight_grads/pallas_call | solution.py:316
  133.5 22.2 %all_to_all.36.own = bf16[8,288,128]{2,1,0:T(8,128)(2,1)S(1)} all-to-all(bf16[8,288,128]{2,1,0:T(8,128)(2,1)} %weight_grads.1), channel_id=1, replica_groups=mesh['z'=8,'xh'=2,'co'=2,'xl'=2,'y'=8] {'z'}, dimensions={0} | all-to-all | bytes 1179648 | tf_op jit(solution)/shard_map/weight_grads/all_to_all | solution.py:414
  155.8 2.9 %collective-permute-start.4 = (bf16[8,288,128]{2,1,0:T(8,128)(2,1)S(1)}, bf16[8,288,128]{2,1,0:T(8,128)(2,1)S(1)}, u32[]{:S(2)}, u32[]{:S(2)}) collective-permute-start(bf16[8,288,128]{2,1,0:T(8,128)(2,1)S(1)} %all_to_all.36.own), channel_id=1, source_target_pairs={{0,16},{16,0},{1,17},{17,1},{2,18},{18,2},{3,19},{19,3},{4,20},{20... | collective-permute-start | bytes 1769480 | tf_op jit(solution)/shard_map/weight_grads/ppermute | solution.py:415
  158.7 1.6 collective-permute-done.4.other
  160.3 1.6 assembled.1
  (24 shorter events, 0.3 us)
Async XLA Ops:
  7.2 34.0 %copy-start = (bf16[512,1024]{1,0:T(8,128)(2,1)S(1)}, bf16[512,1024]{1,0:T(8,128)(2,1)}, u32[]{:S(2)}) copy-start(bf16[512,1024]{1,0:T(8,128)(2,1)} %param.8) | copy-start | bytes 3145732
  7.2 11.0 %copy-start.2 = (bf16[1,128,1024]{2,1,0:T(8,128)(2,1)S(1)}, bf16[1,128,1024]{2,1,0:T(8,128)(2,1)}, u32[]{:S(2)}) copy-start(bf16[1,128,1024]{2,1,0:T(8,128)(2,1)} %param.6) | copy-start | bytes 786436
  7.2 59.2 %all-gather.5.cloned.1.call-start = ((), (), s32[]{:S(2)}) async-start(), calls=%async_computation.6 | async-start | bytes 2359296 | tf_op jit(solution)/shard_map/keys/all_gather | solution.py:347
  7.2 21.1 %copy-start.1 = (bf16[1,128,8192]{2,1,0:T(8,128)(2,1)S(1)}, bf16[1,128,8192]{2,1,0:T(8,128)(2,1)}, u32[]{:S(2)}) copy-start(bf16[1,128,8192]{2,1,0:T(8,128)(2,1)} %param.5) | copy-start | bytes 6291460
  8.4 6.3 %collective-permute-start.3 = (bf16[128,512]{1,0:T(8,128)(2,1)S(1)}, bf16[128,512]{1,0:T(8,128)(2,1)S(1)}, u32[]{:S(2)}, u32[]{:S(2)}) collective-permute-start(bf16[128,512]{1,0:T(8,128)(2,1)S(1)} %get-tuple-element.5), channel_id=1, source_target_pairs={{0,8},{8,0},{1,9},{9,1},{2,10},{10,2},{3,11},{11,3},{4,12},{12,4},... | collective-permute-start | bytes 393224 | tf_op jit(solution)/shard_map/keys/ppermute | solution.py:346
  17.5 24.0 %copy-start.4 = (bf16[64,1024]{1,0:T(8,128)(2,1)S(1)}, bf16[64,1024]{1,0:T(8,128)(2,1)}, u32[]{:S(2)}) copy-start(bf16[64,1024]{1,0:T(8,128)(2,1)} %param.9) | copy-start | bytes 393220
  19.7 16.0 %all-to-all-start = ((bf16[16,2,576]{2,1,0:T(2,128)(2,1)}), bf16[16,2,576]{2,1,0:T(2,128)(2,1)S(1)}, u32[]{:S(2)}, u32[]{:S(2)}) async-start(bf16[16,2,576]{2,1,0:T(2,128)(2,1)} %copy.16), calls=%async_computation | async-start | bytes 81920 | tf_op jit(solution)/shard_map/pool/all_to_all | solution.py:357
  29.4 35.8 %collective-permute-start.2 = (bf16[128,4096]{1,0:T(8,128)(2,1)}, bf16[128,4096]{1,0:T(8,128)(2,1)S(1)}, u32[]{:S(2)}, u32[]{:S(2)}) collective-permute-start(bf16[128,4096]{1,0:T(8,128)(2,1)} %dynamic-slice_bitcast_fusion), channel_id=1, source_target_pairs={{0,8},{8,0},{1,9},{9,1},{2,10},{10,2},{3,11},{11,3},{4,12},{12,4},... | collective-permute-start | bytes 3145736 | tf_op jit(solution)/shard_map/keys/ppermute | solution.py:349
  35.8 26.1 %copy-start.5 = (s32[1,2048]{1,0:T(1,128)S(1)}, s32[1,2048]{1,0:T(1,128)}, u32[]{:S(2)}) copy-start(s32[1,2048]{1,0:T(1,128)} %param.7) | copy-start | bytes 24580
  35.8 10.4 %collective-permute-start = (bf16[32,576]{1,0:T(8,128)(2,1)S(1)}, bf16[32,576]{1,0:T(8,128)(2,1)S(1)}, u32[]{:S(2)}, u32[]{:S(2)}) collective-permute-start(bf16[32,576]{1,0:T(8,128)(2,1)S(1)} %reshape.126), channel_id=1, source_target_pairs={{0,16},{16,0},{1,17},{17,1},{2,18},{18,2},{3,19},{19,3},{4,20},{20... | collective-permute-start | bytes 110600 | tf_op jit(solution)/shard_map/pooled_all/ppermute | solution.py:379
  42.5 22.0 %all-to-all-start.1 = ((f32[16,2,2048]{2,1,0:T(2,128)}), f32[16,2,2048]{2,1,0:T(2,128)S(1)}, u32[]{:S(2)}, u32[]{:S(2)}) async-start(f32[16,2,2048]{2,1,0:T(2,128)} %reshape.128), calls=%async_computation.1 | async-start | bytes 524288 | tf_op jit(solution)/shard_map/gates/all_to_all | solution.py:372
  46.1 70.2 %all-gather.3.cloned.1.call-start = ((), (), s32[]{:S(2)}) async-start(), calls=%async_computation.5 | async-start | bytes 1327104 | tf_op jit(solution)/shard_map/pooled_all/all_gather | solution.py:382
  46.2 14.8 %collective-permute-start.1 = (bf16[2,32,576]{2,1,0:T(8,128)(2,1)S(1)}, bf16[2,32,576]{2,1,0:T(8,128)(2,1)S(1)}, u32[]{:S(2)}, u32[]{:S(2)}) collective-permute-start(bf16[2,32,576]{2,1,0:T(8,128)(2,1)S(1)} %maximum_select_fusion.2), channel_id=1, source_target_pairs={{0,32},{32,0},{1,33},{33,1},{2,34},{34,2},{3,35},{35,3},{4,36},{36... | collective-permute-start | bytes 221192 | tf_op jit(solution)/shard_map/pooled_all/ppermute | solution.py:380
  65.2 1.2 copy-start.6
  100.2 29.0 %all-to-all-start.3 = ((bf16[32,32,128]{2,1,0:T(8,128)(2,1)}), bf16[32,32,128]{2,1,0:T(8,128)(2,1)S(1)}, u32[]{:S(2)}, u32[]{:S(2)}) async-start(bf16[32,32,128]{2,1,0:T(8,128)(2,1)} %bitcast.27), calls=%async_computation.3 | async-start | bytes 524288 | tf_op jit(solution)/shard_map/gate_grads/all_to_all | solution.py:410
  129.2 0.7 copy-start.3
  155.8 4.6 %collective-permute-start.4 = (bf16[8,288,128]{2,1,0:T(8,128)(2,1)S(1)}, bf16[8,288,128]{2,1,0:T(8,128)(2,1)S(1)}, u32[]{:S(2)}, u32[]{:S(2)}) collective-permute-start(bf16[8,288,128]{2,1,0:T(8,128)(2,1)S(1)} %all_to_all.36.own), channel_id=1, source_target_pairs={{0,16},{16,0},{1,17},{17,1},{2,18},{18,2},{3,19},{19,3},{4,20},{20... | collective-permute-start | bytes 1769480 | tf_op jit(solution)/shard_map/weight_grads/ppermute | solution.py:415
Sparse Core Ops, SparseCore 0:
  15.6 50.8 all-gather.4
  68.5 40.8 all-gather.2

commit v7 on v4

--- a/solution.py
+++ b/solution.py
@@ -198,23 +198,30 @@
         total = total + jnp.dot(low, other, preferred_element_type=jnp.float32)
         return (total * scale).astype(jnp.bfloat16).astype(jnp.float32)
 
-    for head in range(KV_HEADS):
-        gq, gk = gates[head], gates[KV_HEADS + head]
-        logits = lax.dot_general(
-            gq, gk, (((1,), (1,)), ((), ())), preferred_element_type=jnp.float32
-        )
-        logits = jnp.where(causal, logits * scale, NEG_FILL)
-        weights = jnp.exp(logits - jnp.max(logits, axis=1, keepdims=True))
-        weights = jnp.where(causal, weights, 0.0)
-        prob = weights / jnp.sum(weights, axis=1, keepdims=True)
-        grad = jnp.where(causal, prob - target[head], 0.0)
-        of_q = product(grad, gk)
-        of_k = product(grad.T, gq)
-        half = GATE_DIM // 2
-        first = jnp.where(left, of_q, pltpu.roll(of_k, half, 1)).astype(jnp.bfloat16)
-        second = jnp.where(left, pltpu.roll(of_q, half, 1), of_k).astype(jnp.bfloat16)
+    heads = range(KV_HEADS)
+    logits = [
+        lax.dot_general(
+            gates[g],
+            gates[KV_HEADS + g],
+            (((1,), (1,)), ((), ())),
+            preferred_element_type=jnp.float32,
+        )
+        for g in heads
+    ]
+    logits = jnp.where(causal[None], jnp.stack(logits) * scale, NEG_FILL)
+    weights = jnp.exp(logits - jnp.max(logits, axis=2, keepdims=True))
+    weights = jnp.where(causal[None], weights, 0.0)
+    prob = weights / jnp.sum(weights, axis=2, keepdims=True)
+    grad = jnp.where(causal[None], prob - target[...], 0.0)
+    turned = [grad[g].T for g in heads]
+    of_q = [product(grad[g], gates[KV_HEADS + g]) for g in heads]
+    of_k = [product(turned[g], gates[g]) for g in heads]
+    half = GATE_DIM // 2
+    for g in heads:
+        first = jnp.where(left, of_q[g], pltpu.roll(of_k[g], half, 1)).astype(jnp.bfloat16)
+        second = jnp.where(left, pltpu.roll(of_q[g], half, 1), of_k[g]).astype(jnp.bfloat16)
         for to in range(4):
-            at = (head * 4 + to) * NUM_BLOCKS
+            at = (g * 4 + to) * NUM_BLOCKS
             out_ref[at : at + NUM_BLOCKS, :] = first if to % 2 == 0 else second
 
 

time: 169 us -> 166 us (0.982)
  Pallas kernels: 24.4 us -> 22.1 us
    pallas_call x2, Pallas kernels: 4.11 us -> 1.85 us  [in_vmem(): pl.pallas_call(kernel, out_shape=out_shape, in_specs=[spec] * len(args),...]
  transfers between devices with their start and end apart: 10 -> 10, of which waited for: 6 -> 6; matrix products, arithmetic and copies ran while one was open for 7% -> 7% of each run, Pallas kernels for 13% -> 12%
where the time goes in v7:
time: 166 us
  starting transfers between devices  48.2 us (29%)
  blocking collectives  34.6 us (21%)
  waiting for transfers between devices  32 us (19%)
  Pallas kernels  22.1 us (13%)
  between operations  14.3 us (9%)
  other arithmetic  7.05 us (4%)
  local copies, waits for them, and re-layouts  6.95 us (4%)
    all_to_all x1, blocking collectives, shards(): lax.all_to_all(pieces, 'z', split_axis=0, concat_axis=0, tiled=True)  21.2 us
    pallas_call x1, Pallas kernels, attention_targets(): pl.pallas_call(attention_kernel, out_shape=jax.ShapeDtypeStruct((16 * 48,...  18.7 us
    all_to_all x1, starting transfers between devices, shards(): lax.all_to_all(grads, SEQ_AXES, split_axis=0, concat_axis=0, tiled=True)  16 us
    all_to_all x1, blocking collectives, shards(): lax.all_to_all(mine, CTX_AXES, split_axis=0, concat_axis=0, tiled=True)  13.4 us
    all_to_all x1, waiting for transfers between devices, shards(): lax.all_to_all(grads, SEQ_AXES, split_axis=0, concat_axis=0, tiled=True)  12.9 us
    ppermute x1, waiting for transfers between devices, shards(): quad = ordered(pair, lax.ppermute(pair, 'xh', SWAP), xh)  10.8 us
    all_to_all x1, starting transfers between devices, shards(): lax.all_to_all(mine.transpose(1, 0, 2), CTX_AXES, split_axis=0, concat_ax...  8.64 us
    ppermute x1, starting transfers between devices, shards(): pair = ordered(pooled, lax.ppermute(pooled, 'co', SWAP), co)  5.41 us
  transfers between devices with their start and end apart: 10, of which 6 were waited for; matrix products, arithmetic and copies ran while one was open for 7% of the time, Pallas kernels for 12%

profile of v7, /device:TPU:1, one launch (start us, length us, event | category | flops | bytes accessed | tf_op | source)
XLA Modules:
  0.0 165.6 jit_solution(457322883510781101)
XLA Ops:
  7.2 0.0 copy-start
  7.2 0.0 all-gather.5.cloned.1.call-start
  7.2 0.0 copy-start.2
  7.3 1.1 dynamic-slice_bitcast_fusion.2
  8.4 3.9 %collective-permute-start.3 = (bf16[128,512]{1,0:T(8,128)(2,1)S(1)}, bf16[128,512]{1,0:T(8,128)(2,1)S(1)}, u32[]{:S(2)}, u32[]{:S(2)}) collective-permute-start(bf16[128,512]{1,0:T(8,128)(2,1)S(1)} %get-tuple-element.5), channel_id=1, source_target_pairs={{0,8},{8,0},{1,9},{9,1},{2,10},{10,2},{3,11},{11,3},{4,12},{12,4},... | collective-permute-start | bytes 393224 | tf_op jit(solution)/shard_map/keys/ppermute | solution.py:309
  12.4 2.3 %collective-permute-done.3 = bf16[128,512]{1,0:T(8,128)(2,1)S(1)} collective-permute-done((bf16[128,512]{1,0:T(8,128)(2,1)S(1)}, bf16[128,512]{1,0:T(8,128)(2,1)S(1)}, u32[]{:S(2)}, u32[]{:S(2)}) %collective-permute-start.3) | collective-permute-done | bytes 131104 | tf_op jit(solution)/shard_map/keys/ppermute | solution.py:309
  14.7 0.7 pad_maximum_fusion
  15.4 0.0 all-gather.5.cloned.1.call-update
  15.4 2.0 %convert_reduce_fusion = f32[2,8192]{1,0:T(2,128)S(1)} fusion(bf16[2,64,8192]{2,1,0:T(8,128)(2,1)} %bitcast.47), kind=kLoop, calls=%fused_computation | loop fusion | flops 2080768 | bytes 2162688 | tf_op jit(solution)/shard_map/pool/reduce_sum | solution.py:316
  17.5 0.6 copy.30
  18.1 0.1 reduce_max.9
  18.2 0.1 reshape.125
  18.3 0.8 maximum_bitcast_fusion
  19.1 0.6 copy.16
  19.7 8.6 %all-to-all-start = ((bf16[16,2,576]{2,1,0:T(2,128)(2,1)}), bf16[16,2,576]{2,1,0:T(2,128)(2,1)S(1)}, u32[]{:S(2)}, u32[]{:S(2)}) async-start(bf16[16,2,576]{2,1,0:T(2,128)(2,1)} %copy.16), calls=%async_computation | async-start | bytes 81920 | tf_op jit(solution)/shard_map/pool/all_to_all | solution.py:320
  28.4 1.0 dynamic-slice_bitcast_fusion
  29.4 3.3 %collective-permute-start.2 = (bf16[128,4096]{1,0:T(8,128)(2,1)}, bf16[128,4096]{1,0:T(8,128)(2,1)S(1)}, u32[]{:S(2)}, u32[]{:S(2)}) collective-permute-start(bf16[128,4096]{1,0:T(8,128)(2,1)} %dynamic-slice_bitcast_fusion), channel_id=1, source_target_pairs={{0,8},{8,0},{1,9},{9,1},{2,10},{10,2},{3,11},{11,3},{4,12},{12,4},... | collective-permute-start | bytes 3145736 | tf_op jit(solution)/shard_map/keys/ppermute | solution.py:312
  32.7 3.0 %all-to-all-done = bf16[16,2,576]{2,1,0:T(2,128)(2,1)S(1)} async-done(((bf16[16,2,576]{2,1,0:T(2,128)(2,1)}), bf16[16,2,576]{2,1,0:T(2,128)(2,1)S(1)}, u32[]{:S(2)}, u32[]{:S(2)}) %all-to-all-start) | async-done | bytes 36896 | tf_op jit(solution)/shard_map/pool/all_to_all | solution.py:320
  35.8 5.4 %collective-permute-start = (bf16[32,576]{1,0:T(8,128)(2,1)S(1)}, bf16[32,576]{1,0:T(8,128)(2,1)S(1)}, u32[]{:S(2)}, u32[]{:S(2)}) collective-permute-start(bf16[32,576]{1,0:T(8,128)(2,1)S(1)} %reshape.126), channel_id=1, source_target_pairs={{0,16},{16,0},{1,17},{17,1},{2,18},{18,2},{3,19},{19,3},{4,20},{20... | collective-permute-start | bytes 110600 | tf_op jit(solution)/shard_map/pooled_all/ppermute | solution.py:342
  41.2 0.3 fusion
  41.5 0.1 fusion.4
  41.7 0.8 reshape.128
  42.5 3.5 %all-to-all-start.1 = ((f32[16,2,2048]{2,1,0:T(2,128)}), f32[16,2,2048]{2,1,0:T(2,128)S(1)}, u32[]{:S(2)}, u32[]{:S(2)}) async-start(f32[16,2,2048]{2,1,0:T(2,128)} %reshape.128), calls=%async_computation.1 | async-start | bytes 524288 | tf_op jit(solution)/shard_map/gates/all_to_all | solution.py:335
  46.1 0.0 all-gather.3.cloned.1.call-start
  46.2 3.9 %collective-permute-start.1 = (bf16[2,32,576]{2,1,0:T(8,128)(2,1)S(1)}, bf16[2,32,576]{2,1,0:T(8,128)(2,1)S(1)}, u32[]{:S(2)}, u32[]{:S(2)}) collective-permute-start(bf16[2,32,576]{2,1,0:T(8,128)(2,1)S(1)} %maximum_select_fusion.2), channel_id=1, source_target_pairs={{0,32},{32,0},{1,33},{33,1},{2,34},{34,2},{3,35},{35,3},{4,36},{36... | collective-permute-start | bytes 221192 | tf_op jit(solution)/shard_map/pooled_all/ppermute | solution.py:343
  50.2 10.8 %collective-permute-done.1 = bf16[2,32,576]{2,1,0:T(8,128)(2,1)S(1)} collective-permute-done((bf16[2,32,576]{2,1,0:T(8,128)(2,1)S(1)}, bf16[2,32,576]{2,1,0:T(8,128)(2,1)S(1)}, u32[]{:S(2)}, u32[]{:S(2)}) %collective-permute-start.1) | collective-permute-done | bytes 73760 | tf_op jit(solution)/shard_map/pooled_all/ppermute | solution.py:343
  61.1 0.8 copy.17
  61.9 0.0 all-gather.3.cloned.1.call-update
  61.9 0.7 fusion.2
  62.6 1.9 %pad_add_fusion.sc = s32[4]{0:T(128)} fusion(s32[1]{0:T(128)} %bitcast.12, s32[1]{0:T(128)} %bitcast.11, s32[1]{0:T(128)} %bitcast.10, s32[1]{0:T(128)} %bitcast.9), kind=kLoop, calls=%fused_computation.21 | loop fusion | flops 12 | bytes 32 | tf_op jit(solution)/shard_map/targets/stack | solution.py:348
  64.5 0.7 reduce_sum.39
  65.2 1.2 all-gather.5.cloned.1.call-done.k_ref
  66.4 18.7 %attention_targets.1 = bf16[768,128]{1,0:T(8,128)(2,1)} custom-call(s32[4]{0:T(128)} %pad_add_fusion.sc, bf16[128,8192]{1,0:T(8,128)(2,1)} %bitcast.48, bf16[128,4096]{1,0:T(8,128)(2,1)} %copy-done.6, bf16[2048,512]{1,0:T(8,128)(2,1)} %all-gather.5.cloned.1.call-done.k_ref, bf16[32,128]{1,0:T(8,128)(2,1)} %bitcast.61, bf16[576,128]{1,0:T(8,128)(2,1)} %bitcast.52), custom_call_target="tpu_custom_call" | custom-call | flops 3221225472 | bytes 4194304 | tf_op jit(solution)/shard_map/targets/attention_targets/pallas_call | solution.py:153
  85.1 13.4 %all_to_all.35 = bf16[16,48,128]{2,1,0:T(8,128)(2,1)S(1)} all-to-all(bf16[16,48,128]{2,1,0:T(8,128)(2,1)} %bitcast.55), channel_id=1, replica_groups=mesh['z'=8,'xh'=2,'co'=2,'xl'=2,'y'=8] {'xl','y'}, dimensions={0} | all-to-all | bytes 393216 | tf_op jit(solution)/shard_map/targets/all_to_all | solution.py:357
  98.5 0.1 fusion.6
  98.6 0.1 copy.20
  98.7 0.1 copy.25
  98.8 0.1 copy.22
  98.9 1.3 gate_grads.1
  100.2 16.0 %all-to-all-start.3 = ((bf16[32,32,128]{2,1,0:T(8,128)(2,1)}), bf16[32,32,128]{2,1,0:T(8,128)(2,1)S(1)}, u32[]{:S(2)}, u32[]{:S(2)}) async-start(bf16[32,32,128]{2,1,0:T(8,128)(2,1)} %bitcast.27), calls=%async_computation.3 | async-start | bytes 524288 | tf_op jit(solution)/shard_map/gate_grads/all_to_all | solution.py:373
  116.2 0.0 all-gather.3.cloned.1.call-done.pooled
  116.3 12.9 %all-to-all-done.3 = bf16[32,32,128]{2,1,0:T(8,128)(2,1)S(1)} async-done(((bf16[32,32,128]{2,1,0:T(8,128)(2,1)}), bf16[32,32,128]{2,1,0:T(8,128)(2,1)S(1)}, u32[]{:S(2)}, u32[]{:S(2)}) %all-to-all-start.3) | async-done | bytes 262176 | tf_op jit(solution)/shard_map/gate_grads/all_to_all | solution.py:373
  129.2 1.3 copy-done.1
  130.4 0.5 weight_grads.1
  131.0 21.2 %all_to_all.36.own = bf16[8,288,128]{2,1,0:T(8,128)(2,1)S(1)} all-to-all(bf16[8,288,128]{2,1,0:T(8,128)(2,1)S(1)} %weight_grads.1), channel_id=1, replica_groups=mesh['z'=8,'xh'=2,'co'=2,'xl'=2,'y'=8] {'z'}, dimensions={0} | all-to-all | bytes 1179648 | tf_op jit(solution)/shard_map/weight_grads/all_to_all | solution.py:384
  152.2 3.4 %collective-permute-start.4 = (bf16[8,288,128]{2,1,0:T(8,128)(2,1)S(1)}, bf16[8,288,128]{2,1,0:T(8,128)(2,1)S(1)}, u32[]{:S(2)}, u32[]{:S(2)}) collective-permute-start(bf16[8,288,128]{2,1,0:T(8,128)(2,1)S(1)} %all_to_all.36.own), channel_id=1, source_target_pairs={{0,16},{16,0},{1,17},{17,1},{2,18},{18,2},{3,19},{19,3},{4,20},{20... | collective-permute-start | bytes 1769480 | tf_op jit(solution)/shard_map/weight_grads/ppermute | solution.py:385
  155.6 1.6 collective-permute-done.4.other
  157.2 1.6 assembled.1
  (24 shorter events, 0.3 us)
Async XLA Ops:
  7.2 34.0 %copy-start = (bf16[512,1024]{1,0:T(8,128)(2,1)S(1)}, bf16[512,1024]{1,0:T(8,128)(2,1)}, u32[]{:S(2)}) copy-start(bf16[512,1024]{1,0:T(8,128)(2,1)} %param.8) | copy-start | bytes 3145732
  7.2 11.0 %copy-start.3 = (bf16[1,128,1024]{2,1,0:T(8,128)(2,1)S(1)}, bf16[1,128,1024]{2,1,0:T(8,128)(2,1)}, u32[]{:S(2)}) copy-start(bf16[1,128,1024]{2,1,0:T(8,128)(2,1)} %param.6) | copy-start | bytes 786436
  7.2 59.2 %all-gather.5.cloned.1.call-start = ((), (), s32[]{:S(2)}) async-start(), calls=%async_computation.6 | async-start | bytes 2359296 | tf_op jit(solution)/shard_map/keys/all_gather | solution.py:310
  7.2 21.1 %copy-start.2 = (bf16[1,128,8192]{2,1,0:T(8,128)(2,1)S(1)}, bf16[1,128,8192]{2,1,0:T(8,128)(2,1)}, u32[]{:S(2)}) copy-start(bf16[1,128,8192]{2,1,0:T(8,128)(2,1)} %param.5) | copy-start | bytes 6291460
  8.4 6.3 %collective-permute-start.3 = (bf16[128,512]{1,0:T(8,128)(2,1)S(1)}, bf16[128,512]{1,0:T(8,128)(2,1)S(1)}, u32[]{:S(2)}, u32[]{:S(2)}) collective-permute-start(bf16[128,512]{1,0:T(8,128)(2,1)S(1)} %get-tuple-element.5), channel_id=1, source_target_pairs={{0,8},{8,0},{1,9},{9,1},{2,10},{10,2},{3,11},{11,3},{4,12},{12,4},... | collective-permute-start | bytes 393224 | tf_op jit(solution)/shard_map/keys/ppermute | solution.py:309
  17.5 24.0 %copy-start.4 = (bf16[64,1024]{1,0:T(8,128)(2,1)S(1)}, bf16[64,1024]{1,0:T(8,128)(2,1)}, u32[]{:S(2)}) copy-start(bf16[64,1024]{1,0:T(8,128)(2,1)} %param.9) | copy-start | bytes 393220
  19.7 16.0 %all-to-all-start = ((bf16[16,2,576]{2,1,0:T(2,128)(2,1)}), bf16[16,2,576]{2,1,0:T(2,128)(2,1)S(1)}, u32[]{:S(2)}, u32[]{:S(2)}) async-start(bf16[16,2,576]{2,1,0:T(2,128)(2,1)} %copy.16), calls=%async_computation | async-start | bytes 81920 | tf_op jit(solution)/shard_map/pool/all_to_all | solution.py:320
  29.4 35.8 %collective-permute-start.2 = (bf16[128,4096]{1,0:T(8,128)(2,1)}, bf16[128,4096]{1,0:T(8,128)(2,1)S(1)}, u32[]{:S(2)}, u32[]{:S(2)}) collective-permute-start(bf16[128,4096]{1,0:T(8,128)(2,1)} %dynamic-slice_bitcast_fusion), channel_id=1, source_target_pairs={{0,8},{8,0},{1,9},{9,1},{2,10},{10,2},{3,11},{11,3},{4,12},{12,4},... | collective-permute-start | bytes 3145736 | tf_op jit(solution)/shard_map/keys/ppermute | solution.py:312
  35.8 26.1 %copy-start.5 = (s32[1,2048]{1,0:T(1,128)S(1)}, s32[1,2048]{1,0:T(1,128)}, u32[]{:S(2)}) copy-start(s32[1,2048]{1,0:T(1,128)} %param.7) | copy-start | bytes 24580
  35.8 10.4 %collective-permute-start = (bf16[32,576]{1,0:T(8,128)(2,1)S(1)}, bf16[32,576]{1,0:T(8,128)(2,1)S(1)}, u32[]{:S(2)}, u32[]{:S(2)}) collective-permute-start(bf16[32,576]{1,0:T(8,128)(2,1)S(1)} %reshape.126), channel_id=1, source_target_pairs={{0,16},{16,0},{1,17},{17,1},{2,18},{18,2},{3,19},{19,3},{4,20},{20... | collective-permute-start | bytes 110600 | tf_op jit(solution)/shard_map/pooled_all/ppermute | solution.py:342
  42.5 22.0 %all-to-all-start.1 = ((f32[16,2,2048]{2,1,0:T(2,128)}), f32[16,2,2048]{2,1,0:T(2,128)S(1)}, u32[]{:S(2)}, u32[]{:S(2)}) async-start(f32[16,2,2048]{2,1,0:T(2,128)} %reshape.128), calls=%async_computation.1 | async-start | bytes 524288 | tf_op jit(solution)/shard_map/gates/all_to_all | solution.py:335
  46.1 70.2 %all-gather.3.cloned.1.call-start = ((), (), s32[]{:S(2)}) async-start(), calls=%async_computation.5 | async-start | bytes 1327104 | tf_op jit(solution)/shard_map/pooled_all/all_gather | solution.py:345
  46.2 14.8 %collective-permute-start.1 = (bf16[2,32,576]{2,1,0:T(8,128)(2,1)S(1)}, bf16[2,32,576]{2,1,0:T(8,128)(2,1)S(1)}, u32[]{:S(2)}, u32[]{:S(2)}) collective-permute-start(bf16[2,32,576]{2,1,0:T(8,128)(2,1)S(1)} %maximum_select_fusion.2), channel_id=1, source_target_pairs={{0,32},{32,0},{1,33},{33,1},{2,34},{34,2},{3,35},{35,3},{4,36},{36... | collective-permute-start | bytes 221192 | tf_op jit(solution)/shard_map/pooled_all/ppermute | solution.py:343
  65.2 1.2 copy-start.6
  100.2 29.0 %all-to-all-start.3 = ((bf16[32,32,128]{2,1,0:T(8,128)(2,1)}), bf16[32,32,128]{2,1,0:T(8,128)(2,1)S(1)}, u32[]{:S(2)}, u32[]{:S(2)}) async-start(bf16[32,32,128]{2,1,0:T(8,128)(2,1)} %bitcast.27), calls=%async_computation.3 | async-start | bytes 524288 | tf_op jit(solution)/shard_map/gate_grads/all_to_all | solution.py:373
  129.2 1.3 copy-start.1
  152.2 5.0 %collective-permute-start.4 = (bf16[8,288,128]{2,1,0:T(8,128)(2,1)S(1)}, bf16[8,288,128]{2,1,0:T(8,128)(2,1)S(1)}, u32[]{:S(2)}, u32[]{:S(2)}) collective-permute-start(bf16[8,288,128]{2,1,0:T(8,128)(2,1)S(1)} %all_to_all.36.own), channel_id=1, source_target_pairs={{0,16},{16,0},{1,17},{17,1},{2,18},{18,2},{3,19},{19,3},{4,20},{20... | collective-permute-start | bytes 1769480 | tf_op jit(solution)/shard_map/weight_grads/ppermute | solution.py:385
Sparse Core Ops, SparseCore 0:
  15.6 50.8 all-gather.4
  68.5 40.8 all-gather.2

commit v8 on v7

--- a/solution.py
+++ b/solution.py
@@ -225,11 +225,17 @@
             out_ref[at : at + NUM_BLOCKS, :] = first if to % 2 == 0 else second
 
 
-def weight_grads_kernel(pooled, grads, out_ref):
+def weight_grads_kernel(pooled_hbm, grads, out_ref, pooled, sems):
     depth = 4 * NUM_BLOCKS
     rows = pooled.shape[0] // 8
+    copies = []
+    for z in range(8):
+        part = pl.ds(z * rows, rows)
+        copies.append(pltpu.make_async_copy(pooled_hbm.at[part], pooled.at[part], sems.at[z]))
+        copies[z].start()
     total = jnp.zeros((rows, GATE_DIM), jnp.float32)
     for z in range(8):
+        copies[z].wait()
         total = total + jnp.dot(
             pooled[z * rows : (z + 1) * rows, :],
             grads[z * depth : (z + 1) * depth, :],
@@ -373,14 +379,19 @@
         grads = lax.all_to_all(grads, SEQ_AXES, split_axis=0, concat_axis=0, tiled=True)
 
     with jax.named_scope("weight_grads"):
-        pieces = in_vmem(
+        in_vmem_spec = pl.BlockSpec(memory_space=pltpu.VMEM)
+        pieces = pl.pallas_call(
             weight_grads_kernel,
-            jax.ShapeDtypeStruct((8, (rows_q + rows_k) // 2, GATE_DIM), jnp.bfloat16),
-            "weight_grads",
-            16,
-            pooled_all,
-            grads,
-        )
+            out_shape=jax.ShapeDtypeStruct((8, (rows_q + rows_k) // 2, GATE_DIM), jnp.bfloat16),
+            in_specs=[pl.BlockSpec(memory_space=pl.ANY), in_vmem_spec],
+            out_specs=in_vmem_spec,
+            scratch_shapes=[
+                pltpu.VMEM(pooled_all.shape, jnp.bfloat16),
+                pltpu.SemaphoreType.DMA((8,)),
+            ],
+            compiler_params=pltpu.CompilerParams(vmem_limit_bytes=56 * 1024 * 1024),
+            name="weight_grads",
+        )(pooled_all, grads)
         pieces = lax.all_to_all(pieces, "z", split_axis=0, concat_axis=0, tiled=True)
         out_q, out_k = assembled(co, pieces, lax.ppermute(pieces, "co", SWAP), rows_q, rows_k)
     return out_q, out_k

time: 166 us -> 170 us (1.024)
  Pallas kernels: 22.1 us -> 25.4 us
    pallas_call x0 -> x1, Pallas kernels: none -> 3.82 us  [shards(): pl.pallas_call(weight_grads_kernel, out_shape=jax.ShapeDtypeStruct((8, (r...]
where the time goes in v8:
time: 170 us; the launch traced here: 169 us
  starting transfers between devices  47.8 us (28%)
  blocking collectives  35.7 us (21%)
  waiting for transfers between devices  32 us (19%)
  Pallas kernels  25.4 us (15%)
  between operations  14.3 us (8%)
  other arithmetic  7.05 us (4%)
  local copies, waits for them, and re-layouts  6.38 us (4%)
    all_to_all x1, blocking collectives, shards(): lax.all_to_all(pieces, 'z', split_axis=0, concat_axis=0, tiled=True)  22.2 us
    pallas_call x1, Pallas kernels, attention_targets(): pl.pallas_call(attention_kernel, out_shape=jax.ShapeDtypeStruct((16 * 48,...  18.7 us
    all_to_all x1, starting transfers between devices, shards(): lax.all_to_all(grads, SEQ_AXES, split_axis=0, concat_axis=0, tiled=True)  16 us
    all_to_all x1, blocking collectives, shards(): lax.all_to_all(mine, CTX_AXES, split_axis=0, concat_axis=0, tiled=True)  13.4 us
    all_to_all x1, waiting for transfers between devices, shards(): lax.all_to_all(grads, SEQ_AXES, split_axis=0, concat_axis=0, tiled=True)  12.9 us
    ppermute x1, waiting for transfers between devices, shards(): quad = ordered(pair, lax.ppermute(pair, 'xh', SWAP), xh)  10.8 us
    all_to_all x1, starting transfers between devices, shards(): lax.all_to_all(mine.transpose(1, 0, 2), CTX_AXES, split_axis=0, concat_ax...  8.64 us
    ppermute x1, starting transfers between devices, shards(): pair = ordered(pooled, lax.ppermute(pooled, 'co', SWAP), co)  5.41 us
  transfers between devices with their start and end apart: 10, of which 6 were waited for; matrix products, arithmetic and copies ran while one was open for 7% of the time, Pallas kernels for 12%

profile of v8, /device:TPU:1, one launch (start us, length us, event | category | flops | bytes accessed | tf_op | source)
XLA Modules:
  0.0 168.9 jit_solution(15890725078869828457)
XLA Ops:
  7.2 0.0 copy-start
  7.2 0.0 all-gather.5.cloned.1.call-start
  7.2 0.0 copy-start.1
  7.3 1.1 dynamic-slice_bitcast_fusion.2
  8.4 3.9 %collective-permute-start.3 = (bf16[128,512]{1,0:T(8,128)(2,1)S(1)}, bf16[128,512]{1,0:T(8,128)(2,1)S(1)}, u32[]{:S(2)}, u32[]{:S(2)}) collective-permute-start(bf16[128,512]{1,0:T(8,128)(2,1)S(1)} %get-tuple-element.5), channel_id=1, source_target_pairs={{0,8},{8,0},{1,9},{9,1},{2,10},{10,2},{3,11},{11,3},{4,12},{12,4},... | collective-permute-start | bytes 393224 | tf_op jit(solution)/shard_map/keys/ppermute | solution.py:315
  12.4 2.3 %collective-permute-done.3 = bf16[128,512]{1,0:T(8,128)(2,1)S(1)} collective-permute-done((bf16[128,512]{1,0:T(8,128)(2,1)S(1)}, bf16[128,512]{1,0:T(8,128)(2,1)S(1)}, u32[]{:S(2)}, u32[]{:S(2)}) %collective-permute-start.3) | collective-permute-done | bytes 131104 | tf_op jit(solution)/shard_map/keys/ppermute | solution.py:315
  14.7 0.7 pad_maximum_fusion
  15.4 0.0 all-gather.5.cloned.1.call-update
  15.4 2.0 %convert_reduce_fusion = f32[2,8192]{1,0:T(2,128)S(1)} fusion(bf16[2,64,8192]{2,1,0:T(8,128)(2,1)} %bitcast.46), kind=kLoop, calls=%fused_computation | loop fusion | flops 2080768 | bytes 2162688 | tf_op jit(solution)/shard_map/pool/reduce_sum | solution.py:322
  17.5 0.6 copy.30
  18.1 0.1 reduce_max.9
  18.2 0.1 reshape.125
  18.3 0.8 maximum_bitcast_fusion
  19.1 0.6 copy.16
  19.7 8.6 %all-to-all-start = ((bf16[16,2,576]{2,1,0:T(2,128)(2,1)}), bf16[16,2,576]{2,1,0:T(2,128)(2,1)S(1)}, u32[]{:S(2)}, u32[]{:S(2)}) async-start(bf16[16,2,576]{2,1,0:T(2,128)(2,1)} %copy.16), calls=%async_computation | async-start | bytes 81920 | tf_op jit(solution)/shard_map/pool/all_to_all | solution.py:326
  28.4 1.0 dynamic-slice_bitcast_fusion
  29.4 3.3 %collective-permute-start.2 = (bf16[128,4096]{1,0:T(8,128)(2,1)}, bf16[128,4096]{1,0:T(8,128)(2,1)S(1)}, u32[]{:S(2)}, u32[]{:S(2)}) collective-permute-start(bf16[128,4096]{1,0:T(8,128)(2,1)} %dynamic-slice_bitcast_fusion), channel_id=1, source_target_pairs={{0,8},{8,0},{1,9},{9,1},{2,10},{10,2},{3,11},{11,3},{4,12},{12,4},... | collective-permute-start | bytes 3145736 | tf_op jit(solution)/shard_map/keys/ppermute | solution.py:318
  32.7 3.0 %all-to-all-done = bf16[16,2,576]{2,1,0:T(2,128)(2,1)S(1)} async-done(((bf16[16,2,576]{2,1,0:T(2,128)(2,1)}), bf16[16,2,576]{2,1,0:T(2,128)(2,1)S(1)}, u32[]{:S(2)}, u32[]{:S(2)}) %all-to-all-start) | async-done | bytes 36896 | tf_op jit(solution)/shard_map/pool/all_to_all | solution.py:326
  35.8 5.4 %collective-permute-start = (bf16[32,576]{1,0:T(8,128)(2,1)S(1)}, bf16[32,576]{1,0:T(8,128)(2,1)S(1)}, u32[]{:S(2)}, u32[]{:S(2)}) collective-permute-start(bf16[32,576]{1,0:T(8,128)(2,1)S(1)} %reshape.126), channel_id=1, source_target_pairs={{0,16},{16,0},{1,17},{17,1},{2,18},{18,2},{3,19},{19,3},{4,20},{20... | collective-permute-start | bytes 110600 | tf_op jit(solution)/shard_map/pooled_all/ppermute | solution.py:348
  41.2 0.3 fusion
  41.5 0.1 fusion.4
  41.7 0.8 reshape.128
  42.5 3.5 %all-to-all-start.1 = ((f32[16,2,2048]{2,1,0:T(2,128)}), f32[16,2,2048]{2,1,0:T(2,128)S(1)}, u32[]{:S(2)}, u32[]{:S(2)}) async-start(f32[16,2,2048]{2,1,0:T(2,128)} %reshape.128), calls=%async_computation.1 | async-start | bytes 524288 | tf_op jit(solution)/shard_map/gates/all_to_all | solution.py:341
  46.1 0.0 all-gather.3.cloned.1.call-start
  46.2 3.9 %collective-permute-start.1 = (bf16[2,32,576]{2,1,0:T(8,128)(2,1)S(1)}, bf16[2,32,576]{2,1,0:T(8,128)(2,1)S(1)}, u32[]{:S(2)}, u32[]{:S(2)}) collective-permute-start(bf16[2,32,576]{2,1,0:T(8,128)(2,1)S(1)} %maximum_select_fusion.2), channel_id=1, source_target_pairs={{0,32},{32,0},{1,33},{33,1},{2,34},{34,2},{3,35},{35,3},{4,36},{36... | collective-permute-start | bytes 221192 | tf_op jit(solution)/shard_map/pooled_all/ppermute | solution.py:349
  50.2 10.8 %collective-permute-done.1 = bf16[2,32,576]{2,1,0:T(8,128)(2,1)S(1)} collective-permute-done((bf16[2,32,576]{2,1,0:T(8,128)(2,1)S(1)}, bf16[2,32,576]{2,1,0:T(8,128)(2,1)S(1)}, u32[]{:S(2)}, u32[]{:S(2)}) %collective-permute-start.1) | collective-permute-done | bytes 73760 | tf_op jit(solution)/shard_map/pooled_all/ppermute | solution.py:349
  61.1 0.8 copy.17
  61.9 0.0 all-gather.3.cloned.1.call-update
  61.9 0.7 fusion.2
  62.6 1.9 %pad_add_fusion.sc = s32[4]{0:T(128)} fusion(s32[1]{0:T(128)} %bitcast.12, s32[1]{0:T(128)} %bitcast.11, s32[1]{0:T(128)} %bitcast.10, s32[1]{0:T(128)} %bitcast.9), kind=kLoop, calls=%fused_computation.21 | loop fusion | flops 12 | bytes 32 | tf_op jit(solution)/shard_map/targets/stack | solution.py:354
  64.5 0.7 reduce_sum.39
  65.2 1.2 all-gather.5.cloned.1.call-done.k_ref
  66.4 18.7 %attention_targets.1 = bf16[768,128]{1,0:T(8,128)(2,1)} custom-call(s32[4]{0:T(128)} %pad_add_fusion.sc, bf16[128,8192]{1,0:T(8,128)(2,1)} %bitcast.47, bf16[128,4096]{1,0:T(8,128)(2,1)} %copy-done.6, bf16[2048,512]{1,0:T(8,128)(2,1)} %all-gather.5.cloned.1.call-done.k_ref, bf16[32,128]{1,0:T(8,128)(2,1)} %bitcast.61, bf16[576,128]{1,0:T(8,128)(2,1)} %bitcast.52), custom_call_target="tpu_custom_call" | custom-call | flops 3221225472 | bytes 4194304 | tf_op jit(solution)/shard_map/targets/attention_targets/pallas_call | solution.py:153
  85.1 13.4 %all_to_all.35 = bf16[16,48,128]{2,1,0:T(8,128)(2,1)S(1)} all-to-all(bf16[16,48,128]{2,1,0:T(8,128)(2,1)} %bitcast.55), channel_id=1, replica_groups=mesh['z'=8,'xh'=2,'co'=2,'xl'=2,'y'=8] {'xl','y'}, dimensions={0} | all-to-all | bytes 393216 | tf_op jit(solution)/shard_map/targets/all_to_all | solution.py:363
  98.5 0.1 fusion.6
  98.6 0.1 copy.20
  98.7 0.1 copy.25
  98.8 0.1 copy.22
  98.9 1.3 gate_grads.1
  100.2 16.0 %all-to-all-start.3 = ((bf16[32,32,128]{2,1,0:T(8,128)(2,1)}), bf16[32,32,128]{2,1,0:T(8,128)(2,1)S(1)}, u32[]{:S(2)}, u32[]{:S(2)}) async-start(bf16[32,32,128]{2,1,0:T(8,128)(2,1)} %bitcast.27), calls=%async_computation.3 | async-start | bytes 524288 | tf_op jit(solution)/shard_map/gate_grads/all_to_all | solution.py:379
  116.2 0.0 all-gather.3.cloned.1.call-done.pooled_hbm
  116.3 12.9 %all-to-all-done.3 = bf16[32,32,128]{2,1,0:T(8,128)(2,1)S(1)} async-done(((bf16[32,32,128]{2,1,0:T(8,128)(2,1)}), bf16[32,32,128]{2,1,0:T(8,128)(2,1)S(1)}, u32[]{:S(2)}, u32[]{:S(2)}) %all-to-all-start.3) | async-done | bytes 262176 | tf_op jit(solution)/shard_map/gate_grads/all_to_all | solution.py:379
  129.2 0.7 copy-done.3
  129.9 3.8 %weight_grads.1 = bf16[8,288,128]{2,1,0:T(8,128)(2,1)} custom-call(bf16[4608,128]{1,0:T(8,128)(2,1)} %all-gather.3.cloned.1.call-done.pooled_hbm, bf16[1024,128]{1,0:T(8,128)(2,1)} %bitcast.49), custom_call_target="tpu_custom_call" | custom-call | tf_op jit(solution)/shard_map/weight_grads/weight_grads/pallas_call | solution.py:383
  133.7 22.2 %all_to_all.36.own = bf16[8,288,128]{2,1,0:T(8,128)(2,1)S(1)} all-to-all(bf16[8,288,128]{2,1,0:T(8,128)(2,1)} %weight_grads.1), channel_id=1, replica_groups=mesh['z'=8,'xh'=2,'co'=2,'xl'=2,'y'=8] {'z'}, dimensions={0} | all-to-all | bytes 1179648 | tf_op jit(solution)/shard_map/weight_grads/all_to_all | solution.py:395
  155.9 3.0 %collective-permute-start.4 = (bf16[8,288,128]{2,1,0:T(8,128)(2,1)S(1)}, bf16[8,288,128]{2,1,0:T(8,128)(2,1)S(1)}, u32[]{:S(2)}, u32[]{:S(2)}) collective-permute-start(bf16[8,288,128]{2,1,0:T(8,128)(2,1)S(1)} %all_to_all.36.own), channel_id=1, source_target_pairs={{0,16},{16,0},{1,17},{17,1},{2,18},{18,2},{3,19},{19,3},{4,20},{20... | collective-permute-start | bytes 1769480 | tf_op jit(solution)/shard_map/weight_grads/ppermute | solution.py:396
  158.9 1.6 collective-permute-done.4.other
  160.5 1.6 assembled.1
  (24 shorter events, 0.3 us)
Async XLA Ops:
  7.2 34.0 %copy-start = (bf16[512,1024]{1,0:T(8,128)(2,1)S(1)}, bf16[512,1024]{1,0:T(8,128)(2,1)}, u32[]{:S(2)}) copy-start(bf16[512,1024]{1,0:T(8,128)(2,1)} %param.8) | copy-start | bytes 3145732
  7.2 11.0 %copy-start.2 = (bf16[1,128,1024]{2,1,0:T(8,128)(2,1)S(1)}, bf16[1,128,1024]{2,1,0:T(8,128)(2,1)}, u32[]{:S(2)}) copy-start(bf16[1,128,1024]{2,1,0:T(8,128)(2,1)} %param.6) | copy-start | bytes 786436
  7.2 59.2 %all-gather.5.cloned.1.call-start = ((), (), s32[]{:S(2)}) async-start(), calls=%async_computation.6 | async-start | bytes 2359296 | tf_op jit(solution)/shard_map/keys/all_gather | solution.py:316
  7.2 21.1 %copy-start.1 = (bf16[1,128,8192]{2,1,0:T(8,128)(2,1)S(1)}, bf16[1,128,8192]{2,1,0:T(8,128)(2,1)}, u32[]{:S(2)}) copy-start(bf16[1,128,8192]{2,1,0:T(8,128)(2,1)} %param.5) | copy-start | bytes 6291460
  8.4 6.3 %collective-permute-start.3 = (bf16[128,512]{1,0:T(8,128)(2,1)S(1)}, bf16[128,512]{1,0:T(8,128)(2,1)S(1)}, u32[]{:S(2)}, u32[]{:S(2)}) collective-permute-start(bf16[128,512]{1,0:T(8,128)(2,1)S(1)} %get-tuple-element.5), channel_id=1, source_target_pairs={{0,8},{8,0},{1,9},{9,1},{2,10},{10,2},{3,11},{11,3},{4,12},{12,4},... | collective-permute-start | bytes 393224 | tf_op jit(solution)/shard_map/keys/ppermute | solution.py:315
  17.5 24.0 %copy-start.4 = (bf16[64,1024]{1,0:T(8,128)(2,1)S(1)}, bf16[64,1024]{1,0:T(8,128)(2,1)}, u32[]{:S(2)}) copy-start(bf16[64,1024]{1,0:T(8,128)(2,1)} %param.9) | copy-start | bytes 393220
  19.7 16.0 %all-to-all-start = ((bf16[16,2,576]{2,1,0:T(2,128)(2,1)}), bf16[16,2,576]{2,1,0:T(2,128)(2,1)S(1)}, u32[]{:S(2)}, u32[]{:S(2)}) async-start(bf16[16,2,576]{2,1,0:T(2,128)(2,1)} %copy.16), calls=%async_computation | async-start | bytes 81920 | tf_op jit(solution)/shard_map/pool/all_to_all | solution.py:326
  29.4 35.8 %collective-permute-start.2 = (bf16[128,4096]{1,0:T(8,128)(2,1)}, bf16[128,4096]{1,0:T(8,128)(2,1)S(1)}, u32[]{:S(2)}, u32[]{:S(2)}) collective-permute-start(bf16[128,4096]{1,0:T(8,128)(2,1)} %dynamic-slice_bitcast_fusion), channel_id=1, source_target_pairs={{0,8},{8,0},{1,9},{9,1},{2,10},{10,2},{3,11},{11,3},{4,12},{12,4},... | collective-permute-start | bytes 3145736 | tf_op jit(solution)/shard_map/keys/ppermute | solution.py:318
  35.8 26.1 %copy-start.5 = (s32[1,2048]{1,0:T(1,128)S(1)}, s32[1,2048]{1,0:T(1,128)}, u32[]{:S(2)}) copy-start(s32[1,2048]{1,0:T(1,128)} %param.7) | copy-start | bytes 24580
  35.8 10.4 %collective-permute-start = (bf16[32,576]{1,0:T(8,128)(2,1)S(1)}, bf16[32,576]{1,0:T(8,128)(2,1)S(1)}, u32[]{:S(2)}, u32[]{:S(2)}) collective-permute-start(bf16[32,576]{1,0:T(8,128)(2,1)S(1)} %reshape.126), channel_id=1, source_target_pairs={{0,16},{16,0},{1,17},{17,1},{2,18},{18,2},{3,19},{19,3},{4,20},{20... | collective-permute-start | bytes 110600 | tf_op jit(solution)/shard_map/pooled_all/ppermute | solution.py:348
  42.5 22.0 %all-to-all-start.1 = ((f32[16,2,2048]{2,1,0:T(2,128)}), f32[16,2,2048]{2,1,0:T(2,128)S(1)}, u32[]{:S(2)}, u32[]{:S(2)}) async-start(f32[16,2,2048]{2,1,0:T(2,128)} %reshape.128), calls=%async_computation.1 | async-start | bytes 524288 | tf_op jit(solution)/shard_map/gates/all_to_all | solution.py:341
  46.1 70.2 %all-gather.3.cloned.1.call-start = ((), (), s32[]{:S(2)}) async-start(), calls=%async_computation.5 | async-start | bytes 1327104 | tf_op jit(solution)/shard_map/pooled_all/all_gather | solution.py:351
  46.2 14.8 %collective-permute-start.1 = (bf16[2,32,576]{2,1,0:T(8,128)(2,1)S(1)}, bf16[2,32,576]{2,1,0:T(8,128)(2,1)S(1)}, u32[]{:S(2)}, u32[]{:S(2)}) collective-permute-start(bf16[2,32,576]{2,1,0:T(8,128)(2,1)S(1)} %maximum_select_fusion.2), channel_id=1, source_target_pairs={{0,32},{32,0},{1,33},{33,1},{2,34},{34,2},{3,35},{35,3},{4,36},{36... | collective-permute-start | bytes 221192 | tf_op jit(solution)/shard_map/pooled_all/ppermute | solution.py:349
  65.2 1.2 copy-start.6
  100.2 29.0 %all-to-all-start.3 = ((bf16[32,32,128]{2,1,0:T(8,128)(2,1)}), bf16[32,32,128]{2,1,0:T(8,128)(2,1)S(1)}, u32[]{:S(2)}, u32[]{:S(2)}) async-start(bf16[32,32,128]{2,1,0:T(8,128)(2,1)} %bitcast.27), calls=%async_computation.3 | async-start | bytes 524288 | tf_op jit(solution)/shard_map/gate_grads/all_to_all | solution.py:379
  129.2 0.7 copy-start.3
  155.9 4.6 %collective-permute-start.4 = (bf16[8,288,128]{2,1,0:T(8,128)(2,1)S(1)}, bf16[8,288,128]{2,1,0:T(8,128)(2,1)S(1)}, u32[]{:S(2)}, u32[]{:S(2)}) collective-permute-start(bf16[8,288,128]{2,1,0:T(8,128)(2,1)S(1)} %all_to_all.36.own), channel_id=1, source_target_pairs={{0,16},{16,0},{1,17},{17,1},{2,18},{18,2},{3,19},{19,3},{4,20},{20... | collective-permute-start | bytes 1769480 | tf_op jit(solution)/shard_map/weight_grads/ppermute | solution.py:396
Sparse Core Ops, SparseCore 0:
  15.6 50.8 all-gather.4
  68.5 40.8 all-gather.2
